TPU v7x, 32 devices: a whole 2x2x4 slice. The times are simulated.
32 devices in a mesh: narrow: 2 (over core), wide: 16 (over z, y, x).
Axes of the slice: x: 2, y: 2, z: 4, core: 2. Of those that a mesh axis runs over, the one named last changes fastest.
Arguments:
- inputs: bfloat16 [2, 32, 256, 1536], P(None, ('narrow', 'wide')), may hold values from -6 to 6
- cotangent: bfloat16 [2, 32, 256, 1536], P(None, ('narrow', 'wide')), may hold values from -6 to 6
- lengths: int32 [2, 32], P(None, ('narrow', 'wide')), may hold values from 32 to 256, as said below
- gains: float32 [2, 1536], P(None, 'wide'), may hold values from 0.5 to 1.5
- gains_momentum: float32 [2, 1536], P(None, 'wide'), may hold values from -768 to 768
- gains_average: float32 [2, 1536], P(None, 'wide'), may hold values from 0.5 to 1.5
- qkv_weight: float32 [3, 1536, 1536], P(None, 'wide'), may hold values from -0.15625 to 0.15625
- qkv_momentum: float32 [3, 1536, 1536], P(None, 'wide'), may hold values from -384 to 384
- qkv_average: float32 [3, 1536, 1536], P(None, 'wide'), may hold values from -0.15625 to 0.15625
- out_weight: float32 [1536, 1536], P('wide'), may hold values from -0.625 to 0.625
- out_momentum: float32 [1536, 1536], P('wide'), may hold values from -160 to 160
- out_average: float32 [1536, 1536], P('wide'), may hold values from -0.625 to 0.625
- conv_taps: float32 [16, 6, 11], replicated, may hold values from -0.5 to 1.5
- taps_momentum: float32 [16, 6, 11], replicated, may hold values from -2560 to 2560
- taps_average: float32 [16, 6, 11], replicated, may hold values from -0.5 to 1.5
- head_mix: float32 [16, 2], replicated, may hold values from -0.5 to 1.3
- mix_momentum: float32 [16, 2], replicated, may hold values from -2560 to 2560
- mix_average: float32 [16, 2], replicated, may hold values from -0.5 to 1.3
- gateup_weight: float32 [1536, 2, 4096], P('wide'), may hold values from -0.15625 to 0.15625
- gateup_momentum: float32 [1536, 2, 4096], P('wide'), may hold values from -224 to 224
- gateup_average: float32 [1536, 2, 4096], P('wide'), may hold values from -0.15625 to 0.15625
- down_weight: float32 [4096, 1536], P('wide'), may hold values from -0.09375 to 0.09375
- down_momentum: float32 [4096, 1536], P('wide'), may hold values from -448 to 448
- down_average: float32 [4096, 1536], P('wide'), may hold values from -0.09375 to 0.09375
Outputs:
- output: bfloat16 [2, 32, 256, 1536], P(None, ('narrow', 'wide'))
- input_grad: bfloat16 [2, 32, 256, 1536], P(None, ('narrow', 'wide'))
- gains_momentum_new: float32 [2, 1536], P(None, 'wide')
- gains_new: float32 [2, 1536], P(None, 'wide')
- gains_average_new: float32 [2, 1536], P(None, 'wide')
- qkv_momentum_new: float32 [3, 1536, 1536], P(None, 'wide')
- qkv_new: float32 [3, 1536, 1536], P(None, 'wide')
- qkv_average_new: float32 [3, 1536, 1536], P(None, 'wide')
- out_momentum_new: float32 [1536, 1536], P('wide')
- out_new: float32 [1536, 1536], P('wide')
- out_average_new: float32 [1536, 1536], P('wide')
- taps_momentum_new: float32 [16, 6, 11], replicated
- taps_new: float32 [16, 6, 11], replicated
- taps_average_new: float32 [16, 6, 11], replicated
- mix_momentum_new: float32 [16, 2], replicated
- mix_new: float32 [16, 2], replicated
- mix_average_new: float32 [16, 2], replicated
- gateup_momentum_new: float32 [1536, 2, 4096], P('wide')
- gateup_new: float32 [1536, 2, 4096], P('wide')
- gateup_average_new: float32 [1536, 2, 4096], P('wide')
- down_momentum_new: float32 [4096, 1536], P('wide')
- down_new: float32 [4096, 1536], P('wide')
- down_average_new: float32 [4096, 1536], P('wide')
Inputs may be any that keep to these rules, and one draw needn't show every extreme that they name: `lengths`: at least one sequence has all 256 tokens valid.
All inputs are finite; a program needn't handle non-finite values.
Results may differ from a plain program's by a relative error of at most 0.017.
The roundings to bfloat16 on the way count: a program that leaves them out, or rounds other values in their place, can miss the bound.
Values may be sent and summed in bfloat16 or wider, within the bound.
No kernel may reach another device: no remote copies, remote signals or barrier semaphores. Data moves between devices by JAX's collectives and lax.ppermute only.
A program may use at most 768 MiB of HBM per device.

v0:
```python
import math

import jax
import jax.numpy as jnp
from jax import lax
from jax.sharding import PartitionSpec as P

H = 16
E = 96
G = 2


EPSILON = 1e-05
MOMENTUM = 0.9
AVERAGE = 0.7
RATES = (0.1, 0.019, 0.19, 0.2, 0.5, 0.031, 0.0097)
PER_PAIR = (False, False, False, True, True, False, False)
HIGHEST = lax.Precision.HIGHEST


def rms_scale(values):
    return lax.rsqrt(jnp.mean(values * values, axis=-1, keepdims=True) + EPSILON)


def attention_core(raw_scores, conv_taps, head_mix, valid_len):
    seq_count = raw_scores.shape[0]
    head_count = raw_scores.shape[1]
    seq_len = raw_scores.shape[2]
    lag_count = conv_taps.shape[1]
    shift_count = conv_taps.shape[2]
    half_keys = shift_count // 2
    row_iota = lax.broadcasted_iota(jnp.int32, (seq_len, seq_len), 0)
    col_iota = lax.broadcasted_iota(jnp.int32, (seq_len, seq_len), 1)
    allowed = (col_iota <= row_iota)[None, None] & (
        col_iota[None, None] < valid_len[:, None, None, None]
    )
    masked = jnp.where(allowed, raw_scores * (1.0 / math.sqrt(E)), 0.0)
    padded = jnp.pad(masked, ((0, 0), (0, 0), (lag_count - 1, 0), (half_keys, half_keys)))
    conv_total = jnp.zeros_like(masked)
    for lag_index in range(lag_count):
        for shift_index in range(shift_count):
            row_start = lag_count - 1 - lag_index
            col_start = 2 * half_keys - shift_index
            tap_slice = padded[
                :, :, row_start : row_start + seq_len, col_start : col_start + seq_len
            ]
            conv_total = (
                conv_total + conv_taps[:, lag_index, shift_index][None, :, None, None] * tap_slice
            )
    logits = jnp.where(allowed, conv_total, -jnp.inf)
    row_top = jnp.max(logits, axis=-1, keepdims=True)
    exp_terms = jnp.exp(logits - row_top)
    softmax_out = exp_terms / jnp.sum(exp_terms, axis=-1, keepdims=True)
    grouped = softmax_out.reshape(seq_count, head_count // G, G, seq_len, seq_len)
    mixing = head_mix.reshape(head_count // G, G, G)
    blended = jnp.einsum("goi,sgikl->sgokl", mixing, grouped, precision=HIGHEST)
    return blended.reshape(seq_count, head_count, seq_len, seq_len)


def norm_back(values, scale_rows, gain_row, upstream):
    normal_rows = values * scale_rows
    gain_grad = jnp.sum(upstream * normal_rows, axis=0)
    weighted = upstream * gain_row
    values_grad = scale_rows * (
        weighted - normal_rows * jnp.mean(weighted * normal_rows, axis=-1, keepdims=True)
    )
    return (gain_grad, values_grad)


def forward_pass(
    sequences,
    valid_len,
    gains_full,
    qkv_full,
    out_full,
    conv_taps,
    head_mix,
    gateup_full,
    down_full,
):
    seq_count = sequences.shape[0]
    seq_len = sequences.shape[1]
    model_width = sequences.shape[2]
    states = sequences.reshape(seq_count * seq_len, model_width).astype(jnp.float32)
    first_scale = rms_scale(states)
    normed = (states * first_scale * gains_full[0].astype(jnp.float32)).astype(jnp.bfloat16)
    projected = jnp.einsum(
        "rd,kde->kre", normed, qkv_full, preferred_element_type=jnp.float32
    ).astype(jnp.bfloat16)
    head_split = projected.reshape(3, seq_count, seq_len, H, E)
    raw_scores = jnp.einsum(
        "sqhe,skhe->shqk", head_split[0], head_split[1], preferred_element_type=jnp.float32
    )
    mixed_low = attention_core(raw_scores, conv_taps, head_mix, valid_len).astype(jnp.bfloat16)
    context = jnp.einsum(
        "shqk,skhe->sqhe", mixed_low, head_split[2], preferred_element_type=jnp.float32
    )
    context = context.reshape(seq_count * seq_len, model_width).astype(jnp.bfloat16)
    middle = states + jnp.dot(context, out_full, preferred_element_type=jnp.float32)
    second_scale = rms_scale(middle)
    second = (middle * second_scale * gains_full[1].astype(jnp.float32)).astype(jnp.bfloat16)
    gate_up = jnp.einsum("rd,dkf->rkf", second, gateup_full, preferred_element_type=jnp.float32)
    hidden = (jax.nn.silu(gate_up[:, 0]) * gate_up[:, 1]).astype(jnp.bfloat16)
    result = middle + jnp.dot(hidden, down_full, preferred_element_type=jnp.float32)
    result = result.astype(jnp.bfloat16).reshape(seq_count, seq_len, model_width)
    kept_values = (
        states,
        first_scale,
        normed,
        projected,
        context,
        middle,
        second_scale,
        second,
        gate_up,
        hidden,
    )
    return (result, kept_values)


def backward_pass(
    kept_values,
    cotangent_mb,
    valid_len,
    gains_full,
    qkv_full,
    out_full,
    conv_taps,
    head_mix,
    gateup_full,
    down_full,
):
    (
        states,
        first_scale,
        normed,
        projected,
        context,
        middle,
        second_scale,
        second,
        gate_up,
        hidden,
    ) = kept_values
    seq_count = cotangent_mb.shape[0]
    seq_len = cotangent_mb.shape[1]
    model_width = cotangent_mb.shape[2]
    d_output = cotangent_mb.reshape(seq_count * seq_len, model_width).astype(jnp.float32)
    d_final = d_output.astype(jnp.bfloat16)
    down_grad = jnp.einsum("rf,rd->fd", hidden, d_final, preferred_element_type=jnp.float32)
    d_hidden = jnp.einsum("rd,fd->rf", d_final, down_full, preferred_element_type=jnp.float32)
    gate_part = gate_up[:, 0]
    up_part = gate_up[:, 1]
    gate_sig = jax.nn.sigmoid(gate_part)
    gate_silu = gate_part * gate_sig
    d_gate = d_hidden * up_part * gate_sig * (1.0 + gate_part * (1.0 - gate_sig))
    d_gate_up = jnp.stack([d_gate, d_hidden * gate_silu], axis=1).astype(jnp.bfloat16)
    gateup_grad = jnp.einsum("rd,rkf->dkf", second, d_gate_up, preferred_element_type=jnp.float32)
    d_second = jnp.einsum("rkf,dkf->rd", d_gate_up, gateup_full, preferred_element_type=jnp.float32)
    second_gain, d_norm_two = norm_back(
        middle, second_scale, gains_full[1].astype(jnp.float32), d_second
    )
    d_middle = d_output + d_norm_two
    d_attended = d_middle.astype(jnp.bfloat16)
    out_grad = jnp.einsum("rc,rd->cd", context, d_attended, preferred_element_type=jnp.float32)
    d_context = jnp.einsum(
        "rd,cd->rc", d_attended, out_full, preferred_element_type=jnp.float32
    ).astype(jnp.bfloat16)
    head_split = projected.reshape(3, seq_count, seq_len, H, E)
    raw_scores = jnp.einsum(
        "sqhe,skhe->shqk", head_split[0], head_split[1], preferred_element_type=jnp.float32
    )

    def core_local(score_block, tap_values, mix_values):
        return attention_core(score_block, tap_values, mix_values, valid_len)

    mixed_full, pull_back = jax.vjp(core_local, raw_scores, conv_taps, head_mix)
    mixed_low = mixed_full.astype(jnp.bfloat16)
    d_context_heads = d_context.reshape(seq_count, seq_len, H, E)
    d_value = jnp.einsum(
        "shqk,sqhe->skhe", mixed_low, d_context_heads, preferred_element_type=jnp.float32
    )
    d_mixed = jnp.einsum(
        "sqhe,skhe->shqk", d_context_heads, head_split[2], preferred_element_type=jnp.float32
    )
    d_raw, taps_grad, mix_grad = pull_back(d_mixed)
    d_raw_low = d_raw.astype(jnp.bfloat16)
    d_query = jnp.einsum(
        "shqk,skhe->sqhe", d_raw_low, head_split[1], preferred_element_type=jnp.float32
    )
    d_key = jnp.einsum(
        "shqk,sqhe->skhe", d_raw_low, head_split[0], preferred_element_type=jnp.float32
    )
    d_projected = (
        jnp.stack([d_query, d_key, d_value])
        .reshape(3, seq_count * seq_len, model_width)
        .astype(jnp.bfloat16)
    )
    qkv_grad = jnp.einsum("rd,kre->kde", normed, d_projected, preferred_element_type=jnp.float32)
    d_normed = jnp.einsum("kre,kde->rd", d_projected, qkv_full, preferred_element_type=jnp.float32)
    first_gain, d_norm_one = norm_back(
        states, first_scale, gains_full[0].astype(jnp.float32), d_normed
    )
    input_grad = (
        (d_middle + d_norm_one).astype(jnp.bfloat16).reshape(seq_count, seq_len, model_width)
    )
    gains_grad = jnp.stack([first_gain, second_gain])
    return (
        input_grad,
        (gains_grad, qkv_grad, out_grad, taps_grad, mix_grad, gateup_grad, down_grad),
    )


def add_trees(left_tree, right_tree):
    if left_tree is None:
        return right_tree
    return jax.tree.map(jnp.add, left_tree, right_tree)


def nesterov(master, moment, average, gradient, step_rate):
    new_moment = MOMENTUM * moment + gradient
    new_master = master - step_rate * (gradient + MOMENTUM * new_moment)
    return (new_moment, new_master, AVERAGE * average + (1.0 - AVERAGE) * new_master)


def on_device(
    inputs,
    cotangent,
    lengths,
    gains,
    gains_momentum,
    gains_average,
    qkv_weight,
    qkv_momentum,
    qkv_average,
    out_weight,
    out_momentum,
    out_average,
    conv_taps,
    taps_momentum,
    taps_average,
    head_mix,
    mix_momentum,
    mix_average,
    gateup_weight,
    gateup_momentum,
    gateup_average,
    down_weight,
    down_momentum,
    down_average,
):
    micro_count = inputs.shape[0]
    gains_low = gains.astype(jnp.bfloat16)
    qkv_low = qkv_weight.astype(jnp.bfloat16)
    out_low = out_weight.astype(jnp.bfloat16)
    gateup_low = gateup_weight.astype(jnp.bfloat16)
    down_low = down_weight.astype(jnp.bfloat16)
    outputs_list = []
    input_grads = []
    shared_total = None
    small_total = None
    for micro_index in range(micro_count):
        gains_full, qkv_full, out_full = (
            lax.all_gather(gains_low, "wide", axis=1, tiled=True),
            lax.all_gather(qkv_low, "wide", axis=1, tiled=True),
            lax.all_gather(out_low, "wide", axis=0, tiled=True),
        )
        gateup_full, down_full = (
            lax.all_gather(gateup_low, "wide", axis=0, tiled=True),
            lax.all_gather(down_low, "wide", axis=0, tiled=True),
        )
        valid_len = lengths[micro_index]
        result, kept_values = forward_pass(
            inputs[micro_index],
            valid_len,
            gains_full,
            qkv_full,
            out_full,
            conv_taps,
            head_mix,
            gateup_full,
            down_full,
        )
        outputs_list.append(result)
        gains_back, qkv_back, out_back = (
            lax.all_gather(gains_low, "wide", axis=1, tiled=True),
            lax.all_gather(qkv_low, "wide", axis=1, tiled=True),
            lax.all_gather(out_low, "wide", axis=0, tiled=True),
        )
        gateup_back, down_back = (
            lax.all_gather(gateup_low, "wide", axis=0, tiled=True),
            lax.all_gather(down_low, "wide", axis=0, tiled=True),
        )
        input_grad, grads = backward_pass(
            kept_values,
            cotangent[micro_index],
            valid_len,
            gains_back,
            qkv_back,
            out_back,
            conv_taps,
            head_mix,
            gateup_back,
            down_back,
        )
        input_grads.append(input_grad)
        large_part = (grads[0], grads[1], grads[2], grads[5], grads[6])
        shared_total = add_trees(shared_total, tuple(large_part))
        small_total = add_trees(small_total, (grads[3], grads[4]))
    shares = (
        lax.psum_scatter(shared_total[0], "wide", scatter_dimension=1, tiled=True),
        lax.psum_scatter(shared_total[1], "wide", scatter_dimension=1, tiled=True),
        lax.psum_scatter(shared_total[2], "wide", scatter_dimension=0, tiled=True),
        lax.psum_scatter(shared_total[3], "wide", scatter_dimension=0, tiled=True),
        lax.psum_scatter(shared_total[4], "wide", scatter_dimension=0, tiled=True),
    )
    small_sum = lax.psum((small_total[0], small_total[1]), "wide")
    reduced = (
        lax.psum(shares[0].astype(jnp.bfloat16), "narrow").astype(jnp.float32),
        lax.psum(shares[1].astype(jnp.bfloat16), "narrow").astype(jnp.float32),
        lax.psum(shares[2].astype(jnp.bfloat16), "narrow").astype(jnp.float32),
        lax.psum(shares[3].astype(jnp.bfloat16), "narrow").astype(jnp.float32),
        lax.psum(shares[4].astype(jnp.bfloat16), "narrow").astype(jnp.float32),
        lax.psum(small_sum[0].astype(jnp.bfloat16), "narrow").astype(jnp.float32),
        lax.psum(small_sum[1].astype(jnp.bfloat16), "narrow").astype(jnp.float32),
    )
    tokens_all = (
        micro_count
        * inputs.shape[1]
        * inputs.shape[2]
        * lax.axis_size("narrow")
        * lax.axis_size("wide")
    )
    seq_len = inputs.shape[2]

    def rate_for(position):
        return RATES[position] / math.sqrt(tokens_all * (seq_len if PER_PAIR[position] else 1))

    gains_out = nesterov(gains, gains_momentum, gains_average, reduced[0], rate_for(0))
    qkv_out = nesterov(qkv_weight, qkv_momentum, qkv_average, reduced[1], rate_for(1))
    out_out = nesterov(out_weight, out_momentum, out_average, reduced[2], rate_for(2))
    taps_out = nesterov(conv_taps, taps_momentum, taps_average, reduced[5], rate_for(3))
    mix_out = nesterov(head_mix, mix_momentum, mix_average, reduced[6], rate_for(4))
    gateup_out = nesterov(gateup_weight, gateup_momentum, gateup_average, reduced[3], rate_for(5))
    down_out = nesterov(down_weight, down_momentum, down_average, reduced[4], rate_for(6))
    return (
        jnp.stack(outputs_list),
        jnp.stack(input_grads),
        gains_out[0],
        gains_out[1],
        gains_out[2],
        qkv_out[0],
        qkv_out[1],
        qkv_out[2],
        out_out[0],
        out_out[1],
        out_out[2],
        taps_out[0],
        taps_out[1],
        taps_out[2],
        mix_out[0],
        mix_out[1],
        mix_out[2],
        gateup_out[0],
        gateup_out[1],
        gateup_out[2],
        down_out[0],
        down_out[1],
        down_out[2],
    )


def solution(mesh):
    in_specs = (
        P(None, ("narrow", "wide"), None, None),
        P(None, ("narrow", "wide"), None, None),
        P(None, ("narrow", "wide")),
        P(None, "wide"),
        P(None, "wide"),
        P(None, "wide"),
        P(None, "wide", None),
        P(None, "wide", None),
        P(None, "wide", None),
        P("wide", None),
        P("wide", None),
        P("wide", None),
        P(),
        P(),
        P(),
        P(),
        P(),
        P(),
        P("wide", None, None),
        P("wide", None, None),
        P("wide", None, None),
        P("wide", None),
        P("wide", None),
        P("wide", None),
    )
    out_specs = (
        P(None, ("narrow", "wide"), None, None),
        P(None, ("narrow", "wide"), None, None),
        P(None, "wide"),
        P(None, "wide"),
        P(None, "wide"),
        P(None, "wide", None),
        P(None, "wide", None),
        P(None, "wide", None),
        P("wide", None),
        P("wide", None),
        P("wide", None),
        P(),
        P(),
        P(),
        P(),
        P(),
        P(),
        P("wide", None, None),
        P("wide", None, None),
        P("wide", None, None),
        P("wide", None),
        P("wide", None),
        P("wide", None),
    )
    return jax.shard_map(
        on_device, mesh=mesh, in_specs=in_specs, out_specs=out_specs, check_vma=False
    )
```

profile of v0, /device:TPU:0, one launch (start us, length us, event | category | flops | bytes accessed | tf_op | source)
XLA Modules:
  0.0 2833.6 jit_solution(12953254845743748330)
XLA Ops:
  20.9 43.2 %all-gather = bf16[16,96,2]{1,2,0:T(2,128)(2,1)S(1)} all-gather(bf16[1,96,2]{1,2,0:T(2,128)(2,1)S(1)} %convert_bitcast_fusion), channel_id=1, replica_groups=mesh['narrow'=2,'wide'=16] {'wide'}, dimensions={0}, use_global_device_ids=true | all-gather | bytes 6528 | tf_op jit(solution)/shard_map/all_gather | solution.py:264
  66.3 114.6 %all-gather.6.cloned.1.call-done = bf16[3,1536,1536]{2,1,0:T(8,128)(2,1)} async-done(((bf16[3,96,1536]{2,1,0:T(8,128)(2,1)}), bf16[3,1536,1536]{2,1,0:T(8,128)(2,1)}) %all-gather.6.cloned.1.call-update) | async-done | bytes 14155792 | tf_op jit(solution)/shard_map/all_gather | solution.py:265
  198.5 206.1 %fusion.259 = (f32[16,256]{1,0:T(8,128)S(1)}, f32[1,16,256,256]{3,2,1,0:T(8,128)}) fusion(f32[16]{0:T(128)} %get-tuple-element.491, f32[16]{0:T(128)S(1)} %get-tuple-element.427, f32[16]{0:T(128)S(1)} %get-tuple-element.428, f32[16]{0:T(128)} %get-tuple-element.429, f32[16]{0:T(128)} %get-tuple-element.430, f32[16]{0:T(128)} %get-tuple-element.431, ...), kind=kLoop, calls=%fused_computation.806 | loop fusion | flops 141553664 | bytes 12745792 | tf_op jit(solution)/shard_map/reduce_max | solution.py:51
  448.2 203.0 %fusion.258 = (f32[16,256]{1,0:T(8,128)S(1)}, f32[1,16,256,256]{3,2,1,0:T(8,128)}) fusion(f32[16]{0:T(128)} %get-tuple-element.491, f32[16]{0:T(128)S(1)} %get-tuple-element.427, f32[16]{0:T(128)S(1)} %get-tuple-element.428, f32[16]{0:T(128)} %get-tuple-element.429, f32[16]{0:T(128)} %get-tuple-element.430, f32[16]{0:T(128)} %get-tuple-element.431, ...), kind=kLoop, calls=%fused_computation.805 | loop fusion | flops 141553664 | bytes 12745792 | tf_op jit(solution)/shard_map/reduce_max | solution.py:51
  882.4 37.0 %multiply_reduce_fusion.62 = (f32[16]{0:T(128)}, f32[16]{0:T(128)}, f32[16]{0:T(128)}, f32[16]{0:T(128)}, f32[16]{0:T(128)}, /*index=5*/f32[16]{0:T(128)}, f32[1...) fusion(f32[1,16,256,256]{3,2,1,0:T(8,128)} %fusion.87, ...), kind=kLoop, calls=%fused_computation.306 | loop fusion | flops 32505664 | bytes 17957632 | tf_op jit(solution)/shard_map/transpose(jvp())/reduce_sum | solution.py:48
  919.5 38.0 %multiply_reduce_fusion.128 = (f32[16]{0:T(128)}, f32[16]{0:T(128)}, f32[16]{0:T(128)}, f32[16]{0:T(128)}, f32[16]{0:T(128)}, /*index=5*/f32[16]{0:T(128)}, f32[...) fusion(f32[1,16,256,256]{3,2,1,0:T(8,128)} %fusion.86, ...), kind=kLoop, calls=%fused_computation.372 | loop fusion | flops 32505664 | bytes 17957632 | tf_op jit(solution)/shard_map/transpose(jvp())/reduce_sum | solution.py:48
  1033.7 35.8 %broadcast_multiply_fusion.8 = (f32[1,16,256,256]{3,2,1,0:T(8,128)}, f32[1,16,256,256]{3,2,1,0:T(8,128)}, f32[1,16,256,256]{3,2,1,0:T(8,128)}, f32[1,16,256,256]...) fusion(f32[1,16,256,256]{3,2,1,0:T(8,128)} %copy-done, ...), kind=kLoop, calls=%fused_computation.481 | loop fusion | flops 25165824 | bytes 109052672 | tf_op jit(solution)/shard_map/transpose(jvp())/mul | solution.py:48
  1069.6 117.1 %pad_add_fusion = f32[1,16,261,266]{3,2,1,0:T(8,128)S(1)} fusion(f32[1,16,256,256]{3,2,1,0:T(8,128)} %get-tuple-element.355, f32[1,16,256,256]{3,2,1,0:T(8,128)} %get-tuple-element.356, f32[1,16,256,256]{3,2,1,0:T(8,128)} %get-tuple-element.357, f32[1,16,256,256]{3,2,1,0:T(8,128)} %get-tuple-element.358, f32[1,16,256,256]{3,2,1,0:T(8,128)} %get-tuple-element.359, ...), kind=kLoop, calls=%fused_computation.134 | loop fusion | flops 65538144 | bytes 256101504 | tf_op jit(solution)/shard_map/transpose(jvp())/add_any | solution.py:44
  1214.1 26.5 broadcast_multiply_fusion.3
  1290.4 117.4 %pad_add_fusion.1 = f32[1,16,261,266]{3,2,1,0:T(8,128)S(1)} fusion(f32[1,16,256,256]{3,2,1,0:T(8,128)} %get-tuple-element.289, f32[1,16,256,256]{3,2,1,0:T(8,128)} %get-tuple-element.290, f32[1,16,256,256]{3,2,1,0:T(8,128)} %get-tuple-element.291, f32[1,16,256,256]{3,2,1,0:T(8,128)} %get-tuple-element.292, f32[1,16,256,256]{3,2,1,0:T(8,128)} %get-tuple-element.293, ...), kind=kLoop, calls=%fused_computation.135 | loop fusion | flops 65538144 | bytes 256101504 | tf_op jit(solution)/shard_map/transpose(jvp())/add_any | solution.py:44
  1460.7 40.4 %copy.234 = f32[3,1536,1536]{2,0,1:T(4,128)} copy(f32[3,1536,1536]{1,2,0:T(8,128)} %add_bitcast_fusion) | data formatting | bytes 56623104
  1501.1 29.3 %copy.236 = f32[192,8,3,1536]{3,1,2,0:T(8,128)} copy(f32[192,8,3,1536]{3,2,1,0:T(4,128)} %bitcast.731) | data formatting | bytes 56623104
  1553.7 35.0 %convolution_add_fusion = f32[1536,2,4096]{2,0,1:T(8,128)} fusion(f32[1536,2,4096]{2,0,1:T(8,128)} %fusion.111, bf16[256,1,4096]{2,0,1:T(8,128)(2,1)} %get-tuple-element.278, bf16[256,1,4096]{2,0,1:T(8,128)(2,1)} %get-tuple-element.277, f32[256,1536]{1,0:T(8,128)S(1)} %copy-done.16, f32[256]{0:T(256)S(1)} %copy-done.96, f32[1536]{0:T(1024)S(1)} %copy-done.75), kind=kOutput, calls=%fused_computation.131 | convolution fusion | flops 6464602112 | bytes 106437632 | tf_op jit(solution)/shard_map/rd,rkf->dkf/dot_general | solution.py:158
  1622.5 52.0 %fusion.173 = f32[8,2,2]{2,1,0:T(2,128)S(1)} fusion(f32[8,2,256,256]{3,2,1,0:T(8,128)} %bitcast.775, f32[1,8,2,256,256]{4,3,2,1,0:T(8,128)} %bitcast.752), kind=kOutput, calls=%fused_computation.648 | convolution fusion | flops 25165824 | bytes 8388736 | tf_op jit(solution)/shard_map/transpose(jvp(goi,sgikl->sgokl))/dot_general | solution.py:56
  1674.6 59.1 %fusion.183 = f32[8,2,2]{2,1,0:T(2,128)S(1)} fusion(f32[8,2,2]{2,1,0:T(2,128)S(1)} %fusion.173, f32[8,2,256,256]{3,2,1,0:T(8,128)S(1)} %bitcast.773, f32[1,8,2,256,256]{4,3,2,1,0:T(8,128)S(1)} %bitcast.750), kind=kOutput, calls=%fused_computation.650 | convolution fusion | flops 25165856 | bytes 8388864 | tf_op jit(solution)/shard_map/transpose(jvp(goi,sgikl->sgokl))/dot_general | solution.py:56
  1733.7 42.7 %multiply_reduce_fusion.64 = (f32[16]{0:T(128)S(1)}, f32[16]{0:T(128)S(1)}, f32[16]{0:T(128)S(1)}, f32[16]{0:T(128)S(1)}, f32[16]{0:T(128)S(1)}, /*index=5*/f32[...) fusion(f32[1,16,256,256]{3,2,1,0:T(8,128)} %copy-done, ...), kind=kLoop, calls=%fused_computation.308 | loop fusion | flops 37748448 | bytes 8389760 | tf_op jit(solution)/shard_map/transpose(jvp())/reduce_sum | solution.py:48
  1776.4 42.4 %multiply_reduce_fusion.63 = (f32[16]{0:T(128)S(1)}, f32[16]{0:T(128)S(1)}, f32[16]{0:T(128)S(1)}, f32[16]{0:T(128)S(1)}, f32[16]{0:T(128)S(1)}, /*index=5*/f32[...) fusion(f32[1,16,256,256]{3,2,1,0:T(8,128)} %copy-done, ...), kind=kLoop, calls=%fused_computation.307 | loop fusion | flops 37748448 | bytes 8389760 | tf_op jit(solution)/shard_map/transpose(jvp())/reduce_sum | solution.py:48
  1818.9 45.3 %multiply_reduce_fusion.130 = (f32[16]{0:T(128)S(1)}, f32[16]{0:T(128)S(1)}, f32[16]{0:T(128)S(1)}, f32[16]{0:T(128)S(1)}, f32[16]{0:T(128)S(1)}, /*index=5*/f32...) fusion(f32[1,16,256,256]{3,2,1,0:T(8,128)} %get-tuple-element.2, ...), kind=kLoop, calls=%fused_computation.374 | loop fusion | flops 37748448 | bytes 8389760 | tf_op jit(solution)/shard_map/transpose(jvp())/reduce_sum | solution.py:48
  1864.2 45.7 %multiply_reduce_fusion.129 = (f32[16]{0:T(128)S(1)}, f32[16]{0:T(128)S(1)}, f32[16]{0:T(128)S(1)}, f32[16]{0:T(128)S(1)}, f32[16]{0:T(128)S(1)}, /*index=5*/f32...) fusion(f32[1,16,256,256]{3,2,1,0:T(8,128)} %get-tuple-element.2, ...), kind=kLoop, calls=%fused_computation.373 | loop fusion | flops 37748448 | bytes 8389760 | tf_op jit(solution)/shard_map/transpose(jvp())/reduce_sum | solution.py:48
  1909.9 48.7 %multiply_reduce_fusion.65 = (f32[16]{0:T(128)}, f32[16]{0:T(128)}, f32[16]{0:T(128)}, f32[16]{0:T(128)}, f32[16]{0:T(128)}, /*index=5*/f32[16]{0:T(128)}, f32[1...) fusion(f32[1,16,256,256]{3,2,1,0:T(8,128)} %copy-done, ...), kind=kLoop, calls=%fused_computation.309 | loop fusion | flops 37748448 | bytes 8389760 | tf_op jit(solution)/shard_map/transpose(jvp())/reduce_sum | solution.py:48
  1958.6 49.5 %multiply_reduce_fusion.131 = (f32[16]{0:T(128)}, f32[16]{0:T(128)}, f32[16]{0:T(128)}, f32[16]{0:T(128)}, f32[16]{0:T(128)}, /*index=5*/f32[16]{0:T(128)}, f32[...) fusion(f32[1,16,256,256]{3,2,1,0:T(8,128)} %get-tuple-element.2, ...), kind=kLoop, calls=%fused_computation.375 | loop fusion | flops 37748448 | bytes 8389760 | tf_op jit(solution)/shard_map/transpose(jvp())/reduce_sum | solution.py:48
  2022.4 80.0 %all-reduce.266 = (bf16[16,6,11]{0,2,1:T(8,128)(2,1)S(1)}, bf16[16,2]{0,1:T(2,128)(2,1)S(1)}) all-reduce(f32[16,6,11]{0,2,1:T(8,128)S(1)} %add_add_fusion, f32[16,2]{0,1:T(2,128)S(1)} %copy.229), channel_id=1, replica_groups=mesh['narrow'=2,'wide'=16] {'wide'}, use_global_device_ids=true, to_apply=%region_160.161 | all-reduce | flops 1088 | bytes 6528 | tf_op jit(solution)/shard_map/psum | solution.py:317
  2111.5 519.7 %reduce-scatter.12.cloned.1.call-done = f32[96,2,4096]{2,0,1:T(8,128)} async-done(((f32[1536,2,4096]{2,0,1:T(8,128)}), f32[96,2,4096]{2,0,1:T(8,128)}) %reduce-scatter.12.cloned.1.call-update) | async-done | bytes 3145744 | tf_op jit(solution)/shard_map/reduce_scatter | solution.py:314
  2649.8 107.8 %reduce-scatter.16.cloned.1.call-done = f32[96,2]{1,0:T(8,128)} async-done(((f32[1536,2]{1,0:T(8,128)}), f32[96,2]{1,0:T(8,128)}) %reduce-scatter.16.cloned.1.call-update) | async-done | bytes 784
  (643 shorter events, 679.7 us)
Async XLA Ops:
  7.2 173.8 %all-gather.6.cloned.1.call-start = ((), (), s32[]{:S(2)}) async-start(), calls=%async_computation.5 | async-start | bytes 15040512 | tf_op jit(solution)/shard_map/all_gather | solution.py:265
  9.7 667.9 %all-gather.8.cloned.1.call-start = ((), (), s32[]{:S(2)}) async-start(), calls=%async_computation.6 | async-start | bytes 5013504 | tf_op jit(solution)/shard_map/all_gather | solution.py:266
  11.8 674.1 %all-gather.10.cloned.1.call-start = ((), (), s32[]{:S(2)}) async-start(), calls=%async_computation.7 | async-start | bytes 26738688 | tf_op jit(solution)/shard_map/all_gather | solution.py:269
  16.7 697.3 %all-gather.12.cloned.1.call-start = ((), (), s32[]{:S(2)}) async-start(), calls=%async_computation.8 | async-start | bytes 13369344 | tf_op jit(solution)/shard_map/all_gather | solution.py:270
  17.7 2084.7 %reduce-scatter.10.cloned.1.call-start = ((), (), s32[]{:S(2)}) async-start(), calls=%async_computation.9 | async-start | bytes 10027008 | tf_op jit(solution)/shard_map/reduce_scatter | solution.py:313
  18.4 429.5 %copy-start.173 = (f32[16]{0:T(128)}, f32[16]{0:T(128)S(1)}, u32[]{:S(2)}) copy-start(f32[16]{0:T(128)S(1)} %get-tuple-element.483) | copy-start | bytes 196
  19.0 428.9 %copy-start.101 = (f32[16]{0:T(128)}, f32[16]{0:T(128)S(1)}, u32[]{:S(2)}) copy-start(f32[16]{0:T(128)S(1)} %get-tuple-element.428) | copy-start | bytes 196
  19.0 428.9 %copy-start.104 = (f32[16]{0:T(128)}, f32[16]{0:T(128)S(1)}, u32[]{:S(2)}) copy-start(f32[16]{0:T(128)S(1)} %get-tuple-element.441) | copy-start | bytes 196
  19.0 428.9 %copy-start.107 = (f32[16]{0:T(128)}, f32[16]{0:T(128)S(1)}, u32[]{:S(2)}) copy-start(f32[16]{0:T(128)S(1)} %get-tuple-element.442) | copy-start | bytes 196
  19.1 428.9 %copy-start.110 = (f32[16]{0:T(128)}, f32[16]{0:T(128)S(1)}, u32[]{:S(2)}) copy-start(f32[16]{0:T(128)S(1)} %get-tuple-element.443) | copy-start | bytes 196
  19.1 428.9 %copy-start.113 = (f32[16]{0:T(128)}, f32[16]{0:T(128)S(1)}, u32[]{:S(2)}) copy-start(f32[16]{0:T(128)S(1)} %get-tuple-element.444) | copy-start | bytes 196
  19.1 428.9 %copy-start.155 = (f32[16]{0:T(128)}, f32[16]{0:T(128)S(1)}, u32[]{:S(2)}) copy-start(f32[16]{0:T(128)S(1)} %get-tuple-element.427) | copy-start | bytes 196
  19.7 428.3 %copy-start.128 = (f32[16]{0:T(128)}, f32[16]{0:T(128)S(1)}, u32[]{:S(2)}) copy-start(f32[16]{0:T(128)S(1)} %get-tuple-element.450) | copy-start | bytes 196
  19.7 428.3 %copy-start.131 = (f32[16]{0:T(128)}, f32[16]{0:T(128)S(1)}, u32[]{:S(2)}) copy-start(f32[16]{0:T(128)S(1)} %get-tuple-element.451) | copy-start | bytes 196
  19.7 428.3 %copy-start.134 = (f32[16]{0:T(128)}, f32[16]{0:T(128)S(1)}, u32[]{:S(2)}) copy-start(f32[16]{0:T(128)S(1)} %get-tuple-element.452) | copy-start | bytes 196
  19.7 428.3 %copy-start.137 = (f32[16]{0:T(128)}, f32[16]{0:T(128)S(1)}, u32[]{:S(2)}) copy-start(f32[16]{0:T(128)S(1)} %get-tuple-element.453) | copy-start | bytes 196
  19.7 428.3 %copy-start.140 = (f32[16]{0:T(128)}, f32[16]{0:T(128)S(1)}, u32[]{:S(2)}) copy-start(f32[16]{0:T(128)S(1)} %get-tuple-element.454) | copy-start | bytes 196
  64.2 697.6 %copy-start.74 = (f32[1536]{0:T(1024)}, f32[1536]{0:T(1024)S(1)}, u32[]{:S(2)}) copy-start(f32[1536]{0:T(1024)S(1)} %get-tuple-element.236) | copy-start | bytes 18436
  65.6 590.6 %copy-start.93 = (f32[8,2,2]{1,0,2:T(8,128)}, f32[8,2,2]{1,0,2:T(8,128)S(1)}, u32[]{:S(2)}) copy-start(f32[8,2,2]{1,0,2:T(8,128)S(1)} %reshape.1478) | copy-start | bytes 388
  769.7 1334.5 %reduce-scatter.14.cloned.1.call-start = ((), (), s32[]{:S(2)}) async-start(), calls=%async_computation.11 | async-start | bytes 26738688 | tf_op jit(solution)/shard_map/reduce_scatter | solution.py:315
  804.7 1302.0 %reduce-scatter.18.cloned.1.call-start = ((), (), s32[]{:S(2)}) async-start(), calls=%async_computation.13 | async-start | bytes 30081024
  1530.5 1100.7 %reduce-scatter.12.cloned.1.call-start = ((), (), s32[]{:S(2)}) async-start(), calls=%async_computation.10 | async-start | bytes 53477376 | tf_op jit(solution)/shard_map/reduce_scatter | solution.py:314
  1588.7 1169.0 %reduce-scatter.16.cloned.1.call-start = ((), (), s32[]{:S(2)}) async-start(), calls=%async_computation.12 | async-start | bytes 835584
  2008.3 776.9 %all-reduce.271.cloned.1.call-start = ((), (), s32[]{:S(2)}) async-start(), calls=%async_computation.14 | async-start | bytes 7667712 | tf_op jit(solution)/shard_map/psum | solution.py:320
  (221 other events, 11382.1 us)
Sparse Core Ops, SparseCore 0:
  11.3 169.6 all-gather.5
  184.3 78.6 all-gather.7
  266.3 269.8 all-gather.9
  539.4 150.1 all-gather.11
  769.8 169.0 reduce-scatter.9
  945.5 360.5 reduce-scatter.13
  1530.6 396.8 reduce-scatter.17
  1934.5 696.6 reduce-scatter.11
  2636.4 121.2 reduce-scatter.15
  2761.2 23.9 all-reduce.270
where the time goes:
time: 2840 us; the launch traced here: 2830 us
  other arithmetic  1270 us (45%)
  waiting for transfers between devices  762 us (27%)
  matrix products  485 us (17%)
  local copies, waits for them, and re-layouts  170 us (6%)
  blocking collectives  127 us (4%)
    reduce_scatter x1, waiting for transfers between devices, on_device(): lax.psum_scatter(shared_total[3], 'wide', scatter_dimension=0, tiled=True)  520 us
    reduce_max x2, other arithmetic, attention_core(): row_top = jnp.max(logits, axis=-1, keepdims=True)  409 us
    reduce_sum x8, other arithmetic, attention_core(): conv_taps[:, lag_index, shift_index][None, :, None, None] * tap_slice  349 us
    add_any x2, other arithmetic, attention_core(): padded[:, :, row_start:row_start + seq_len, col_start:col_start + seq_len]  234 us
    mul x7, other arithmetic, attention_core(): conv_taps[:, lag_index, shift_index][None, :, None, None] * tap_slice  187 us
    dot_general x6, matrix products, attention_core(): blended = jnp.einsum('goi,sgikl->sgokl', mixing, grouped, precision=HIGHEST)  183 us
    unnamed x490, local copies, waits for them, and re-layouts  140 us
    all_gather x1, waiting for transfers between devices, on_device(): lax.all_gather(qkv_low, 'wide', axis=1, tiled=True)  115 us
  transfers between devices with their start and end apart: 10, of which 4 were waited for; matrix products, arithmetic and copies ran while one was open for 64% of the time, Pallas kernels for 0%

commit v1 on v0

v1 whole, which is shorter than its diff:
```python
import math

import jax
import jax.numpy as jnp
from jax import lax
from jax.experimental import pallas as pl
from jax.experimental.pallas import tpu as pltpu
from jax.sharding import PartitionSpec as P

H = 16
E = 96
G = 2


EPSILON = 1e-05
MOMENTUM = 0.9
AVERAGE = 0.7
RATES = (0.1, 0.019, 0.19, 0.2, 0.5, 0.031, 0.0097)
PER_PAIR = (False, False, False, True, True, False, False)
F32 = jnp.float32
BF16 = jnp.bfloat16
SCALE = 1.0 / math.sqrt(E)


def permute(values, pairs):
    return lax.ppermute(values, "wide", pairs)


def swap_cores(values):
    return lax.ppermute(values, "narrow", [(0, 1), (1, 0)])


BLOCK = 16


def z_pairs(moves):
    return [(a * 4 + q, b * 4 + q) for a, b in moves for q in range(4)]


Z_PAIR = z_pairs([(0, 1), (1, 0), (2, 3), (3, 2)])
Z_MID = z_pairs([(1, 2), (2, 1)])
Z_OUT = z_pairs([(1, 0), (2, 3)])
Z_IN = z_pairs([(0, 1), (3, 2)])
X_PAIR = [(i, i ^ 1) for i in range(BLOCK)]
Y_PAIR = [(i, i ^ 2) for i in range(BLOCK)]


def cut_columns(columns):
    tiles = columns // 128
    return (tiles - tiles // 5) * 128


def after(values, *needed):
    def nothing(*refs):
        del refs

    return pl.pallas_call(
        nothing,
        out_shape=jax.ShapeDtypeStruct(values.shape, values.dtype),
        in_specs=[pl.BlockSpec(memory_space=pl.ANY)] * (1 + len(needed)),
        out_specs=pl.BlockSpec(memory_space=pl.ANY),
        input_output_aliases={0: 0},
    )(values, *needed)


def line_gather(piece):
    z = lax.axis_index("wide") // 4
    odd = (z % 2) == 1
    other = permute(piece, Z_PAIR)
    near = jnp.stack([jnp.where(odd, other, piece), jnp.where(odd, piece, other)])
    crossed = permute(near, Z_MID)
    handed = permute(crossed, Z_OUT)
    far = jnp.where((z == 1) | (z == 2), crossed, handed)
    return near, far


def gather_begin(piece, *needed):
    if lax.axis_size("wide") != BLOCK:
        return (piece,)
    if needed:
        piece = after(piece, *needed)
    cut = cut_columns(piece.shape[1])
    lines = [line_gather(piece[:, :cut])]
    own = piece[:, cut:]
    by_x = permute(own, X_PAIR)
    by_y = permute(own, Y_PAIR)
    plane = jnp.stack([own, by_x, by_y, permute(by_x, Y_PAIR)])
    lines.append(line_gather(plane))
    return lines


def gather_end(lines, *needed):
    count = lax.axis_size("wide")
    if count != BLOCK:
        return lax.all_gather(lines[0], "wide", axis=0, tiled=True)
    (near, far), rest = lines
    rows, cut = near.shape[1:]
    columns = cut + rest[0].shape[-1]
    if needed:
        near, far = after(near, *needed), after(far, *needed)
    me = lax.axis_index("wide")
    index = jnp.stack([me // 4, me % 4]).astype(jnp.int32)
    arrays = []
    places = []

    def place(array, pick, half, lane, low, high):
        position = [n for n, known in enumerate(arrays) if known is array]
        if not position:
            arrays.append(array)
            position = [len(arrays) - 1]
        places.append((position[0], pick, half, lane, low, high))

    for half, block in enumerate((near, far)):
        by_x = permute(block, X_PAIR)
        by_y = permute(block, Y_PAIR)
        both = permute(by_y, X_PAIR) if half == 0 else permute(by_x, Y_PAIR)
        for lane, array in enumerate((block, by_x, by_y, both)):
            place(array, None, half, lane, 0, cut)
    for half, block in enumerate(rest):
        for lane in range(4):
            place(block, lane, half, lane, cut, columns)

    def assemble(index_ref, *refs):
        out_ref, sems = refs[len(arrays)], refs[len(arrays) + 1]
        pair, lane_me = index_ref[0] // 2, index_ref[1]
        copies = []
        for n, (position, pick, half, lane, low, high) in enumerate(places):
            source = refs[position] if pick is None else refs[position].at[:, pick]
            target = out_ref.at[
                pl.ds(2 * (pair ^ half), 2), lane_me ^ lane, :, pl.ds(low, high - low)
            ]
            copies.append(pltpu.make_async_copy(source, target, sems.at[n]))
        for copy in copies:
            copy.start()
        for copy in copies:
            copy.wait()

    full = pl.pallas_call(
        assemble,
        out_shape=jax.ShapeDtypeStruct((4, 4, rows, columns), near.dtype),
        in_specs=[pl.BlockSpec(memory_space=pltpu.SMEM)]
        + [pl.BlockSpec(memory_space=pl.ANY)] * len(arrays),
        out_specs=pl.BlockSpec(memory_space=pltpu.VMEM),
        scratch_shapes=[pltpu.SemaphoreType.DMA((len(places),))],
        compiler_params=pltpu.CompilerParams(vmem_limit_bytes=48 << 20),
    )(index, *arrays)
    return full.reshape(count * rows, columns)


def fold(*terms):
    return sum(term.astype(F32) for term in terms).astype(BF16)


def trade(values, bit, pairs):
    keep = lax.dynamic_index_in_dim(values, bit, 0, keepdims=False)
    give = lax.dynamic_index_in_dim(values, 1 - bit, 0, keepdims=False)
    return fold(keep, permute(give, pairs))


def line_sum(near, far, odd):
    far = fold(far, permute(far, Z_IN))
    near = fold(near, permute(far, Z_MID))
    return trade(near, odd, Z_PAIR)


def scatter_sum(partial):
    count = lax.axis_size("wide")
    if count != BLOCK:
        return lax.psum_scatter(partial, "wide", scatter_dimension=0, tiled=True)
    me = lax.axis_index("wide")
    pair, odd, y, x = me // 8, (me // 4) % 2, (me // 2) % 2, me % 2
    columns = partial.shape[1]
    rows = partial.shape[0] // count
    cut = cut_columns(columns)
    blocks = partial.reshape(2, 2, 2, 2, rows, columns)

    def block(half, y_at, x_at):
        found = lax.dynamic_slice(
            blocks, (half, 0, y_at, x_at, 0, 0), (1, 2, 1, 1, rows, cut)
        )
        return found.reshape(2, rows, cut)

    far = fold(block(1 - pair, y, 1 - x), permute(block(1 - pair, 1 - y, 1 - x), Y_PAIR))
    far = fold(
        block(1 - pair, y, x),
        permute(block(1 - pair, 1 - y, x), Y_PAIR),
        permute(far, X_PAIR),
    )
    near = fold(block(pair, 1 - y, x), permute(block(pair, 1 - y, 1 - x), X_PAIR))
    near = fold(
        block(pair, y, x),
        permute(block(pair, y, 1 - x), X_PAIR),
        permute(near, Y_PAIR),
    )
    done = line_sum(near, far, odd)
    if columns > cut:
        rest = blocks[..., cut:]
        near = lax.dynamic_index_in_dim(rest, pair, 0, keepdims=False)
        far = lax.dynamic_index_in_dim(rest, 1 - pair, 0, keepdims=False)
        last = trade(trade(line_sum(near, far, odd), y, Y_PAIR), x, X_PAIR)
        done = jnp.concatenate([done, last], axis=1)
    return done


def gather_small(values):
    if lax.axis_size("wide") != BLOCK:
        return lax.all_gather(values, "wide")
    me = lax.axis_index("wide")
    pair, y, x = me // 8, (me // 2) % 2, me % 2

    def both(mine, other, bit):
        return jnp.where(bit == 0, jnp.stack([mine, other]), jnp.stack([other, mine]))

    row = both(values, permute(values, X_PAIR), x)
    plane = both(row, permute(row, Y_PAIR), y)
    near, far = line_gather(plane)
    return both(near, far, pair).reshape((BLOCK,) + values.shape)


def sum_small(values):
    values = values + swap_cores(values)
    if lax.axis_size("wide") != BLOCK:
        return lax.psum(values, "wide")
    z = lax.axis_index("wide") // 4
    for pairs in (X_PAIR, Y_PAIR, Z_PAIR):
        values = values + permute(values, pairs)
    total = values + permute(values, Z_MID)
    return jnp.where((z == 1) | (z == 2), total, permute(total, Z_OUT))


def allowed_mask(length, size):
    rows = lax.broadcasted_iota(jnp.int32, (size, size), 0)
    cols = lax.broadcasted_iota(jnp.int32, (size, size), 1)
    return (cols <= rows) & (cols < length)


def near_diagonal(size, reach):
    rows = lax.broadcasted_iota(jnp.int32, (size, size), 0)
    cols = lax.broadcasted_iota(jnp.int32, (size, size), 1)
    return jnp.abs(rows - cols) <= reach


def dot_nn(a, b):
    return lax.dot_general(a, b, (((1,), (0,)), ((), ())), preferred_element_type=F32)


def dot_nt(a, b):
    return lax.dot_general(a, b, (((1,), (1,)), ((), ())), preferred_element_type=F32)


def dot_tn(a, b):
    return lax.dot_general(a, b, (((0,), (0,)), ((), ())), preferred_element_type=F32)


def split_low(values):
    top = values.astype(BF16)
    return top, (values - top.astype(F32)).astype(BF16)


def attention_forward(projected, base_rows, head_mix, seq_lengths, lags, reach):
    heads = head_mix.shape[0]
    groups = heads // G
    seqs = seq_lengths.shape[0]
    size = projected.shape[0] // seqs

    def kernel(
        len_ref, mix_ref, base_ref, proj_ref, ctx_ref, p_ref,
        top_taps, low_taps, pad_top, pad_low, left_top, left_low, split, joined,
    ):
        seq = pl.program_id(0)

        @pl.when(seq == 0)
        def _():
            band = near_diagonal(size, reach)

            def build(h, carry):
                for a in range(lags):
                    row = jnp.broadcast_to(base_ref[h, a : a + 1, :], (size, size))
                    rolled = pltpu.roll(row, 0, 1, stride=1, stride_axis=0)
                    top, low = split_low(jnp.where(band, rolled, 0.0))
                    top_taps[h, a * size : (a + 1) * size, :] = top
                    low_taps[h, a * size : (a + 1) * size, :] = low
                return carry

            lax.fori_loop(0, heads, build, 0)
            pad_top[0:8, :] = jnp.zeros((8, size), F32)
            pad_low[0:8, :] = jnp.zeros((8, size), F32)

        for n in range(3 * heads):
            split[n] = proj_ref[:, n * E : (n + 1) * E]
        allowed = allowed_mask(len_ref[seq], size)

        def group_step(group, carry):
            probs = []
            for c in range(G):
                h = G * group + c
                raw = dot_nt(split[h], split[heads + h])
                masked = jnp.where(allowed, raw * SCALE, 0.0)
                top = masked.astype(BF16).astype(F32)
                pad_top[8 : 8 + size, :] = top
                pad_low[8 : 8 + size, :] = masked - top
                for a in range(lags):
                    cols = slice(a * size, (a + 1) * size)
                    left_top[:, cols] = pad_top[8 - a : 8 - a + size, :].astype(BF16)
                    left_low[:, cols] = pad_low[8 - a : 8 - a + size, :].astype(BF16)
                logits = (
                    dot_nn(left_top[...], top_taps[h])
                    + dot_nn(left_low[...], top_taps[h])
                    + dot_nn(left_top[...], low_taps[h])
                )
                logits = jnp.where(allowed, logits, -jnp.inf)
                terms = jnp.exp(logits - jnp.max(logits, axis=-1, keepdims=True))
                prob = terms * (1.0 / jnp.sum(terms, axis=-1, keepdims=True))
                p_ref[h, 0] = prob
                probs.append(prob)
            for c in range(G):
                h = G * group + c
                mixed = sum(mix_ref[h, i] * probs[i] for i in range(G))
                joined[h] = dot_nn(mixed.astype(BF16), split[2 * heads + h]).astype(BF16)
            return carry

        lax.fori_loop(0, groups, group_step, 0)
        for h in range(heads):
            ctx_ref[:, h * E : (h + 1) * E] = joined[h]

    flops = 2 * heads * seqs * size * size * (3 * lags * size + 2 * E)
    return pl.pallas_call(
        kernel,
        grid=(seqs,),
        out_shape=(
            jax.ShapeDtypeStruct((seqs * size, heads * E), BF16),
            jax.ShapeDtypeStruct((heads, seqs, size, size), F32),
        ),
        in_specs=[
            pl.BlockSpec(memory_space=pltpu.SMEM),
            pl.BlockSpec(memory_space=pltpu.SMEM),
            pl.BlockSpec((heads, 8, size), lambda s: (0, 0, 0)),
            pl.BlockSpec((size, 3 * heads * E), lambda s: (s, 0)),
        ],
        out_specs=(
            pl.BlockSpec((size, heads * E), lambda s: (s, 0)),
            pl.BlockSpec((heads, 1, size, size), lambda s: (0, s, 0, 0)),
        ),
        scratch_shapes=[
            pltpu.VMEM((heads, lags * size, size), BF16),
            pltpu.VMEM((heads, lags * size, size), BF16),
            pltpu.VMEM((size + 8, size), F32),
            pltpu.VMEM((size + 8, size), F32),
            pltpu.VMEM((size, lags * size), BF16),
            pltpu.VMEM((size, lags * size), BF16),
            pltpu.VMEM((3 * heads, size, E), BF16),
            pltpu.VMEM((heads, size, E), BF16),
        ],
        compiler_params=pltpu.CompilerParams(vmem_limit_bytes=48 << 20),
        cost_estimate=pl.CostEstimate(
            flops=flops, bytes_accessed=20 << 20, transcendentals=heads * seqs * size * size
        ),
    )(seq_lengths, head_mix, base_rows, projected)


def attention_backward(projected, probs, d_context, base_rows, head_mix, seq_lengths, lags, reach):
    heads = head_mix.shape[0]
    groups = heads // G
    seqs = seq_lengths.shape[0]
    size = projected.shape[0] // seqs

    def kernel(
        len_ref, mix_ref, base_ref, proj_ref, p_ref, dc_ref, dproj_ref, tap_ref, dmix_ref,
        back_taps, pad, left, products, split, split_dc, joined,
    ):
        seq = pl.program_id(0)
        rows = lax.broadcasted_iota(jnp.int32, (size, size), 0)
        cols = lax.broadcasted_iota(jnp.int32, (size, size), 1)

        @pl.when(seq == 0)
        def _():
            band = near_diagonal(size, reach)

            def build(h, carry):
                for a in range(lags):
                    row = jnp.broadcast_to(base_ref[h, a : a + 1, :], (size, size))
                    rolled = pltpu.roll(row, 0, 1, stride=1, stride_axis=0)
                    back_taps[h, a * size : (a + 1) * size, :] = jnp.where(
                        band, rolled, 0.0
                    ).astype(BF16)
                products[h] = jnp.zeros((size, lags * size), F32)
                return carry

            lax.fori_loop(0, heads, build, 0)
            pad[size : size + 8, :] = jnp.zeros((8, size), F32)
            dmix_ref[...] = jnp.zeros_like(dmix_ref)

        for n in range(3 * heads):
            split[n] = proj_ref[:, n * E : (n + 1) * E]
        for h in range(heads):
            split_dc[h] = dc_ref[:, h * E : (h + 1) * E]
        allowed = allowed_mask(len_ref[seq], size)
        reverse = (rows + cols == size - 1).astype(F32).astype(BF16)

        def group_step(group, carry):
            d_probs = [None] * G
            sums = []
            for c in range(G):
                h = G * group + c
                d_mixed = dot_nt(split_dc[h], split[2 * heads + h])
                mixed = sum(mix_ref[h, i] * p_ref[G * group + i, 0] for i in range(G))
                joined[2 * heads + h] = dot_tn(mixed.astype(BF16), split_dc[h]).astype(BF16)
                for i in range(G):
                    prob = p_ref[G * group + i, 0]
                    sums.append(jnp.sum(d_mixed * prob, axis=0, keepdims=True))
                    term = mix_ref[h, i] * d_mixed
                    d_probs[i] = term if d_probs[i] is None else d_probs[i] + term
            sums.append(jnp.zeros((8 - G * G, size), F32))
            dmix_ref[group] += jnp.concatenate(sums, axis=0)
            for c in range(G):
                h = G * group + c
                prob = p_ref[h, 0]
                weighted = prob * d_probs[c]
                pad[0:size, :] = weighted - prob * jnp.sum(weighted, axis=-1, keepdims=True)
                for a in range(lags):
                    left[:, a * size : (a + 1) * size] = pad[a : a + size, :].astype(BF16)
                d_masked = dot_nn(left[...], back_taps[h])
                raw = dot_nt(split[h], split[heads + h])
                masked = jnp.where(allowed, raw * SCALE, 0.0).astype(BF16)
                turned = dot_nn(masked, reverse).astype(BF16)
                products[h] += dot_tn(turned, left[...])
                d_raw = jnp.where(allowed, d_masked * SCALE, 0.0).astype(BF16)
                joined[h] = dot_nn(d_raw, split[heads + h]).astype(BF16)
                joined[heads + h] = dot_tn(d_raw, split[h]).astype(BF16)
            return carry

        lax.fori_loop(0, groups, group_step, 0)
        for n in range(3 * heads):
            dproj_ref[:, n * E : (n + 1) * E] = joined[n]

        @pl.when(seq == seqs - 1)
        def _():
            band = jnp.abs(size - 1 - rows - cols) <= reach

            def collect(h, carry):
                for a in range(lags):
                    kept = jnp.where(band, products[h, :, a * size : (a + 1) * size], 0.0)
                    rolled = pltpu.roll(kept, 0, 1, stride=1, stride_axis=0)
                    tap_ref[h, a : a + 1, :] = jnp.sum(rolled, axis=0, keepdims=True)
                tap_ref[h, lags:8, :] = jnp.zeros((8 - lags, size), F32)
                return carry

            lax.fori_loop(0, heads, collect, 0)

    flops = 2 * heads * seqs * size * size * ((2 * lags + 1) * size + 5 * E)
    d_projected, taps_rows, mix_rows = pl.pallas_call(
        kernel,
        grid=(seqs,),
        out_shape=(
            jax.ShapeDtypeStruct(projected.shape, BF16),
            jax.ShapeDtypeStruct((heads, 8, size), F32),
            jax.ShapeDtypeStruct((groups, 8, size), F32),
        ),
        in_specs=[
            pl.BlockSpec(memory_space=pltpu.SMEM),
            pl.BlockSpec(memory_space=pltpu.SMEM),
            pl.BlockSpec((heads, 8, size), lambda s: (0, 0, 0)),
            pl.BlockSpec((size, 3 * heads * E), lambda s: (s, 0)),
            pl.BlockSpec((heads, 1, size, size), lambda s: (0, s, 0, 0)),
            pl.BlockSpec((size, heads * E), lambda s: (s, 0)),
        ],
        out_specs=(
            pl.BlockSpec((size, 3 * heads * E), lambda s: (s, 0)),
            pl.BlockSpec((heads, 8, size), lambda s: (0, 0, 0)),
            pl.BlockSpec((groups, 8, size), lambda s: (0, 0, 0)),
        ),
        scratch_shapes=[
            pltpu.VMEM((heads, lags * size, size), BF16),
            pltpu.VMEM((size + 8, size), F32),
            pltpu.VMEM((size, lags * size), BF16),
            pltpu.VMEM((heads, size, lags * size), F32),
            pltpu.VMEM((3 * heads, size, E), BF16),
            pltpu.VMEM((heads, size, E), BF16),
            pltpu.VMEM((3 * heads, size, E), BF16),
        ],
        compiler_params=pltpu.CompilerParams(vmem_limit_bytes=52 << 20),
        cost_estimate=pl.CostEstimate(
            flops=flops, bytes_accessed=20 << 20, transcendentals=0
        ),
    )(seq_lengths, head_mix, base_rows, projected, probs, d_context)
    shifts = 2 * reach + 1
    at = [(size - 1 - reach + b) % size for b in range(shifts)]
    taps_grad = jnp.stack([taps_rows[:, :lags, i] for i in at], axis=-1)
    mix_grad = jnp.sum(mix_rows[:, : G * G], axis=-1).reshape(heads, G)
    return d_projected, taps_grad, mix_grad


def base_rows_of(taps, size, turned):
    heads, lags, shifts = taps.shape
    reach = shifts // 2
    rows = taps[:, :, ::-1] if turned else taps
    rows = jnp.concatenate(
        [rows[:, :, reach:], jnp.zeros((heads, lags, size - shifts), F32), rows[:, :, :reach]],
        axis=-1,
    )
    return jnp.pad(rows, ((0, 0), (0, 8 - lags), (0, 0)))


HIDDEN_BLOCK = 256


def feed_forward(second, second_turned, d_final, gateup, down):
    tokens, width = second.shape
    hidden_count = down.shape[0]
    block = HIDDEN_BLOCK
    part = tokens // 2

    def kernel(x_ref, xt_ref, d_ref, gu_ref, down_ref, hidden_ref, dgu_ref, grad_ref):
        for m in range(0, tokens, part):
            rows = slice(m, m + part)
            gate_up = dot_nn(x_ref[rows, :], gu_ref[...])
            gate, up = gate_up[:, :block], gate_up[:, block:]
            sig = jax.nn.sigmoid(gate)
            silu = gate * sig
            hidden_ref[rows, :] = (silu * up).astype(BF16)
            d_hidden = dot_nt(d_ref[rows, :], down_ref[...])
            d_gate = d_hidden * up * sig * (1.0 + gate * (1.0 - sig))
            dgu_ref[rows, :block] = d_gate.astype(BF16)
            dgu_ref[rows, block:] = (d_hidden * silu).astype(BF16)
        grad_ref[...] = dot_nn(xt_ref[...], dgu_ref[...]).astype(BF16)

    def whole(shape):
        return pl.BlockSpec(shape, lambda j: (0, 0), pipeline_mode=pl.Buffered(1))

    return pl.pallas_call(
        kernel,
        grid=(hidden_count // block,),
        out_shape=(
            jax.ShapeDtypeStruct((tokens, hidden_count), BF16),
            jax.ShapeDtypeStruct((tokens, 2 * hidden_count), BF16),
            jax.ShapeDtypeStruct((width, 2 * hidden_count), BF16),
        ),
        in_specs=[
            whole((tokens, width)),
            whole((width, tokens)),
            whole((tokens, width)),
            pl.BlockSpec((width, 2 * block), lambda j: (0, j)),
            pl.BlockSpec((block, width), lambda j: (j, 0)),
        ],
        out_specs=(
            pl.BlockSpec((tokens, block), lambda j: (0, j)),
            pl.BlockSpec((tokens, 2 * block), lambda j: (0, j)),
            pl.BlockSpec((width, 2 * block), lambda j: (0, j)),
        ),
        compiler_params=pltpu.CompilerParams(vmem_limit_bytes=52 << 20),
        cost_estimate=pl.CostEstimate(
            flops=10 * tokens * width * hidden_count,
            bytes_accessed=48 << 20,
            transcendentals=tokens * hidden_count,
        ),
    )(second, second_turned, d_final, gateup, down)


def rms_scale(values):
    return lax.rsqrt(jnp.mean(values * values, axis=-1, keepdims=True) + EPSILON)


def norm_back(values, scale_rows, gain_row, upstream):
    normal_rows = values * scale_rows
    gain_grad = jnp.sum(upstream * normal_rows, axis=0)
    weighted = upstream * gain_row
    values_grad = scale_rows * (
        weighted - normal_rows * jnp.mean(weighted * normal_rows, axis=-1, keepdims=True)
    )
    return (gain_grad, values_grad)


def matmul(a, b, dims, out=F32):
    return lax.dot_general(a, b, (dims, ((), ())), preferred_element_type=F32).astype(out)


def nesterov(master, moment, average, gradient, step_rate):
    new_moment = MOMENTUM * moment + gradient
    new_master = master - step_rate * (gradient + MOMENTUM * new_moment)
    return (new_moment, new_master, AVERAGE * average + (1.0 - AVERAGE) * new_master)


def on_device(
    inputs,
    cotangent,
    lengths,
    gains,
    gains_momentum,
    gains_average,
    qkv_weight,
    qkv_momentum,
    qkv_average,
    out_weight,
    out_momentum,
    out_average,
    conv_taps,
    taps_momentum,
    taps_average,
    head_mix,
    mix_momentum,
    mix_average,
    gateup_weight,
    gateup_momentum,
    gateup_average,
    down_weight,
    down_momentum,
    down_average,
):
    micro_count, seq_count, seq_len, width = inputs.shape
    lags, shifts = conv_taps.shape[1:]
    reach = shifts // 2
    core = lax.axis_index("narrow")
    me = lax.axis_index("wide")
    wide = lax.axis_size("wide")
    cores = lax.axis_size("narrow")
    rows = width // wide
    own_heads = H // cores
    own_cols = own_heads * E
    hidden_all = gateup_weight.shape[2]
    own_hidden = hidden_all // cores
    units = hidden_all // (wide * cores)
    tokens = micro_count * seq_count * seq_len

    def by_core(mine, other, axis):
        return jnp.where(
            core == 0,
            jnp.concatenate([mine, other], axis=axis),
            jnp.concatenate([other, mine], axis=axis),
        )

    def core_part(values, axis):
        return lax.dynamic_index_in_dim(values, core, axis, keepdims=False)

    def other_part(values, axis):
        return lax.dynamic_index_in_dim(values, 1 - core, axis, keepdims=False)

    def rows_of_core(values, axis):
        shape = values.shape
        split = values.reshape(
            shape[:axis] + (cores, shape[axis] // cores) + shape[axis + 1 :]
        )
        return core_part(split, axis), other_part(split, axis)

    gains_full = gather_small(gains.astype(BF16)).transpose(1, 0, 2)
    gains_full = gains_full.reshape(2, width).astype(F32)
    qkv_piece = rows_of_core(qkv_weight.astype(BF16).transpose(1, 0, 2), 2)[0]
    qkv_piece = qkv_piece.reshape(rows, 3 * own_cols)
    out_piece = rows_of_core(out_weight.astype(BF16), 0)[0]
    group = HIDDEN_BLOCK // units
    gateup_split = gateup_weight.astype(BF16).reshape(rows, 2, wide // group, group, cores, units)
    gateup_piece = core_part(gateup_split, 4).transpose(0, 2, 1, 3, 4)
    gateup_piece = gateup_piece.reshape(rows, 2 * own_hidden)
    down_piece = rows_of_core(down_weight.astype(BF16), 0)[0]

    half = rows // cores
    qkv_lines = gather_begin(qkv_piece)
    rows_lines = gather_begin(jnp.concatenate([out_piece, down_piece]), qkv_lines[0][0])
    gateup_lines = gather_begin(gateup_piece, rows_lines[0][0])
    qkv_full = gather_end(qkv_lines)
    rows_full = gather_end(rows_lines, qkv_full)
    rows_full = rows_full.reshape(wide, half + units, width)
    out_half = rows_full[:, :half]
    out_full = by_core(out_half[:, None], swap_cores(out_half)[:, None], 1)
    out_full = out_full.reshape(width, width)
    down_full = rows_full[:, half:].reshape(own_hidden, width)

    states = inputs.reshape(tokens, width).astype(F32)
    first_scale = rms_scale(states)
    normed_own = (states * first_scale * gains_full[0]).astype(BF16)
    normed = jnp.concatenate([normed_own, swap_cores(normed_own)])
    d_final_own = cotangent.reshape(tokens, width)
    d_final = jnp.concatenate([d_final_own, swap_cores(d_final_own)])
    lengths_own = lengths.reshape(-1)
    seq_lengths = jnp.concatenate([lengths_own, swap_cores(lengths_own)])
    all_tokens = cores * tokens

    taps_own = rows_of_core(conv_taps, 0)[0]
    mix_own = rows_of_core(head_mix, 0)[0]

    projected = matmul(normed, qkv_full, ((1,), (0,)), BF16)
    context_own, probs = attention_forward(
        projected, base_rows_of(taps_own, seq_len, False), mix_own, seq_lengths, lags, reach
    )
    gateup_full = gather_end(gateup_lines, context_own)
    context = by_core(context_own[:tokens], swap_cores(context_own[tokens:]), 1)
    middle = states + matmul(context, out_full, ((1,), (0,)))
    second_scale = rms_scale(middle)
    second_own = (middle * second_scale * gains_full[1]).astype(BF16)
    second = jnp.concatenate([second_own, swap_cores(second_own)])

    hidden, d_gate_up, gateup_grad = feed_forward(
        second, second.T, d_final, gateup_full, down_full
    )
    gateup_share = lax.psum_scatter(gateup_grad, "wide", scatter_dimension=0, tiled=True)
    down_grad = matmul(hidden, d_final, ((0,), (0,)), BF16)
    d_second_parts = matmul(d_gate_up, gateup_full, ((1,), (1,)))
    d_second = d_second_parts[:tokens] + swap_cores(d_second_parts[tokens:])
    result_parts = matmul(hidden, down_full, ((1,), (0,)))
    output = middle + (result_parts[:tokens] + swap_cores(result_parts[tokens:]))
    output = output.astype(BF16).reshape(inputs.shape)

    d_output = d_final_own.astype(F32)
    second_gain, d_norm_two = norm_back(middle, second_scale, gains_full[1], d_second)
    d_middle = d_output + d_norm_two
    d_attended = d_middle.astype(BF16)
    d_context = matmul(d_attended, out_full, ((1,), (1,)), BF16)
    mine, theirs = rows_of_core(d_context, 1)
    d_context_all = jnp.concatenate([mine, swap_cores(theirs)])
    out_grad = matmul(context, d_attended, ((0,), (0,)), BF16).reshape(wide, rows, width)
    out_mine, out_theirs = rows_of_core(out_grad, 1)
    out_grad = fold(out_mine, swap_cores(out_theirs))
    rows_grad = jnp.concatenate([out_grad, down_grad.reshape(wide, units, width)], axis=1)
    rows_share = scatter_sum(rows_grad.reshape(-1, width))
    out_share, down_share = rows_share[:half], rows_share[half:]

    d_projected, taps_grad, mix_grad = attention_backward(
        projected,
        probs,
        d_context_all,
        base_rows_of(taps_own, seq_len, True),
        mix_own,
        seq_lengths,
        lags,
        reach,
    )
    qkv_grad = matmul(normed, d_projected, ((0,), (0,)), BF16)
    qkv_share = scatter_sum(qkv_grad)
    d_normed_parts = matmul(d_projected, qkv_full, ((1,), (1,)))
    d_normed = d_normed_parts[:tokens] + swap_cores(d_normed_parts[tokens:])
    first_gain, d_norm_one = norm_back(states, first_scale, gains_full[0], d_normed)
    input_grad = (d_middle + d_norm_one).astype(BF16).reshape(inputs.shape)

    def spread(values):
        held = jnp.zeros((cores,) + values.shape, F32)
        return lax.dynamic_update_index_in_dim(held, values, core, 0).reshape(-1)

    packed = jnp.concatenate([first_gain, second_gain, spread(taps_grad), spread(mix_grad)])
    packed = sum_small(packed)
    gains_grad = lax.dynamic_slice_in_dim(
        packed[: 2 * width].reshape(2, width), me * rows, rows, axis=1
    )
    taps_total = packed[2 * width : 2 * width + conv_taps.size].reshape(conv_taps.shape)
    mix_total = packed[2 * width + conv_taps.size :].reshape(head_mix.shape)

    qkv_other = swap_cores(qkv_share)
    qkv_total = by_core(
        qkv_share.reshape(rows, 3, own_cols), qkv_other.reshape(rows, 3, own_cols), 2
    ).transpose(1, 0, 2)
    rows_other = swap_cores(rows_share)
    out_total = by_core(out_share, rows_other[:half], 0)
    gateup_other = swap_cores(gateup_share)
    split_shape = (rows, wide // group, 2, group, 1, units)
    gateup_total = by_core(
        gateup_share.reshape(split_shape), gateup_other.reshape(split_shape), 4
    ).transpose(0, 2, 1, 3, 4, 5).reshape(gateup_weight.shape)
    down_total = by_core(down_share, rows_other[half:], 0)

    tokens_all = tokens * cores * wide

    def rate_for(position):
        return RATES[position] / math.sqrt(tokens_all * (seq_len if PER_PAIR[position] else 1))

    def step(master, moment, average, gradient, position):
        return nesterov(master, moment, average, gradient.astype(F32), rate_for(position))

    return (
        output,
        input_grad,
        *step(gains, gains_momentum, gains_average, gains_grad, 0),
        *step(qkv_weight, qkv_momentum, qkv_average, qkv_total, 1),
        *step(out_weight, out_momentum, out_average, out_total, 2),
        *step(conv_taps, taps_momentum, taps_average, taps_total, 3),
        *step(head_mix, mix_momentum, mix_average, mix_total, 4),
        *step(gateup_weight, gateup_momentum, gateup_average, gateup_total, 5),
        *step(down_weight, down_momentum, down_average, down_total, 6),
    )


def solution(mesh):
    batch = P(None, ("narrow", "wide"), None, None)
    gain = P(None, "wide")
    qkv = P(None, "wide", None)
    row = P("wide", None)
    row3 = P("wide", None, None)
    params = (gain,) * 3 + (qkv,) * 3 + (row,) * 3 + (P(),) * 6 + (row3,) * 3 + (row,) * 3
    return jax.shard_map(
        on_device,
        mesh=mesh,
        in_specs=(batch, batch, P(None, ("narrow", "wide"))) + params,
        out_specs=(batch, batch) + params,
        check_vma=False,
    )
```

time: 2840 us -> 869 us (0.31)
  other arithmetic: 1270 us -> 111 us
  waiting for transfers between devices: 762 us -> 304 us
  matrix products: 485 us -> 77.8 us
  Pallas kernels: 0 us -> 148 us
  blocking collectives: 127 us -> 0 us
  starting transfers between devices: 0.41 us -> 113 us
  local copies, waits for them, and re-layouts: 170 us -> 88.7 us
    reduce_scatter x3 -> x1, waiting for transfers between devices: 520 us -> 0.02 us  [on_device(): lax.psum_scatter(gateup_grad, 'wide', scatter_dimension=0, tiled=True)]
    reduce_max x2 -> x0, other arithmetic: 409 us -> none  [attention_core(): row_top = jnp.max(logits, axis=-1, keepdims=True)]
    dot_general x42 -> x9, matrix products: 485 us -> 77.8 us  [matmul(): lax.dot_general(a, b, (dims, ((), ())), preferred_element_type=F32)]
    reduce_sum x14 -> x3, other arithmetic: 366 us -> 7.9 us  [the longest x2 7.82 us: norm_back(): gain_grad = jnp.sum(upstream * normal_rows, axis=0)]
    ppermute x0 -> x98, waiting for transfers between devices: none -> 304 us  [the longest x83 304 us: permute(): return lax.ppermute(values, 'wide', pairs)]
    add_any x2 -> x0, other arithmetic: 234 us -> none  [attention_core(): padded[:, :, row_start:row_start + seq_len, col_start:col_start + seq_len]]
    mul x8 -> x0, other arithmetic: 187 us -> none  [the longest x7 187 us: attention_core(): conv_taps[:, lag_index, shift_index][None, :, None, None] * tap_slice]
    pallas_call x0 -> x12, Pallas kernels: none -> 148 us  [the longest x1 47 us: attention_backward(): pl.pallas_call(kernel, grid=(seqs,), out_shape=(jax.ShapeDtypeStruct(proj...]
  transfers between devices with their start and end apart: 10 -> 99, of which waited for: 4 -> 36; matrix products, arithmetic and copies ran while one was open for 64% -> 23% of each run, Pallas kernels for 0% -> 13%
where the time goes in v1:
time: 869 us; the launch traced here: 859 us
  waiting for transfers between devices  304 us (35%)
  Pallas kernels  148 us (17%)
  starting transfers between devices  113 us (13%)
  other arithmetic  111 us (13%)
  local copies, waits for them, and re-layouts  88.7 us (10%)
  matrix products  77.8 us (9%)
  between operations  16.6 us (2%)
    ppermute x83, waiting for transfers between devices, permute(): return lax.ppermute(values, 'wide', pairs)  304 us
    ppermute x83, starting transfers between devices, permute(): return lax.ppermute(values, 'wide', pairs)  111 us
    dot_general x9, matrix products, matmul(): lax.dot_general(a, b, (dims, ((), ())), preferred_element_type=F32)  77.8 us
    pallas_call x1, Pallas kernels, attention_backward(): pl.pallas_call(kernel, grid=(seqs,), out_shape=(jax.ShapeDtypeStruct(proj...  47 us
    pallas_call x1, Pallas kernels, feed_forward(): pl.pallas_call(kernel, grid=(hidden_count // block,), out_shape=(jax.Shap...  40.7 us
    pallas_call x1, Pallas kernels, attention_forward(): pl.pallas_call(kernel, grid=(seqs,), out_shape=(jax.ShapeDtypeStruct((seq...  40.5 us
    unnamed x244, local copies, waits for them, and re-layouts  30.1 us
    add x7, other arithmetic, nesterov(): AVERAGE * average + (1.0 - AVERAGE) * new_master  27.7 us
  transfers between devices with their start and end apart: 99, of which 36 were waited for; matrix products, arithmetic and copies ran while one was open for 23% of the time, Pallas kernels for 13%

profile of v1, /device:TPU:0, one launch (start us, length us, event | category | flops | bytes accessed | tf_op | source)
XLA Modules:
  0.0 859.3 jit_solution(9328104024012710293)
XLA Ops:
  101.6 24.5 %collective-permute-done.21 = bf16[2,4,96,384]{3,2,1,0:T(8,128)(2,1)S(1)} collective-permute-done((bf16[2,4,96,384]{3,2,1,0:T(8,128)(2,1)S(1)}, bf16[2,4,96,384]{3,2,1,0:T(8,128)(2,1)S(1)}, u32[]{:S(2)}, u32[]{:S(2)}) %collective-permute-start.21) | collective-permute-done | bytes 589856 | tf_op jit(solution)/shard_map/ppermute | solution.py:26
  130.9 14.4 %collective-permute-done.14.refs_6_ = bf16[2,96,1920]{2,1,0:T(8,128)(2,1)S(1)} collective-permute-done((bf16[2,96,1920]{2,1,0:T(8,128)(2,1)S(1)}, bf16[2,96,1920]{2,1,0:T(8,128)(2,1)S(1)}, u32[]{:S(2)}, u32[]{:S(2)}) %collective-permute-start.14) | collective-permute-done | bytes 737312 | tf_op jit(solution)/shard_map/ppermute | solution.py:26
  169.6 13.3 %collective-permute-done.29.refs_5_ = bf16[2,176,1280]{2,1,0:T(8,128)(2,1)} collective-permute-done((bf16[2,176,1280]{2,1,0:T(8,128)(2,1)}, bf16[2,176,1280]{2,1,0:T(8,128)(2,1)}, u32[]{:S(2)}, u32[]{:S(2)}) %collective-permute-start.29) | collective-permute-done | bytes 901152 | tf_op jit(solution)/shard_map/ppermute | solution.py:26
  184.7 12.9 %convolution_convert_fusion.3.proj_ref = bf16[1024,2304]{1,0:T(8,128)(2,1)} fusion(bf16[1536,2304]{1,0:T(8,128)(2,1)} %bitcast.292, bf16[512,1536]{1,0:T(8,128)(2,1)} %collective-permute-done.6, bf16[512,1536]{1,0:T(8,128)(2,1)} %multiply_convert_fusion.1), kind=kOutput, calls=%fused_computation.19 | convolution fusion | flops 7256408064 | bytes 14942208 | tf_op jit(solution)/shard_map/dot_general | solution.py:574
  205.9 14.9 %collective-permute-done.31.refs_7_ = bf16[2,176,1280]{2,1,0:T(8,128)(2,1)S(1)} collective-permute-done((bf16[2,176,1280]{2,1,0:T(8,128)(2,1)}, bf16[2,176,1280]{2,1,0:T(8,128)(2,1)S(1)}, u32[]{:S(2)}, u32[]{:S(2)}) %collective-permute-start.31) | collective-permute-done | bytes 901152 | tf_op jit(solution)/shard_map/ppermute | solution.py:26
  232.4 40.5 %shard_map.408 = (bf16[1024,768]{1,0:T(8,128)(2,1)S(1)}, f32[8,4,256,256]{3,2,1,0:T(8,128)}) custom-call(s32[4]{0:T(128)S(1)} %pad_add_fusion.len_ref, f32[8,2]{1,0:T(8,128)S(1)} %copy.119.mix_ref, f32[8,8,256]{2,1,0:T(8,128)S(1)} %pad.7.base_ref, bf16[1024,2304]{1,0:T(8,128)(2,1)} %convolution_convert_fusion.3.proj_ref), custom_call_target="tpu_custom_call" | custom-call | flops 20132659200 | bytes 20971520 | tf_op jit(solution)/shard_map/pallas_call | solution.py:327
  292.0 13.2 %collective-permute-done.43.refs_2_ = bf16[2,96,3328]{2,1,0:T(8,128)(2,1)} collective-permute-done((bf16[2,96,3328]{2,1,0:T(8,128)(2,1)}, bf16[2,96,3328]{2,1,0:T(8,128)(2,1)}, u32[]{:S(2)}, u32[]{:S(2)}) %collective-permute-start.43) | collective-permute-done | bytes 1277984 | tf_op jit(solution)/shard_map/ppermute | solution.py:26
  322.4 15.8 %collective-permute-done.42.refs_1_ = bf16[2,96,3328]{2,1,0:T(8,128)(2,1)S(1)} collective-permute-done((bf16[2,96,3328]{2,1,0:T(8,128)(2,1)S(1)}, bf16[2,96,3328]{2,1,0:T(8,128)(2,1)S(1)}, u32[]{:S(2)}, u32[]{:S(2)}) %collective-permute-start.42) | collective-permute-done | bytes 1277984 | tf_op jit(solution)/shard_map/ppermute | solution.py:26
  338.2 26.4 %collective-permute-done.44.refs_3_ = bf16[2,96,3328]{2,1,0:T(8,128)(2,1)S(1)} collective-permute-done((bf16[2,96,3328]{2,1,0:T(8,128)(2,1)}, bf16[2,96,3328]{2,1,0:T(8,128)(2,1)S(1)}, u32[]{:S(2)}, u32[]{:S(2)}) %collective-permute-start.44) | collective-permute-done | bytes 1277984 | tf_op jit(solution)/shard_map/ppermute | solution.py:26
  379.3 40.7 %shard_map.417 = (bf16[1024,2048]{1,0:T(8,128)(2,1)}, bf16[1024,4096]{1,0:T(8,128)(2,1)}, bf16[1536,4096]{1,0:T(8,128)(2,1)}) custom-call(bf16[1024,1536]{1,0:T(8,128)(2,1)} %get-tuple-element.151.x_ref, bf16[1536,1024]{1,0:T(8,128)(2,1)} %copy.121.xt_ref, bf16[1024,1536]{1,0:T(8,128)(2,1)} %pad_maximum_fusion.2.d_ref, bf16[1536,4096]{1,0:T(8,128)(2,1)} %bitcast.301, ...), custom_call_target="tpu_custom_call" | custom-call | flops 32212254720 | bytes 50331648 | tf_op jit(solution)/shard_map/pallas_call | solution.py:530
  420.0 16.6 %fusion.67 = f32[1024,1536]{1,0:T(8,128)S(1)} fusion(bf16[1024,4096]{1,0:T(8,128)(2,1)} %get-tuple-element.33, bf16[1536,4096]{1,0:T(8,128)(2,1)} %bitcast.302), kind=kOutput, calls=%fused_computation.251 | convolution fusion | flops 12884901888 | bytes 27262976 | tf_op jit(solution)/shard_map/dot_general | solution.py:574
  478.7 9.0 %convolution_convert_fusion.1 = bf16[2048,1536]{1,0:T(8,128)(2,1)S(1)} fusion(bf16[1024,2048]{1,0:T(8,128)(2,1)S(1)} %copy-done.101, bf16[512,1536]{1,0:T(8,128)(2,1)} %collective-permute-done.40, bf16[512,1536]{1,0:T(8,128)(2,1)} %bitcast.46), kind=kOutput, calls=%fused_computation.17 | convolution fusion | flops 6451888128 | bytes 13631488 | tf_op jit(solution)/shard_map/dot_general | solution.py:574
  497.8 47.0 %shard_map.418 = (bf16[1024,2304]{1,0:T(8,128)(2,1)}, f32[8,8,256]{2,1,0:T(8,128)S(1)}, f32[4,8,256]{2,1,0:T(8,128)S(1)}) custom-call(s32[4]{0:T(128)S(1)} %pad_add_fusion.len_ref, f32[8,2]{1,0:T(8,128)S(1)} %copy.119.mix_ref, f32[8,8,256]{2,1,0:T(8,128)S(1)} %pad.8.base_ref, bf16[1024,2304]{1,0:T(8,128)(2,1)} %convolution_convert_fusion.3.proj_ref, ...), custom_call_target="tpu_custom_call" | custom-call | flops 15971909632 | bytes 20971520 | tf_op jit(solution)/shard_map/pallas_call | solution.py:451
  544.8 10.9 %convolution_convert_fusion = bf16[1536,2304]{1,0:T(8,128)(2,1)S(1)} fusion(bf16[1024,2304]{1,0:T(8,128)(2,1)} %get-tuple-element.35, bf16[512,1536]{1,0:T(8,128)(2,1)} %collective-permute-done.6, bf16[512,1536]{1,0:T(8,128)(2,1)} %multiply_convert_fusion.1), kind=kOutput, calls=%fused_computation.8 | convolution fusion | flops 7257587712 | bytes 14942208 | tf_op jit(solution)/shard_map/dot_general | solution.py:574
  571.3 9.6 %fusion.68 = f32[1024,1536]{1,0:T(8,128)} fusion(bf16[1024,2304]{1,0:T(8,128)(2,1)S(1)} %bitcast.360, bf16[1536,2304]{1,0:T(8,128)(2,1)S(1)} %bitcast.295), kind=kOutput, calls=%fused_computation.252 | convolution fusion | flops 7247757312 | bytes 18087936 | tf_op jit(solution)/shard_map/dot_general | solution.py:574
  595.8 16.9 %collective-permute-done.77 = bf16[2,2,96,384]{3,2,1,0:T(8,128)(2,1)} collective-permute-done((bf16[2,2,96,384]{3,2,1,0:T(8,128)(2,1)}, bf16[2,2,96,384]{3,2,1,0:T(8,128)(2,1)}, u32[]{:S(2)}, u32[]{:S(2)}) %collective-permute-start.77) | collective-permute-done | bytes 294944 | tf_op jit(solution)/shard_map/ppermute | solution.py:26
  632.7 14.1 %collective-permute-done.72 = bf16[2,96,1920]{2,1,0:T(8,128)(2,1)S(1)} collective-permute-done((bf16[2,96,1920]{2,1,0:T(8,128)(2,1)S(1)}, bf16[2,96,1920]{2,1,0:T(8,128)(2,1)S(1)}, u32[]{:S(2)}, u32[]{:S(2)}) %collective-permute-start.72) | collective-permute-done | bytes 737312 | tf_op jit(solution)/shard_map/ppermute | solution.py:26
  648.8 12.0 %collective-permute-done.91 = bf16[2,2,2,176,256]{4,3,2,1,0:T(8,128)(2,1)S(1)} collective-permute-done((bf16[2,2,2,176,256]{4,3,2,1,0:T(8,128)(2,1)S(1)}, bf16[2,2,2,176,256]{4,3,2,1,0:T(8,128)(2,1)S(1)}, u32[]{:S(2)}, u32[]{:S(2)}) %collective-permute-start.91) | collective-permute-done | bytes 720928 | tf_op jit(solution)/shard_map/ppermute | solution.py:26
  673.0 13.1 %collective-permute-done.68 = bf16[2,96,1920]{2,1,0:T(8,128)(2,1)} collective-permute-done((bf16[2,96,1920]{2,1,0:T(8,128)(2,1)}, bf16[2,96,1920]{2,1,0:T(8,128)(2,1)}, u32[]{:S(2)}, u32[]{:S(2)}) %collective-permute-start.68) | collective-permute-done | bytes 737312 | tf_op jit(solution)/shard_map/ppermute | solution.py:26
  690.4 18.8 %collective-permute-done.61 = f32[4160]{0:T(1024)S(1)} collective-permute-done((f32[4160]{0:T(1024)S(1)}, f32[4160]{0:T(1024)S(1)}, u32[]{:S(2)}, u32[]{:S(2)}) %collective-permute-start.61) | collective-permute-done | bytes 16672 | tf_op jit(solution)/shard_map/ppermute | solution.py:26
  711.6 19.4 %collective-permute-done.62 = f32[4160]{0:T(1024)S(1)} collective-permute-done((f32[4160]{0:T(1024)S(1)}, f32[4160]{0:T(1024)S(1)}, u32[]{:S(2)}, u32[]{:S(2)}) %collective-permute-start.62) | collective-permute-done | bytes 16672 | tf_op jit(solution)/shard_map/ppermute | solution.py:26
  757.6 21.2 %collective-permute-done.88 = bf16[2,176,1280]{2,1,0:T(8,128)(2,1)S(1)} collective-permute-done((bf16[2,176,1280]{2,1,0:T(8,128)(2,1)S(1)}, bf16[2,176,1280]{2,1,0:T(8,128)(2,1)S(1)}, u32[]{:S(2)}, u32[]{:S(2)}) %collective-permute-start.88) | collective-permute-done | bytes 901152 | tf_op jit(solution)/shard_map/ppermute | solution.py:26
  789.5 14.2 %collective-permute-start.90 = (bf16[176,1280]{1,0:T(8,128)(2,1)}, bf16[176,1280]{1,0:T(8,128)(2,1)}, u32[]{:S(2)}, u32[]{:S(2)}) collective-permute-start(bf16[176,1280]{1,0:T(8,128)(2,1)} %dynamic-slice_bitcast_fusion.6), channel_id=1, source_target_pairs={{0,4},{1,5},{2,6},{3,7},{4,0},{5,1},{6,2},{7,3},{8,12},{9,13},{10,... | collective-permute-start | bytes 1351688 | tf_op jit(solution)/shard_map/ppermute | solution.py:26
  838.0 14.1 %multiply_add_fusion = (f32[96,2,4096]{2,1,0:T(2,128)}, f32[96,2,4096]{2,1,0:T(2,128)}, f32[96,2,4096]{2,1,0:T(2,128)}) fusion(f32[96,2,4096]{2,1,0:T(2,128)} %param.44, f32[96,2,4096]{2,1,0:T(2,128)} %param.42, f32[96,2,4096]{2,1,0:T(2,128)} %reshape.378, f32[96,2,4096]{2,1,0:T(2,128)} %param.43), kind=kLoop, calls=%fused_computation.34 | loop fusion | flops 7077888 | bytes 22020096 | tf_op jit(solution)/shard_map/add | solution.py:580
  (622 shorter events, 389.5 us)
Async XLA Ops:
  7.2 810.3 %reduce-scatter.2.cloned.1.call-start = ((), (), s32[]{:S(2)}) async-start(), calls=%async_computation.1 | async-start | bytes 13369344 | tf_op jit(solution)/shard_map/reduce_scatter | solution.py:694
  14.3 40.4 %collective-permute-start.17 = (bf16[96,384]{1,0:T(8,128)(2,1)}, bf16[96,384]{1,0:T(8,128)(2,1)}, u32[]{:S(2)}, u32[]{:S(2)}) collective-permute-start(bf16[96,384]{1,0:T(8,128)(2,1)} %get-tuple-element.173), channel_id=1, source_target_pairs={{0,2},{1,3},{2,0},{3,1},{4,6},{5,7},{6,4},{7,5},{8,10},{9,11},{10,... | collective-permute-start | bytes 221192 | tf_op jit(solution)/shard_map/ppermute | solution.py:26
  96.7 50.3 %collective-permute-start.28 = (bf16[2,176,1280]{2,1,0:T(8,128)(2,1)S(1)}, bf16[2,176,1280]{2,1,0:T(8,128)(2,1)S(1)}, u32[]{:S(2)}, u32[]{:S(2)}) collective-permute-start(bf16[2,176,1280]{2,1,0:T(8,128)(2,1)S(1)} %collective-permute-done.27), channel_id=1, source_target_pairs={{4,0},{5,1},{6,2},{7,3},{8,12},{9,13},{10,14},{11,15},{20,16},{21,... | collective-permute-start | bytes 2703368 | tf_op jit(solution)/shard_map/ppermute | solution.py:26
  126.3 40.6 %collective-permute-start.6 = (bf16[512,1536]{1,0:T(8,128)(2,1)}, bf16[512,1536]{1,0:T(8,128)(2,1)}, u32[]{:S(2)}, u32[]{:S(2)}) collective-permute-start(bf16[512,1536]{1,0:T(8,128)(2,1)} %multiply_convert_fusion.1), channel_id=1, source_target_pairs={{0,16},{16,0},{1,17},{17,1},{2,18},{18,2},{3,19},{19,3},{4,20},{20... | collective-permute-start | bytes 4718600 | tf_op jit(solution)/shard_map/ppermute | solution.py:30
  166.9 36.0 %collective-permute-start.30 = (bf16[2,176,1280]{2,1,0:T(8,128)(2,1)S(1)}, bf16[2,176,1280]{2,1,0:T(8,128)(2,1)S(1)}, u32[]{:S(2)}, u32[]{:S(2)}) collective-permute-start(bf16[2,176,1280]{2,1,0:T(8,128)(2,1)S(1)} %copy-done.6), channel_id=1, source_target_pairs={{0,2},{1,3},{2,0},{3,1},{4,6},{5,7},{6,4},{7,5},{8,10},{9,11},{10,... | collective-permute-start | bytes 2703368 | tf_op jit(solution)/shard_map/ppermute | solution.py:26
  168.5 35.7 %collective-permute-start.24 = (bf16[2,176,1280]{2,1,0:T(8,128)(2,1)S(1)}, bf16[2,176,1280]{2,1,0:T(8,128)(2,1)S(1)}, u32[]{:S(2)}, u32[]{:S(2)}) collective-permute-start(bf16[2,176,1280]{2,1,0:T(8,128)(2,1)S(1)} %copy-done.1), channel_id=1, source_target_pairs={{0,1},{1,0},{2,3},{3,2},{4,5},{5,4},{6,7},{7,6},{8,9},{9,8},{10,11... | collective-permute-start | bytes 2703368 | tf_op jit(solution)/shard_map/ppermute | solution.py:26
  182.8 38.0 %collective-permute-start.31 = (bf16[2,176,1280]{2,1,0:T(8,128)(2,1)}, bf16[2,176,1280]{2,1,0:T(8,128)(2,1)S(1)}, u32[]{:S(2)}, u32[]{:S(2)}) collective-permute-start(bf16[2,176,1280]{2,1,0:T(8,128)(2,1)} %collective-permute-done.29.refs_5_), channel_id=1, source_target_pairs={{0,2},{1,3},{2,0},{3,1},{4,6},{5,7},{6,4},{7,5},{8,10},{9,11},{10,... | collective-permute-start | bytes 2703368 | tf_op jit(solution)/shard_map/ppermute | solution.py:26
  183.7 37.2 %collective-permute-start.26 = (bf16[2,176,1280]{2,1,0:T(8,128)(2,1)}, bf16[2,176,1280]{2,1,0:T(8,128)(2,1)S(1)}, u32[]{:S(2)}, u32[]{:S(2)}) collective-permute-start(bf16[2,176,1280]{2,1,0:T(8,128)(2,1)} %collective-permute-done.25.refs_2_), channel_id=1, source_target_pairs={{0,1},{1,0},{2,3},{3,2},{4,5},{5,4},{6,7},{7,6},{8,9},{9,8},{10,11... | collective-permute-start | bytes 2703368 | tf_op jit(solution)/shard_map/ppermute | solution.py:26
  197.6 92.1 %collective-permute-start.40 = (bf16[512,1536]{1,0:T(8,128)(2,1)}, bf16[512,1536]{1,0:T(8,128)(2,1)}, u32[]{:S(2)}, u32[]{:S(2)}) collective-permute-start(bf16[512,1536]{1,0:T(8,128)(2,1)} %bitcast.46), channel_id=1, source_target_pairs={{0,16},{16,0},{1,17},{17,1},{2,18},{18,2},{3,19},{19,3},{4,20},{20... | collective-permute-start | bytes 4718600 | tf_op jit(solution)/shard_map/ppermute | solution.py:30
  202.9 73.8 %collective-permute-start.46 = (bf16[2,96,3328]{2,1,0:T(8,128)(2,1)}, bf16[2,96,3328]{2,1,0:T(8,128)(2,1)}, u32[]{:S(2)}, u32[]{:S(2)}) collective-permute-start(bf16[2,96,3328]{2,1,0:T(8,128)(2,1)} %collective-permute-done.45), channel_id=1, source_target_pairs={{4,0},{5,1},{6,2},{7,3},{8,12},{9,13},{10,14},{11,15},{20,16},{21,... | collective-permute-start | bytes 3833864 | tf_op jit(solution)/shard_map/ppermute | solution.py:26
  204.2 87.5 %collective-permute-start.55 = (bf16[2,4,96,768]{3,2,1,0:T(8,128)(2,1)}, bf16[2,4,96,768]{3,2,1,0:T(8,128)(2,1)}, u32[]{:S(2)}, u32[]{:S(2)}) collective-permute-start(bf16[2,4,96,768]{3,2,1,0:T(8,128)(2,1)} %collective-permute-done.54), channel_id=1, source_target_pairs={{4,0},{5,1},{6,2},{7,3},{8,12},{9,13},{10,14},{11,15},{20,16},{21,... | collective-permute-start | bytes 3538952 | tf_op jit(solution)/shard_map/ppermute | solution.py:26
  232.3 47.3 %collective-permute-start.38 = (bf16[16,48,1536]{2,1,0:T(8,128)(2,1)}, bf16[16,48,1536]{2,1,0:T(8,128)(2,1)}, u32[]{:S(2)}, u32[]{:S(2)}) collective-permute-start(bf16[16,48,1536]{2,1,0:T(8,128)(2,1)} %get-tuple-element.141), channel_id=1, source_target_pairs={{0,16},{16,0},{1,17},{17,1},{2,18},{18,2},{3,19},{19,3},{4,20},{20... | collective-permute-start | bytes 7077896 | tf_op jit(solution)/shard_map/ppermute | solution.py:30
  289.7 84.6 %collective-permute-start.39 = (bf16[512,1536]{1,0:T(8,128)(2,1)S(1)}, bf16[512,1536]{1,0:T(8,128)(2,1)S(1)}, u32[]{:S(2)}, u32[]{:S(2)}) collective-permute-start(bf16[512,1536]{1,0:T(8,128)(2,1)S(1)} %multiply_convert_fusion), channel_id=1, source_target_pairs={{0,16},{16,0},{1,17},{17,1},{2,18},{18,2},{3,19},{19,3},{4,20},{20... | collective-permute-start | bytes 4718600 | tf_op jit(solution)/shard_map/ppermute | solution.py:30
  290.4 47.8 %collective-permute-start.42 = (bf16[2,96,3328]{2,1,0:T(8,128)(2,1)S(1)}, bf16[2,96,3328]{2,1,0:T(8,128)(2,1)S(1)}, u32[]{:S(2)}, u32[]{:S(2)}) collective-permute-start(bf16[2,96,3328]{2,1,0:T(8,128)(2,1)S(1)} %copy-done.5), channel_id=1, source_target_pairs={{0,1},{1,0},{2,3},{3,2},{4,5},{5,4},{6,7},{7,6},{8,9},{9,8},{10,11... | collective-permute-start | bytes 3833864 | tf_op jit(solution)/shard_map/ppermute | solution.py:26
  291.7 46.5 %collective-permute-start.48 = (bf16[2,96,3328]{2,1,0:T(8,128)(2,1)S(1)}, bf16[2,96,3328]{2,1,0:T(8,128)(2,1)S(1)}, u32[]{:S(2)}, u32[]{:S(2)}) collective-permute-start(bf16[2,96,3328]{2,1,0:T(8,128)(2,1)S(1)} %copy-done.25), channel_id=1, source_target_pairs={{0,2},{1,3},{2,0},{3,1},{4,6},{5,7},{6,4},{7,5},{8,10},{9,11},{10,... | collective-permute-start | bytes 3833864 | tf_op jit(solution)/shard_map/ppermute | solution.py:26
  305.2 59.4 %collective-permute-start.44 = (bf16[2,96,3328]{2,1,0:T(8,128)(2,1)}, bf16[2,96,3328]{2,1,0:T(8,128)(2,1)S(1)}, u32[]{:S(2)}, u32[]{:S(2)}) collective-permute-start(bf16[2,96,3328]{2,1,0:T(8,128)(2,1)} %collective-permute-done.43.refs_2_), channel_id=1, source_target_pairs={{0,1},{1,0},{2,3},{3,2},{4,5},{5,4},{6,7},{7,6},{8,9},{9,8},{10,11... | collective-permute-start | bytes 3833864 | tf_op jit(solution)/shard_map/ppermute | solution.py:26
  310.8 53.8 %collective-permute-start.49 = (bf16[2,96,3328]{2,1,0:T(8,128)(2,1)S(1)}, bf16[2,96,3328]{2,1,0:T(8,128)(2,1)}, u32[]{:S(2)}, u32[]{:S(2)}) collective-permute-start(bf16[2,96,3328]{2,1,0:T(8,128)(2,1)S(1)} %collective-permute-done.47.refs_5_), channel_id=1, source_target_pairs={{0,2},{1,3},{2,0},{3,1},{4,6},{5,7},{6,4},{7,5},{8,10},{9,11},{10,... | collective-permute-start | bytes 3833864 | tf_op jit(solution)/shard_map/ppermute | solution.py:26
  559.4 61.8 %collective-permute-start.81 = (bf16[16,48,1536]{2,1,0:T(8,128)(2,1)}, bf16[16,48,1536]{2,1,0:T(8,128)(2,1)}, u32[]{:S(2)}, u32[]{:S(2)}) collective-permute-start(bf16[16,48,1536]{2,1,0:T(8,128)(2,1)} %dynamic-slice_bitcast_fusion), channel_id=1, source_target_pairs={{0,16},{16,0},{1,17},{17,1},{2,18},{18,2},{3,19},{19,3},{4,20},{20... | collective-permute-start | bytes 7077896 | tf_op jit(solution)/shard_map/ppermute | solution.py:30
  595.1 72.3 %collective-permute-start.59 = (f32[512,1536]{1,0:T(8,128)}, f32[512,1536]{1,0:T(8,128)}, u32[]{:S(2)}, u32[]{:S(2)}) collective-permute-start(f32[512,1536]{1,0:T(8,128)} %slice.189), channel_id=1, source_target_pairs={{0,16},{16,0},{1,17},{17,1},{2,18},{18,2},{3,19},{19,3},{4,20},{20... | collective-permute-start | bytes 9437192 | tf_op jit(solution)/shard_map/ppermute | solution.py:30
  662.9 84.7 %collective-permute-start.85 = (bf16[2,176,1280]{2,1,0:T(8,128)(2,1)}, bf16[2,176,1280]{2,1,0:T(8,128)(2,1)}, u32[]{:S(2)}, u32[]{:S(2)}) collective-permute-start(bf16[2,176,1280]{2,1,0:T(8,128)(2,1)} %get-tuple-element.135), channel_id=1, source_target_pairs={{0,2},{1,3},{2,0},{3,1},{4,6},{5,7},{6,4},{7,5},{8,10},{9,11},{10,... | collective-permute-start | bytes 2703368 | tf_op jit(solution)/shard_map/ppermute | solution.py:26
  667.3 119.5 %collective-permute-start.82 = (bf16[2,176,1280]{2,1,0:T(8,128)(2,1)}, bf16[2,176,1280]{2,1,0:T(8,128)(2,1)}, u32[]{:S(2)}, u32[]{:S(2)}) collective-permute-start(bf16[2,176,1280]{2,1,0:T(8,128)(2,1)} %get-tuple-element.134), channel_id=1, source_target_pairs={{0,1},{1,0},{2,3},{3,2},{4,5},{5,4},{6,7},{7,6},{8,9},{9,8},{10,11... | collective-permute-start | bytes 2703368 | tf_op jit(solution)/shard_map/ppermute | solution.py:26
  672.2 38.6 %collective-permute-start.92 = (bf16[2,2,2,176,256]{4,3,2,1,0:T(8,128)(2,1)}, bf16[2,2,2,176,256]{4,3,2,1,0:T(8,128)(2,1)S(1)}, u32[]{:S(2)}, u32[]{:S(2)}) collective-permute-start(bf16[2,2,2,176,256]{4,3,2,1,0:T(8,128)(2,1)} %add_convert_fusion.5), channel_id=1, source_target_pairs={{4,8},{5,9},{6,10},{7,11},{8,4},{9,5},{10,6},{11,7},{20,24},{21,25... | collective-permute-start | bytes 2162696 | tf_op jit(solution)/shard_map/ppermute | solution.py:26
  686.1 61.6 %collective-permute-start.87 = (bf16[2,176,1280]{2,1,0:T(8,128)(2,1)}, bf16[2,176,1280]{2,1,0:T(8,128)(2,1)}, u32[]{:S(2)}, u32[]{:S(2)}) collective-permute-start(bf16[2,176,1280]{2,1,0:T(8,128)(2,1)} %get-tuple-element.139), channel_id=1, source_target_pairs={{0,1},{1,0},{2,3},{3,2},{4,5},{5,4},{6,7},{7,6},{8,9},{9,8},{10,11... | collective-permute-start | bytes 2703368 | tf_op jit(solution)/shard_map/ppermute | solution.py:26
  709.2 77.5 %collective-permute-start.84 = (bf16[2,176,1280]{2,1,0:T(8,128)(2,1)}, bf16[2,176,1280]{2,1,0:T(8,128)(2,1)}, u32[]{:S(2)}, u32[]{:S(2)}) collective-permute-start(bf16[2,176,1280]{2,1,0:T(8,128)(2,1)} %get-tuple-element.138), channel_id=1, source_target_pairs={{0,2},{1,3},{2,0},{3,1},{4,6},{5,7},{6,4},{7,5},{8,10},{9,11},{10,... | collective-permute-start | bytes 2703368 | tf_op jit(solution)/shard_map/ppermute | solution.py:26
  (191 other events, 2691.2 us)
Sparse Core Ops, SparseCore 0:
  456.6 234.6 reduce-scatter.1

commit v2 on v1

--- a/solution.py
+++ b/solution.py
@@ -45,11 +45,6 @@
 Y_PAIR = [(i, i ^ 2) for i in range(BLOCK)]
 
 
-def cut_columns(columns):
-    tiles = columns // 128
-    return (tiles - tiles // 5) * 128
-
-
 def after(values, *needed):
     def nothing(*refs):
         del refs
@@ -66,70 +61,93 @@
 def line_gather(piece):
     z = lax.axis_index("wide") // 4
     odd = (z % 2) == 1
-    other = permute(piece, Z_PAIR)
-    near = jnp.stack([jnp.where(odd, other, piece), jnp.where(odd, piece, other)])
-    crossed = permute(near, Z_MID)
-    handed = permute(crossed, Z_OUT)
-    far = jnp.where((z == 1) | (z == 2), crossed, handed)
-    return near, far
-
-
-def gather_begin(piece, *needed):
-    if lax.axis_size("wide") != BLOCK:
-        return (piece,)
-    if needed:
-        piece = after(piece, *needed)
-    cut = cut_columns(piece.shape[1])
-    lines = [line_gather(piece[:, :cut])]
-    own = piece[:, cut:]
-    by_x = permute(own, X_PAIR)
-    by_y = permute(own, Y_PAIR)
-    plane = jnp.stack([own, by_x, by_y, permute(by_x, Y_PAIR)])
-    lines.append(line_gather(plane))
-    return lines
-
-
-def gather_end(lines, *needed):
+    up = [permute(piece, z_pairs([(0, 1), (1, 2), (2, 3)]))]
+    down = [permute(piece, z_pairs([(1, 0), (2, 1), (3, 2)]))]
+    up.append(permute(up[0], z_pairs([(1, 2), (2, 3)])))
+    down.append(permute(down[0], z_pairs([(1, 0), (2, 1)])))
+    up.append(permute(up[1], z_pairs([(2, 3)])))
+    down.append(permute(down[1], z_pairs([(1, 0)])))
+    near = jnp.stack([jnp.where(odd, up[0], piece), jnp.where(odd, piece, down[0])])
+
+    def by_place(*choices):
+        return jnp.where(
+            z < 2,
+            jnp.where(z == 0, choices[0], choices[1]),
+            jnp.where(z == 2, choices[2], choices[3]),
+        )
+
+    def far(*needed):
+        up_last, down_last = after(up[2], *needed), after(down[2], *needed)
+        return jnp.stack(
+            [
+                by_place(down[1], down[0], up[1], up_last),
+                by_place(down_last, down[1], up[0], up[1]),
+            ]
+        )
+
+    return near, far, up[1], down[1]
+
+
+def line_and_plane(piece):
+    z = lax.axis_index("wide") // 4
+    odd = (z % 2) == 1
+
+    def across(values, x_first):
+        return (values, permute(values, X_PAIR), permute(values, Y_PAIR), x_first)
+
+    own = across(piece, False)
+    up = permute(piece, z_pairs([(0, 1), (1, 2), (2, 3)]))
+    down = permute(piece, z_pairs([(1, 0), (2, 1), (3, 2)]))
+    beside = across(jnp.where(odd, up, down), True)
+    up_two = permute(after(up, *own[1:3]), z_pairs([(1, 2), (2, 3)]))
+    down_two = permute(after(down, *own[1:3]), z_pairs([(1, 0), (2, 1)]))
+    up_three = permute(after(up_two, *beside[1:3]), z_pairs([(2, 3)]))
+    down_three = permute(after(down_two, *beside[1:3]), z_pairs([(1, 0)]))
+
+    def by_place(*choices):
+        return jnp.where(
+            z < 2,
+            jnp.where(z == 0, choices[0], choices[1]),
+            jnp.where(z == 2, choices[2], choices[3]),
+        )
+
+    far0 = across(by_place(down_two, down, up_two, up_three), False)
+    far1 = across(by_place(down_three, down_two, up, up_two), True)
+    return [("own", own), ("beside", beside), ("far0", far0), ("far1", far1)]
+
+
+def gather(piece, lines, widths, needed=()):
     count = lax.axis_size("wide")
+    rows = piece.shape[0]
+    starts = [sum(widths[:i]) for i in range(len(widths))]
     if count != BLOCK:
-        return lax.all_gather(lines[0], "wide", axis=0, tiled=True)
-    (near, far), rest = lines
-    rows, cut = near.shape[1:]
-    columns = cut + rest[0].shape[-1]
-    if needed:
-        near, far = after(near, *needed), after(far, *needed)
+        full = lax.all_gather(piece, "wide", axis=0, tiled=True)
+        return [full[:, low : low + width] for low, width in zip(starts, widths)]
     me = lax.axis_index("wide")
     index = jnp.stack([me // 4, me % 4]).astype(jnp.int32)
     arrays = []
     places = []
-
-    def place(array, pick, half, lane, low, high):
-        position = [n for n, known in enumerate(arrays) if known is array]
-        if not position:
+    for place, across in lines:
+        kept, by_x, by_y, x_first = across
+        both = permute(by_x, Y_PAIR) if x_first else permute(by_y, X_PAIR)
+        for lane, array in enumerate((kept, by_x, by_y, both)):
             arrays.append(array)
-            position = [len(arrays) - 1]
-        places.append((position[0], pick, half, lane, low, high))
-
-    for half, block in enumerate((near, far)):
-        by_x = permute(block, X_PAIR)
-        by_y = permute(block, Y_PAIR)
-        both = permute(by_y, X_PAIR) if half == 0 else permute(by_x, Y_PAIR)
-        for lane, array in enumerate((block, by_x, by_y, both)):
-            place(array, None, half, lane, 0, cut)
-    for half, block in enumerate(rest):
-        for lane in range(4):
-            place(block, lane, half, lane, cut, columns)
+            places.append((place, lane))
 
     def assemble(index_ref, *refs):
-        out_ref, sems = refs[len(arrays)], refs[len(arrays) + 1]
-        pair, lane_me = index_ref[0] // 2, index_ref[1]
+        out_refs, sems = refs[-1 - len(widths) : -1], refs[-1]
+        z = index_ref[0]
+        z_places = {"own": z, "beside": z ^ 1, "far0": 2 - (z // 2) * 2, "far1": 3 - (z // 2) * 2}
         copies = []
-        for n, (position, pick, half, lane, low, high) in enumerate(places):
-            source = refs[position] if pick is None else refs[position].at[:, pick]
-            target = out_ref.at[
-                pl.ds(2 * (pair ^ half), 2), lane_me ^ lane, :, pl.ds(low, high - low)
-            ]
-            copies.append(pltpu.make_async_copy(source, target, sems.at[n]))
+        for n, (place, lane) in enumerate(places):
+            for out_ref, low, width in zip(out_refs, starts, widths):
+                copies.append(
+                    pltpu.make_async_copy(
+                        refs[n].at[:, pl.ds(low, width)],
+                        out_ref.at[z_places[place], index_ref[1] ^ lane],
+                        sems.at[len(copies)],
+                    )
+                )
         for copy in copies:
             copy.start()
         for copy in copies:
@@ -137,14 +155,14 @@
 
     full = pl.pallas_call(
         assemble,
-        out_shape=jax.ShapeDtypeStruct((4, 4, rows, columns), near.dtype),
+        out_shape=[jax.ShapeDtypeStruct((4, 4, rows, width), piece.dtype) for width in widths],
         in_specs=[pl.BlockSpec(memory_space=pltpu.SMEM)]
-        + [pl.BlockSpec(memory_space=pl.ANY)] * len(arrays),
-        out_specs=pl.BlockSpec(memory_space=pltpu.VMEM),
-        scratch_shapes=[pltpu.SemaphoreType.DMA((len(places),))],
+        + [pl.BlockSpec(memory_space=pl.ANY)] * (len(arrays) + len(needed)),
+        out_specs=[pl.BlockSpec(memory_space=pltpu.VMEM)] * len(widths),
+        scratch_shapes=[pltpu.SemaphoreType.DMA((len(arrays) * len(widths),))],
         compiler_params=pltpu.CompilerParams(vmem_limit_bytes=48 << 20),
-    )(index, *arrays)
-    return full.reshape(count * rows, columns)
+    )(index, *arrays, *needed)
+    return [part.reshape(count * rows, -1) for part in full]
 
 
 def fold(*terms):
@@ -157,49 +175,195 @@
     return fold(keep, permute(give, pairs))
 
 
-def line_sum(near, far, odd):
-    far = fold(far, permute(far, Z_IN))
-    near = fold(near, permute(far, Z_MID))
-    return trade(near, odd, Z_PAIR)
-
-
-def scatter_sum(partial):
+def line_begin(far):
+    z = lax.axis_index("wide") // 4
+    farthest = jnp.where(z < 2, far[1], far[0])
+    up = permute(farthest, z_pairs([(0, 1)]))
+    down = permute(farthest, z_pairs([(3, 2)]))
+    return up, down
+
+
+def line_middle(far, up, down):
+    z = lax.axis_index("wide") // 4
+    up = permute(fold(jnp.where(z == 0, far[0], far[1]), up), z_pairs([(0, 1), (1, 2)]))
+    down = permute(fold(jnp.where(z == 3, far[1], far[0]), down), z_pairs([(3, 2), (2, 1)]))
+    return up, down
+
+
+def line_end(near, far, up, down):
+    z = lax.axis_index("wide") // 4
+    up = permute(
+        fold(jnp.where(z == 1, far[0], near[1]), up), z_pairs([(0, 1), (1, 2), (2, 3)])
+    )
+    down = permute(
+        fold(jnp.where(z == 2, far[1], near[0]), down), z_pairs([(3, 2), (2, 1), (1, 0)])
+    )
+    return fold(jnp.where(z % 2 == 1, near[1], near[0]), up, down)
+
+
+def scatter_begin(*partials):
     count = lax.axis_size("wide")
     if count != BLOCK:
-        return lax.psum_scatter(partial, "wide", scatter_dimension=0, tiled=True)
+        return (jnp.concatenate(partials, axis=1),), None
     me = lax.axis_index("wide")
-    pair, odd, y, x = me // 8, (me // 4) % 2, (me // 2) % 2, me % 2
-    columns = partial.shape[1]
-    rows = partial.shape[0] // count
-    cut = cut_columns(columns)
-    blocks = partial.reshape(2, 2, 2, 2, rows, columns)
+    pair, y, x = me // 8, (me // 2) % 2, me % 2
 
     def block(half, y_at, x_at):
+        found = []
+        for partial in partials:
+            rows, columns = partial.shape[0] // count, partial.shape[1]
+            part = lax.dynamic_slice(
+                partial.reshape(2, 2, 2, 2, rows, columns),
+                (half, 0, y_at, x_at, 0, 0),
+                (1, 2, 1, 1, rows, columns),
+            )
+            found.append(part.reshape(2, rows, columns))
+        return jnp.concatenate(found, axis=2)
+
+    out = (
+        block(1 - pair, 1 - y, 1 - x),
+        block(pair, 1 - y, 1 - x),
+        block(1 - pair, 1 - y, x),
+        block(pair, y, 1 - x),
+    )
+    return out, block
+
+
+def scatter_first(out, block):
+    if block is None:
+        return ()
+    return permute(out[0], Y_PAIR), permute(out[1], X_PAIR)
+
+
+def scatter_plane(out, block, arrivals, needed):
+    if block is None:
+        return out
+    me = lax.axis_index("wide")
+    pair, y, x = me // 8, (me // 2) % 2, me % 2
+    by_y, by_x = permute(out[2], Y_PAIR), after(permute(out[3], X_PAIR), *needed)
+    far = fold(block(1 - pair, y, 1 - x), arrivals[0])
+    near = fold(block(pair, 1 - y, x), arrivals[1])
+    far = fold(block(1 - pair, y, x), by_y, permute(far, X_PAIR))
+    near = fold(block(pair, y, x), by_x, permute(near, Y_PAIR))
+    return near, far
+
+
+def scatter_line(sums, *needed):
+    if lax.axis_size("wide") != BLOCK:
+        return lax.psum_scatter(sums[0], "wide", scatter_dimension=0, tiled=True)
+    near, far = sums
+    steps = line_middle(far, *line_begin(far))
+    return line_end(after(near, *needed), far, *steps)
+
+
+def pair_groups():
+    count = lax.axis_size("wide")
+    return [[i for i in range(count) if i % 2 == x] for x in range(2)]
+
+
+def x_pairs():
+    return [(i, i ^ 1) for i in range(lax.axis_size("wide"))]
+
+
+def both_by(bit, mine, other):
+    return jnp.where(bit == 0, jnp.stack([mine, other]), jnp.stack([other, mine]))
+
+
+def ff_pair(mine, theirs):
+    return both_by(lax.axis_index("wide") % 2, mine, permute(theirs, x_pairs()))
+
+
+def ff_cross(lines):
+    return permute(lines, Y_PAIR)
+
+
+def ff_end(arrays, rows, units):
+    count = lax.axis_size("wide")
+    tall, columns = arrays[0].shape[-2:]
+    cols = (rows * count) // columns
+    blocks = (tall - cols * units) // rows
+    gateup_shape = (blocks, count * rows, columns)
+    down_shape = (count * units, cols * columns)
+    if count != BLOCK:
+        full = lax.all_gather(arrays[0], "wide", axis_index_groups=pair_groups())
+        full = full.reshape(count, tall, columns)
+        gateup = full[:, : blocks * rows].reshape(count, blocks, rows, columns)
+        down = full[:, blocks * rows :].reshape(count, cols, units, columns)
+        return (
+            gateup.transpose(1, 0, 2, 3).reshape(gateup_shape),
+            down.transpose(0, 2, 1, 3).reshape(down_shape),
+        )
+    me = lax.axis_index("wide")
+    index = jnp.stack([me // 8, (me // 2) % 2]).astype(jnp.int32)
+
+    def assemble(index_ref, *refs):
+        gateup_ref, down_ref, sems = refs[len(arrays) :]
+        copies = []
+
+        def copy(source, target):
+            copies.append(pltpu.make_async_copy(source, target, sems.at[len(copies)]))
+
+        for n in range(len(arrays)):
+            half, lane = n // 2, n % 2
+            for z in range(2):
+                for x in range(2):
+                    z_at = 2 * (index_ref[0] ^ half) + z
+                    at = z_at * 4 + (index_ref[1] ^ lane) * 2 + x
+                    source = refs[n].at[z, x]
+                    for j in range(blocks):
+                        target = gateup_ref.at[j, pl.ds(pl.multiple_of(at * rows, 16), rows)]
+                        copy(source.at[pl.ds(j * rows, rows)], target)
+                    for i in range(cols):
+                        target = down_ref.at[
+                            pl.ds(pl.multiple_of(at * units, 16), units),
+                            pl.ds(i * columns, columns),
+                        ]
+                        copy(source.at[pl.ds(blocks * rows + i * units, units)], target)
+        for started in copies:
+            started.start()
+        for started in copies:
+            started.wait()
+
+    return pl.pallas_call(
+        assemble,
+        out_shape=(
+            jax.ShapeDtypeStruct(gateup_shape, BF16),
+            jax.ShapeDtypeStruct(down_shape, BF16),
+        ),
+        in_specs=[pl.BlockSpec(memory_space=pltpu.SMEM)]
+        + [pl.BlockSpec(memory_space=pl.ANY)] * len(arrays),
+        out_specs=(pl.BlockSpec(memory_space=pltpu.VMEM),) * 2,
+        scratch_shapes=[pltpu.SemaphoreType.DMA((len(arrays) * 4 * (blocks + cols),))],
+        compiler_params=pltpu.CompilerParams(vmem_limit_bytes=48 << 20),
+    )(index, *arrays)
+
+
+def ff_part(gateup_grad, down_grad, half, y):
+    parts = []
+    for grad in (gateup_grad, down_grad):
+        blocks = grad.reshape((2, 2, 2, 2) + grad.shape[1:])
         found = lax.dynamic_slice(
-            blocks, (half, 0, y_at, x_at, 0, 0), (1, 2, 1, 1, rows, cut)
+            blocks, (half, 0, y, 0, 0, 0), (1, 2, 1, 2) + grad.shape[1:]
         )
-        return found.reshape(2, rows, cut)
-
-    far = fold(block(1 - pair, y, 1 - x), permute(block(1 - pair, 1 - y, 1 - x), Y_PAIR))
-    far = fold(
-        block(1 - pair, y, x),
-        permute(block(1 - pair, 1 - y, x), Y_PAIR),
-        permute(far, X_PAIR),
-    )
-    near = fold(block(pair, 1 - y, x), permute(block(pair, 1 - y, 1 - x), X_PAIR))
-    near = fold(
-        block(pair, y, x),
-        permute(block(pair, y, 1 - x), X_PAIR),
-        permute(near, Y_PAIR),
-    )
-    done = line_sum(near, far, odd)
-    if columns > cut:
-        rest = blocks[..., cut:]
-        near = lax.dynamic_index_in_dim(rest, pair, 0, keepdims=False)
-        far = lax.dynamic_index_in_dim(rest, 1 - pair, 0, keepdims=False)
-        last = trade(trade(line_sum(near, far, odd), y, Y_PAIR), x, X_PAIR)
-        done = jnp.concatenate([done, last], axis=1)
-    return done
+        parts.append(found.reshape((2, 2) + grad.shape[1:]))
+    return jnp.concatenate(parts, axis=2)
+
+
+def ff_scatter_whole(gateup_grad, down_grad):
+    packed = jnp.concatenate([gateup_grad, down_grad], axis=1)
+    return lax.psum_scatter(
+        packed.reshape((packed.shape[0] // 2, 2) + packed.shape[1:]),
+        "wide",
+        scatter_dimension=0,
+        axis_index_groups=pair_groups(),
+    )
+
+
+def ff_last(total):
+    x = lax.axis_index("wide") % 2
+    keep = lax.dynamic_index_in_dim(total, x, 0, keepdims=False)
+    give = lax.dynamic_index_in_dim(total, 1 - x, 0, keepdims=False)
+    return keep, permute(give, x_pairs())
 
 
 def gather_small(values):
@@ -213,19 +377,22 @@
 
     row = both(values, permute(values, X_PAIR), x)
     plane = both(row, permute(row, Y_PAIR), y)
-    near, far = line_gather(plane)
-    return both(near, far, pair).reshape((BLOCK,) + values.shape)
+    near, far = line_gather(plane)[:2]
+    return both(near, far(), pair).reshape((BLOCK,) + values.shape)
 
 
 def sum_small(values):
     values = values + swap_cores(values)
     if lax.axis_size("wide") != BLOCK:
         return lax.psum(values, "wide")
-    z = lax.axis_index("wide") // 4
-    for pairs in (X_PAIR, Y_PAIR, Z_PAIR):
-        values = values + permute(values, pairs)
-    total = values + permute(values, Z_MID)
-    return jnp.where((z == 1) | (z == 2), total, permute(total, Z_OUT))
+    corner = [(i, i ^ 3) for i in range(BLOCK)]
+    values = (values + permute(values, X_PAIR)) + (
+        permute(values, Y_PAIR) + permute(values, corner)
+    )
+    one, two, three = (
+        permute(values, z_pairs([(z, (z + hop) % 4) for z in range(4)])) for hop in (1, 2, 3)
+    )
+    return (values + two) + (one + three)
 
 
 def allowed_mask(length, size):
@@ -504,56 +671,216 @@
 HIDDEN_BLOCK = 256
 
 
-def feed_forward(second, second_turned, d_final, gateup, down):
-    tokens, width = second.shape
-    hidden_count = down.shape[0]
+def feed_forward(seconds, d_finals, gateup, down, count):
+    part, width = seconds[0].shape
+    tokens = 4 * part
+    blocks = gateup.shape[0]
     block = HIDDEN_BLOCK
-    part = tokens // 2
-
-    def kernel(x_ref, xt_ref, d_ref, gu_ref, down_ref, hidden_ref, dgu_ref, grad_ref):
-        for m in range(0, tokens, part):
-            rows = slice(m, m + part)
-            gate_up = dot_nn(x_ref[rows, :], gu_ref[...])
+    rows, units = width // count, down.shape[0] // count
+    cols = width // (2 * block)
+    packed = count == BLOCK
+
+    def kernel(*refs):
+        x_refs, d_refs, (gu_ref, down_ref) = refs[:4], refs[4:8], refs[8:10]
+        hidden_ref, dgu_ref, grad_ref, down_grad_ref, turned = refs[10:]
+
+        @pl.when(pl.program_id(0) == 0)
+        def _():
+            for m in range(0, tokens, 256):
+                source = x_refs[m // part][m % part : m % part + 256, :]
+                turned[:, m : m + 256] = source.T
+
+        down_grad = None
+        for n in range(4):
+            at = slice(n * part, (n + 1) * part)
+            gate_up = dot_nn(x_refs[n][...], gu_ref[0])
             gate, up = gate_up[:, :block], gate_up[:, block:]
             sig = jax.nn.sigmoid(gate)
             silu = gate * sig
-            hidden_ref[rows, :] = (silu * up).astype(BF16)
-            d_hidden = dot_nt(d_ref[rows, :], down_ref[...])
+            hidden = (silu * up).astype(BF16)
+            hidden_ref[at, :] = hidden
+            d_hidden = dot_nt(d_refs[n][...], down_ref[...])
             d_gate = d_hidden * up * sig * (1.0 + gate * (1.0 - sig))
-            dgu_ref[rows, :block] = d_gate.astype(BF16)
-            dgu_ref[rows, block:] = (d_hidden * silu).astype(BF16)
-        grad_ref[...] = dot_nn(xt_ref[...], dgu_ref[...]).astype(BF16)
+            dgu_ref[at, :block] = d_gate.astype(BF16)
+            dgu_ref[at, block:] = (d_hidden * silu).astype(BF16)
+            term = dot_tn(hidden, d_refs[n][...])
+            down_grad = term if down_grad is None else down_grad + term
+        grad = dot_nn(turned[...], dgu_ref[...]).astype(BF16)
+        down_grad = down_grad.astype(BF16)
+        if packed:
+            grad_ref[...] = grad.reshape(count, rows, 2 * block)
+            for i in range(cols):
+                columns = down_grad[:, i * 2 * block : (i + 1) * 2 * block]
+                down_grad_ref[:, i * units : (i + 1) * units, :] = columns.reshape(
+                    block // units, units, 2 * block
+                )
+        else:
+            grad_ref[0] = grad
+            down_grad_ref[...] = down_grad
 
     def whole(shape):
         return pl.BlockSpec(shape, lambda j: (0, 0), pipeline_mode=pl.Buffered(1))
 
-    return pl.pallas_call(
+    gateup_part = pl.BlockSpec((1, width, 2 * block), lambda j: (j, 0, 0))
+    down_part = pl.BlockSpec((block, width), lambda j: (j, 0))
+    if packed:
+        grad_shapes = ((count, blocks * rows, 2 * block), (count, cols * units, 2 * block))
+        grad_specs = (
+            pl.BlockSpec((count, rows, 2 * block), lambda j: (0, j, 0)),
+            pl.BlockSpec((block // units, cols * units, 2 * block), lambda j: (j, 0, 0)),
+        )
+    else:
+        grad_shapes = (gateup.shape, down.shape)
+        grad_specs = (gateup_part, down_part)
+    hidden, d_gate_up, gateup_grad, down_grad = pl.pallas_call(
         kernel,
-        grid=(hidden_count // block,),
+        grid=(blocks,),
         out_shape=(
-            jax.ShapeDtypeStruct((tokens, hidden_count), BF16),
-            jax.ShapeDtypeStruct((tokens, 2 * hidden_count), BF16),
-            jax.ShapeDtypeStruct((width, 2 * hidden_count), BF16),
-        ),
-        in_specs=[
-            whole((tokens, width)),
-            whole((width, tokens)),
-            whole((tokens, width)),
-            pl.BlockSpec((width, 2 * block), lambda j: (0, j)),
-            pl.BlockSpec((block, width), lambda j: (j, 0)),
-        ],
+            jax.ShapeDtypeStruct((tokens, blocks * block), BF16),
+            jax.ShapeDtypeStruct((tokens, 2 * blocks * block), BF16),
+        )
+        + tuple(jax.ShapeDtypeStruct(shape, BF16) for shape in grad_shapes),
+        in_specs=[whole((part, width))] * 8 + [gateup_part, down_part],
         out_specs=(
             pl.BlockSpec((tokens, block), lambda j: (0, j)),
             pl.BlockSpec((tokens, 2 * block), lambda j: (0, j)),
-            pl.BlockSpec((width, 2 * block), lambda j: (0, j)),
+        )
+        + grad_specs,
+        scratch_shapes=[pltpu.VMEM((width, tokens), BF16)],
+        compiler_params=pltpu.CompilerParams(vmem_limit_bytes=56 << 20),
+        cost_estimate=pl.CostEstimate(
+            flops=12 * tokens * width * blocks * block,
+            bytes_accessed=48 << 20,
+            transcendentals=tokens * blocks * block,
         ),
-        compiler_params=pltpu.CompilerParams(vmem_limit_bytes=52 << 20),
+    )(*seconds, *d_finals, gateup, down)
+    if not packed:
+        gateup_grad = gateup_grad.reshape(blocks, count, rows, 2 * block)
+        gateup_grad = gateup_grad.transpose(1, 0, 2, 3).reshape(count, -1, 2 * block)
+        down_grad = down_grad.reshape(count, units, cols, 2 * block)
+        down_grad = down_grad.transpose(0, 2, 1, 3).reshape(count, -1, 2 * block)
+    return hidden, d_gate_up, gateup_grad, down_grad
+
+
+def back_through_gateup(d_gate_up, gateup, first, count, kind, needed=()):
+    blocks, width, columns = gateup.shape
+    part = 256
+
+    def kernel(d_ref, gu_ref, *refs):
+        total = dot_nt(d_ref[:, :columns], gu_ref[0])
+        for j in range(1, blocks):
+            total = total + dot_nt(d_ref[:, j * columns : (j + 1) * columns], gu_ref[j])
+        refs[-1][...] = total.astype(kind)
+
+    return pl.pallas_call(
+        kernel,
+        grid=(count // part,),
+        out_shape=jax.ShapeDtypeStruct((count, width), kind),
+        in_specs=[
+            pl.BlockSpec((part, blocks * columns), lambda m: (first // part + m, 0)),
+            pl.BlockSpec(gateup.shape, lambda m: (0, 0, 0), pipeline_mode=pl.Buffered(1)),
+        ]
+        + [pl.BlockSpec(memory_space=pl.ANY)] * len(needed),
+        out_specs=pl.BlockSpec((part, width), lambda m: (m, 0)),
+        compiler_params=pltpu.CompilerParams(vmem_limit_bytes=48 << 20),
         cost_estimate=pl.CostEstimate(
-            flops=10 * tokens * width * hidden_count,
-            bytes_accessed=48 << 20,
-            transcendentals=tokens * hidden_count,
+            flops=2 * count * width * blocks * columns,
+            bytes_accessed=16 << 20,
+            transcendentals=0,
         ),
-    )(second, second_turned, d_final, gateup, down)
+    )(d_gate_up, gateup, *needed)
+
+
+def quarter_columns(wide, hidden_all):
+    units = hidden_all // (4 * wide)
+    return units, HIDDEN_BLOCK // units
+
+
+def gateup_cast(weight, quarter):
+    rows, _, hidden_all = weight.shape
+    wide = lax.axis_size("wide")
+    units, each = quarter_columns(wide, hidden_all)
+    block = HIDDEN_BLOCK
+    blocks = hidden_all // (4 * block)
+    if wide != BLOCK:
+        split = weight.astype(BF16).reshape(rows, 2, blocks, each, 4, units)
+        split = split.transpose(4, 2, 0, 1, 3, 5).reshape(4, blocks * rows, 2 * block)
+        return split[quarter], split[quarter ^ 2]
+
+    def kernel(quarter_ref, in_ref, mine_ref, theirs_ref):
+        found = []
+        for t in range(4):
+            parts = []
+            for k in range(2):
+                for w in range(each):
+                    low = (4 * w + t) * units
+                    parts.append(in_ref[:, k, low : low + units])
+            found.append(jnp.concatenate(parts, axis=1).astype(BF16).astype(F32))
+        for ref, flip in ((mine_ref, 0), (theirs_ref, 2)):
+            at = quarter_ref[0] ^ flip
+            chosen = found[0]
+            for t in range(1, 4):
+                chosen = jnp.where(at == t, found[t], chosen)
+            ref[...] = chosen.astype(BF16)
+
+    part = pl.BlockSpec((rows, 2 * block), lambda j: (j, 0))
+    return pl.pallas_call(
+        kernel,
+        grid=(blocks,),
+        out_shape=(jax.ShapeDtypeStruct((blocks * rows, 2 * block), BF16),) * 2,
+        in_specs=[
+            pl.BlockSpec(memory_space=pltpu.SMEM),
+            pl.BlockSpec((rows, 2, 4 * block), lambda j: (0, 0, j)),
+        ],
+        out_specs=(part, part),
+        compiler_params=pltpu.CompilerParams(vmem_limit_bytes=32 << 20),
+    )(quarter.reshape(1).astype(jnp.int32), weight)
+
+
+def gateup_step(master, moment, average, shares, quarter, rate):
+    rows, _, hidden_all = master.shape
+    wide = lax.axis_size("wide")
+    units, each = quarter_columns(wide, hidden_all)
+    block = HIDDEN_BLOCK
+    blocks = hidden_all // (4 * block)
+    if wide != BLOCK:
+        split = jnp.stack(shares)[jnp.arange(4) ^ quarter]
+        split = split.reshape(4, blocks, rows, 2, each, units).transpose(2, 3, 1, 4, 0, 5)
+        return nesterov(
+            master, moment, average, split.reshape(master.shape).astype(F32), rate
+        )
+
+    def kernel(quarter_ref, p_ref, m_ref, a_ref, *refs):
+        ins, outs = refs[:4], refs[4:]
+        given = [ref[...].astype(F32) for ref in ins]
+        found = []
+        for t in range(4):
+            at = quarter_ref[0] ^ t
+            chosen = given[0]
+            for n in range(1, 4):
+                chosen = jnp.where(at == n, given[n], chosen)
+            found.append(chosen)
+        for k in range(2):
+            parts = []
+            for w in range(each):
+                low = k * block + w * units
+                parts += [found[t][:, low : low + units] for t in range(4)]
+            done = nesterov(
+                p_ref[:, k, :], m_ref[:, k, :], a_ref[:, k, :], jnp.concatenate(parts, 1), rate
+            )
+            for ref, value in zip(outs, done):
+                ref[:, k, :] = value
+
+    whole = pl.BlockSpec((rows, 2, 4 * block), lambda j: (0, 0, j))
+    part = pl.BlockSpec((rows, 2 * block), lambda j: (j, 0))
+    return pl.pallas_call(
+        kernel,
+        grid=(blocks,),
+        out_shape=(jax.ShapeDtypeStruct(master.shape, F32),) * 3,
+        in_specs=[pl.BlockSpec(memory_space=pltpu.SMEM)] + [whole] * 3 + [part] * 4,
+        out_specs=(whole,) * 3,
+        compiler_params=pltpu.CompilerParams(vmem_limit_bytes=32 << 20),
+    )(quarter.reshape(1).astype(jnp.int32), master, moment, average, *shares)
 
 
 def rms_scale(values):
@@ -617,8 +944,8 @@
     own_heads = H // cores
     own_cols = own_heads * E
     hidden_all = gateup_weight.shape[2]
-    own_hidden = hidden_all // cores
-    units = hidden_all // (wide * cores)
+    units = hidden_all // (wide * 2 * cores)
+    quarter = (me % 2) * cores + core
     tokens = micro_count * seq_count * seq_len
 
     def by_core(mine, other, axis):
@@ -641,78 +968,133 @@
         )
         return core_part(split, axis), other_part(split, axis)
 
-    gains_full = gather_small(gains.astype(BF16)).transpose(1, 0, 2)
-    gains_full = gains_full.reshape(2, width).astype(F32)
+    def to_beside(partial):
+        other = swap_cores(partial[tokens:].astype(BF16))
+        return fold(partial[:tokens], other)
+
+    def on_chip(partial):
+        other = swap_cores(partial[tokens:].astype(BF16))
+        return partial[:tokens].astype(F32) + other.astype(F32)
+
+    def when(values, *needed):
+        return after(values, *needed) if wide == BLOCK else values
+
     qkv_piece = rows_of_core(qkv_weight.astype(BF16).transpose(1, 0, 2), 2)[0]
     qkv_piece = qkv_piece.reshape(rows, 3 * own_cols)
-    out_piece = rows_of_core(out_weight.astype(BF16), 0)[0]
-    group = HIDDEN_BLOCK // units
-    gateup_split = gateup_weight.astype(BF16).reshape(rows, 2, wide // group, group, cores, units)
-    gateup_piece = core_part(gateup_split, 4).transpose(0, 2, 1, 3, 4)
-    gateup_piece = gateup_piece.reshape(rows, 2 * own_hidden)
-    down_piece = rows_of_core(down_weight.astype(BF16), 0)[0]
-
-    half = rows // cores
-    qkv_lines = gather_begin(qkv_piece)
-    rows_lines = gather_begin(jnp.concatenate([out_piece, down_piece]), qkv_lines[0][0])
-    gateup_lines = gather_begin(gateup_piece, rows_lines[0][0])
-    qkv_full = gather_end(qkv_lines)
-    rows_full = gather_end(rows_lines, qkv_full)
-    rows_full = rows_full.reshape(wide, half + units, width)
-    out_half = rows_full[:, :half]
-    out_full = by_core(out_half[:, None], swap_cores(out_half)[:, None], 1)
-    out_full = out_full.reshape(width, width)
-    down_full = rows_full[:, half:].reshape(own_hidden, width)
-
-    states = inputs.reshape(tokens, width).astype(F32)
-    first_scale = rms_scale(states)
-    normed_own = (states * first_scale * gains_full[0]).astype(BF16)
-    normed = jnp.concatenate([normed_own, swap_cores(normed_own)])
-    d_final_own = cotangent.reshape(tokens, width)
-    d_final = jnp.concatenate([d_final_own, swap_cores(d_final_own)])
+    gains_piece = jnp.pad(gains.T.astype(BF16), ((0, 0), (0, 126)))
+    out_piece = rows_of_core(out_weight.astype(BF16), 1)[0]
+    first_piece = jnp.concatenate([qkv_piece, out_piece, gains_piece], axis=1)
+    widths = (3 * own_cols, width // cores, 128)
+    wide_block = 2 * HIDDEN_BLOCK
+    gateup_mine, gateup_theirs = gateup_cast(gateup_weight, quarter)
+    down_split = down_weight.astype(BF16).reshape(4, units, width // wide_block, wide_block)
+    down_split = down_split.transpose(0, 2, 1, 3).reshape(4, -1, wide_block)
+
+    def ff_piece(gateup_part, at):
+        down_part = lax.dynamic_index_in_dim(down_split, at, 0, keepdims=False)
+        return jnp.concatenate([gateup_part, down_part])
+
+    inputs_own = inputs.reshape(tokens, width)
+    inputs_other = swap_cores(inputs_own)
     lengths_own = lengths.reshape(-1)
     seq_lengths = jnp.concatenate([lengths_own, swap_cores(lengths_own)])
+    pair = ff_pair(ff_piece(gateup_mine, quarter), ff_piece(gateup_theirs, quarter ^ 2))
+    if wide == BLOCK:
+        first_lines = line_and_plane(first_piece)
+        ff_lines = line_gather(after(pair, first_lines[2][1][0], first_lines[3][1][0]))
+        first_full = gather(first_piece, first_lines, widths, ff_lines[2:])
+    else:
+        first_full = gather(first_piece, None, widths)
+    qkv_full, out_half, gains_full = first_full
+    gains_full = gains_full[:, :2].T.astype(F32)
+    out_full = by_core(out_half, swap_cores(out_half), 1)
+    out_mine, out_theirs = rows_of_core(out_full, 0)
+
+    states = inputs_own.astype(F32)
+    first_scale = rms_scale(states)
+
+    def first_norm(values):
+        values = values.astype(F32)
+        return (values * rms_scale(values) * gains_full[0]).astype(BF16)
+
+    normed = jnp.concatenate([first_norm(inputs_own), first_norm(inputs_other)])
+    d_final_own = cotangent.reshape(tokens, width)
+    d_final_beside = permute(when(d_final_own, qkv_full), x_pairs())
+    d_finals = [d_final_own, swap_cores(d_final_own), d_final_beside, swap_cores(d_final_beside)]
     all_tokens = cores * tokens
 
     taps_own = rows_of_core(conv_taps, 0)[0]
     mix_own = rows_of_core(head_mix, 0)[0]
 
     projected = matmul(normed, qkv_full, ((1,), (0,)), BF16)
+    if wide == BLOCK:
+        ff_near = after(ff_lines[0], qkv_full)
+        ff_near_across = ff_cross(ff_near)
+        ff_far = ff_lines[1](projected)
+        ff_far_across = ff_cross(ff_far)
     context_own, probs = attention_forward(
         projected, base_rows_of(taps_own, seq_len, False), mix_own, seq_lengths, lags, reach
     )
-    gateup_full = gather_end(gateup_lines, context_own)
-    context = by_core(context_own[:tokens], swap_cores(context_own[tokens:]), 1)
-    middle = states + matmul(context, out_full, ((1,), (0,)))
+    if wide == BLOCK:
+        context_own = after(context_own, ff_near_across, d_final_beside)
+        ff_arrays = (ff_near, ff_near_across, ff_far, ff_far_across)
+    else:
+        ff_arrays = (pair,)
+    gateup_full, down_full = ff_end(ff_arrays, rows, units)
+    context_mine = context_own[:tokens]
+    context_theirs = swap_cores(context_own[tokens:])
+    context = by_core(context_mine, context_theirs, 1)
+    middle = states + (
+        matmul(context_mine, out_mine, ((1,), (0,)))
+        + matmul(context_theirs, out_theirs, ((1,), (0,)))
+    )
     second_scale = rms_scale(middle)
     second_own = (middle * second_scale * gains_full[1]).astype(BF16)
-    second = jnp.concatenate([second_own, swap_cores(second_own)])
-
-    hidden, d_gate_up, gateup_grad = feed_forward(
-        second, second.T, d_final, gateup_full, down_full
-    )
-    gateup_share = lax.psum_scatter(gateup_grad, "wide", scatter_dimension=0, tiled=True)
-    down_grad = matmul(hidden, d_final, ((0,), (0,)), BF16)
-    d_second_parts = matmul(d_gate_up, gateup_full, ((1,), (1,)))
-    d_second = d_second_parts[:tokens] + swap_cores(d_second_parts[tokens:])
+    second_beside = permute(second_own, x_pairs())
+    seconds = [second_own, swap_cores(second_own), second_beside, swap_cores(second_beside)]
+
+    hidden, d_gate_up, gateup_grad, down_grad = feed_forward(
+        seconds, d_finals, gateup_full, down_full, wide
+    )
+    beside = to_beside(
+        back_through_gateup(d_gate_up, gateup_full, 2 * tokens, 2 * tokens, BF16)
+    )
+    gateup_grad, down_grad = when(gateup_grad, beside), when(down_grad, beside)
+    ff_sends = ()
+    if wide == BLOCK:
+        pair_at, y = me // 8, (me // 2) % 2
+        ff_sends = [
+            ff_part(gateup_grad, down_grad, at, 1 - y) for at in (1 - pair_at, pair_at)
+        ]
+        arrived_far, arrived_near = (permute(send, Y_PAIR) for send in ff_sends)
+    hidden = when(hidden, *ff_sends)
     result_parts = matmul(hidden, down_full, ((1,), (0,)))
-    output = middle + (result_parts[:tokens] + swap_cores(result_parts[tokens:]))
+    d_second_here = on_chip(
+        back_through_gateup(d_gate_up, gateup_full, 0, 2 * tokens, F32, ff_sends)
+    )
+    d_second_here = when(d_second_here, result_parts)
+    d_second = d_second_here + permute(beside, x_pairs()).astype(F32)
+    result_beside = when(to_beside(result_parts[2 * tokens :]), d_second)
+    result_arrived = permute(result_beside, x_pairs())
+    output = middle + (on_chip(result_parts[: 2 * tokens]) + result_arrived.astype(F32))
     output = output.astype(BF16).reshape(inputs.shape)
 
     d_output = d_final_own.astype(F32)
     second_gain, d_norm_two = norm_back(middle, second_scale, gains_full[1], d_second)
     d_middle = d_output + d_norm_two
     d_attended = d_middle.astype(BF16)
-    d_context = matmul(d_attended, out_full, ((1,), (1,)), BF16)
-    mine, theirs = rows_of_core(d_context, 1)
+    theirs = matmul(d_attended, out_theirs, ((1,), (1,)), BF16)
+    mine = matmul(d_attended, out_mine, ((1,), (1,)), BF16)
     d_context_all = jnp.concatenate([mine, swap_cores(theirs)])
-    out_grad = matmul(context, d_attended, ((0,), (0,)), BF16).reshape(wide, rows, width)
-    out_mine, out_theirs = rows_of_core(out_grad, 1)
-    out_grad = fold(out_mine, swap_cores(out_theirs))
-    rows_grad = jnp.concatenate([out_grad, down_grad.reshape(wide, units, width)], axis=1)
-    rows_share = scatter_sum(rows_grad.reshape(-1, width))
-    out_share, down_share = rows_share[:half], rows_share[half:]
-
+    out_part = lax.dynamic_slice_in_dim(d_attended, (1 - core) * own_cols, own_cols, axis=1)
+    out_sent = matmul(context, out_part, ((0,), (0,)), BF16)
+    out_part = lax.dynamic_slice_in_dim(d_attended, core * own_cols, own_cols, axis=1)
+    out_kept = matmul(context, out_part, ((0,), (0,)), BF16)
+    d_context_all = when(d_context_all, out_sent, out_kept)
+    if wide == BLOCK:
+        far = fold(ff_part(gateup_grad, down_grad, 1 - pair_at, y), arrived_far)
+        d_context_all = after(d_context_all, far)
+        ff_steps = line_begin(far)
     d_projected, taps_grad, mix_grad = attention_backward(
         projected,
         probs,
@@ -723,9 +1105,26 @@
         lags,
         reach,
     )
+    if wide == BLOCK:
+        d_projected = after(d_projected, result_arrived, *ff_steps)
     qkv_grad = matmul(normed, d_projected, ((0,), (0,)), BF16)
-    qkv_share = scatter_sum(qkv_grad)
-    d_normed_parts = matmul(d_projected, qkv_full, ((1,), (1,)))
+    out_grad = fold(out_kept, swap_cores(out_sent))
+    sends, kept = scatter_begin(qkv_grad, out_grad)
+    arrivals = scatter_first(sends, kept)
+    d_normed_parts = matmul(when(d_projected, *sends), qkv_full, ((1,), (1,)))
+    ff_steps_done = ()
+    if wide == BLOCK:
+        ff_steps = line_middle(far, *(after(step, *sends) for step in ff_steps))
+        d_normed_parts = after(d_normed_parts, *ff_steps)
+        near = fold(
+            ff_part(gateup_grad, down_grad, pair_at, y), after(arrived_near, *sends)
+        )
+        ff_total = line_end(near, far, *ff_steps)
+        ff_steps_done = (ff_total,)
+    else:
+        ff_total = ff_scatter_whole(gateup_grad, down_grad)
+    ff_mine, ff_theirs = ff_last(ff_total)
+    first_sums = scatter_plane(sends, kept, arrivals, ff_steps_done)
     d_normed = d_normed_parts[:tokens] + swap_cores(d_normed_parts[tokens:])
     first_gain, d_norm_one = norm_back(states, first_scale, gains_full[0], d_normed)
     input_grad = (d_middle + d_norm_one).astype(BF16).reshape(inputs.shape)
@@ -742,19 +1141,6 @@
     taps_total = packed[2 * width : 2 * width + conv_taps.size].reshape(conv_taps.shape)
     mix_total = packed[2 * width + conv_taps.size :].reshape(head_mix.shape)
 
-    qkv_other = swap_cores(qkv_share)
-    qkv_total = by_core(
-        qkv_share.reshape(rows, 3, own_cols), qkv_other.reshape(rows, 3, own_cols), 2
-    ).transpose(1, 0, 2)
-    rows_other = swap_cores(rows_share)
-    out_total = by_core(out_share, rows_other[:half], 0)
-    gateup_other = swap_cores(gateup_share)
-    split_shape = (rows, wide // group, 2, group, 1, units)
-    gateup_total = by_core(
-        gateup_share.reshape(split_shape), gateup_other.reshape(split_shape), 4
-    ).transpose(0, 2, 1, 3, 4, 5).reshape(gateup_weight.shape)
-    down_total = by_core(down_share, rows_other[half:], 0)
-
     tokens_all = tokens * cores * wide
 
     def rate_for(position):
@@ -763,6 +1149,29 @@
     def step(master, moment, average, gradient, position):
         return nesterov(master, moment, average, gradient.astype(F32), rate_for(position))
 
+    ff_shares = [ff_mine, swap_cores(ff_mine), ff_theirs, swap_cores(ff_theirs)]
+    gateup_tall = ff_mine.shape[0] - width // wide_block * units
+    down_shares = jnp.stack([share[gateup_tall:] for share in ff_shares])
+    down_total = down_shares[jnp.arange(4) ^ quarter].reshape(4, -1, units, wide_block)
+    down_total = down_total.transpose(0, 2, 1, 3).reshape(down_weight.shape)
+    gateup_done = gateup_step(
+        gateup_weight,
+        gateup_momentum,
+        gateup_average,
+        [share[:gateup_tall] for share in ff_shares],
+        quarter,
+        rate_for(5),
+    )
+    down_done = step(down_weight, down_momentum, down_average, down_total, 6)
+
+    first_share = scatter_line(first_sums, gateup_done[0], down_done[0], packed)
+    first_other = swap_cores(first_share)
+    qkv_total = by_core(
+        first_share[:, : 3 * own_cols].reshape(rows, 3, own_cols),
+        first_other[:, : 3 * own_cols].reshape(rows, 3, own_cols),
+        2,
+    ).transpose(1, 0, 2)
+    out_total = by_core(first_share[:, 3 * own_cols :], first_other[:, 3 * own_cols :], 1)
     return (
         output,
         input_grad,
@@ -771,8 +1180,8 @@
         *step(out_weight, out_momentum, out_average, out_total, 2),
         *step(conv_taps, taps_momentum, taps_average, taps_total, 3),
         *step(head_mix, mix_momentum, mix_average, mix_total, 4),
-        *step(gateup_weight, gateup_momentum, gateup_average, gateup_total, 5),
-        *step(down_weight, down_momentum, down_average, down_total, 6),
+        *gateup_done,
+        *down_done,
     )
 
 

time: 869 us -> 726 us (0.84)
  waiting for transfers between devices: 304 us -> 161 us
  Pallas kernels: 148 us -> 191 us
  local copies, waits for them, and re-layouts: 88.7 us -> 70.8 us
  starting transfers between devices: 113 us -> 96.6 us
  other arithmetic: 111 us -> 126 us
  between operations: 16.6 us -> 2.65 us
  matrix products: 77.8 us -> 68.7 us
    ppermute x83 -> x58, waiting for transfers between devices: 304 us -> 159 us  [permute(): return lax.ppermute(values, 'wide', pairs)]
    pallas_call x4 -> x7, Pallas kernels: 60.8 us -> 104 us  [the longest x1 50.6 us: feed_forward(): pl.pallas_call(kernel, grid=(blocks,), out_shape=(jax.ShapeDtypeStruct((t...]
    convert_element_type x21 -> x15, other arithmetic: 22.6 us -> 45.4 us  [fold(): return sum((term.astype(F32) for term in terms)).astype(BF16)]
    ppermute x83 -> x58, starting transfers between devices: 111 us -> 94.1 us  [permute(): return lax.ppermute(values, 'wide', pairs)]
    add x7 -> x6, other arithmetic: 27.7 us -> 10.4 us  [nesterov(): AVERAGE * average + (1.0 - AVERAGE) * new_master]
    dot_general x9 -> x10, matrix products: 77.8 us -> 68.7 us  [matmul(): lax.dot_general(a, b, (dims, ((), ())), preferred_element_type=F32)]
    unnamed x244 -> x214, local copies, waits for them, and re-layouts: 30.1 us -> 37 us
  transfers between devices with their start and end apart: 99 -> 77, of which waited for: 36 -> 28; matrix products, arithmetic and copies ran while one was open for 23% -> 31% of each run, Pallas kernels for 13% -> 18%
where the time goes in v2:
time: 726 us; the launch traced here: 717 us
  Pallas kernels  191 us (26%)
  waiting for transfers between devices  161 us (22%)
  other arithmetic  126 us (17%)
  starting transfers between devices  96.6 us (13%)
  local copies, waits for them, and re-layouts  70.8 us (10%)
  matrix products  68.7 us (9%)
    ppermute x58, waiting for transfers between devices, permute(): return lax.ppermute(values, 'wide', pairs)  159 us
    ppermute x58, starting transfers between devices, permute(): return lax.ppermute(values, 'wide', pairs)  94.1 us
    dot_general x10, matrix products, matmul(): lax.dot_general(a, b, (dims, ((), ())), preferred_element_type=F32)  68.7 us
    pallas_call x1, Pallas kernels, feed_forward(): pl.pallas_call(kernel, grid=(blocks,), out_shape=(jax.ShapeDtypeStruct((t...  50.6 us
    pallas_call x1, Pallas kernels, attention_backward(): pl.pallas_call(kernel, grid=(seqs,), out_shape=(jax.ShapeDtypeStruct(proj...  46.3 us
    convert_element_type x15, other arithmetic, fold(): return sum((term.astype(F32) for term in terms)).astype(BF16)  45.4 us
    pallas_call x1, Pallas kernels, attention_forward(): pl.pallas_call(kernel, grid=(seqs,), out_shape=(jax.ShapeDtypeStruct((seq...  40.4 us
    unnamed x214, local copies, waits for them, and re-layouts  37 us
  transfers between devices with their start and end apart: 77, of which 28 were waited for; matrix products, arithmetic and copies ran while one was open for 31% of the time, Pallas kernels for 18%

profile of v2, /device:TPU:0, one launch (start us, length us, event | category | flops | bytes accessed | tf_op | source)
XLA Modules:
  0.0 716.9 jit_solution(15686259757888449154)
XLA Ops:
  16.3 7.6 %collective-permute-done.5 = bf16[96,3200]{1,0:T(8,128)(2,1)S(1)} collective-permute-done((bf16[96,3200]{1,0:T(8,128)(2,1)S(1)}, bf16[96,3200]{1,0:T(8,128)(2,1)S(1)}, u32[]{:S(2)}, u32[]{:S(2)}) %collective-permute-start.5) | collective-permute-done | bytes 614432 | tf_op jit(solution)/shard_map/ppermute | solution.py:26
  54.3 7.2 %collective-permute-done.19 = bf16[576,512]{1,0:T(8,128)(2,1)} collective-permute-done((bf16[576,512]{1,0:T(8,128)(2,1)}, bf16[576,512]{1,0:T(8,128)(2,1)}, u32[]{:S(2)}, u32[]{:S(2)}) %collective-permute-start.19) | collective-permute-done | bytes 589856 | tf_op jit(solution)/shard_map/ppermute | solution.py:26
  64.0 5.5 collective-permute-done.15
  78.2 12.6 %collective-permute-done.3.refs_3_ = bf16[96,3200]{1,0:T(8,128)(2,1)S(1)} collective-permute-done((bf16[96,3200]{1,0:T(8,128)(2,1)S(1)}, bf16[96,3200]{1,0:T(8,128)(2,1)S(1)}, u32[]{:S(2)}, u32[]{:S(2)}) %collective-permute-start.3) | collective-permute-done | bytes 614432 | tf_op jit(solution)/shard_map/ppermute | solution.py:26
  109.0 11.8 %collective-permute-done.16.refs_13_ = bf16[96,3200]{1,0:T(8,128)(2,1)} collective-permute-done((bf16[96,3200]{1,0:T(8,128)(2,1)}, bf16[96,3200]{1,0:T(8,128)(2,1)}, u32[]{:S(2)}, u32[]{:S(2)}) %collective-permute-start.16) | collective-permute-done | bytes 614432 | tf_op jit(solution)/shard_map/ppermute | solution.py:26
  123.5 5.5 collective-permute-done.14.refs_11_
  132.4 7.8 %shard_map.413 = (bf16[4,4,96,2304]{3,2,1,0:T(8,128)(2,1)}, bf16[4,4,96,768]{3,2,1,0:T(8,128)(2,1)}, bf16[4,4,96,128]{3,2,1,0:T(8,128)(2,1)S(1)}) custom-call(s32[2]{0:T(128)S(1)} %pad_add_fusion.1.index_ref, bf16[96,3200]{1,0:T(8,128)(2,1)S(1)} %copy-done.17, bf16[96,3200]{1,0:T(8,128)(2,1)S(1)} %copy-done.10, bf16[96,3200]{1,0:T(8,128)(2,1)S(1)} %copy-done.12, ...), custom_call_target="tpu_custom_call" | custom-call | tf_op jit(solution)/shard_map/pallas_call | solution.py:156
  145.8 14.3 %convolution_convert_fusion.1.proj_ref.refs_1_ = bf16[1024,2304]{1,0:T(8,128)(2,1)} fusion(bf16[1536,2304]{1,0:T(8,128)(2,1)} %bitcast.269, bf16[512,1536]{1,0:T(8,128)(2,1)S(1)} %get-tuple-element.231, bf16[512,1536]{1,0:T(8,128)(2,1)S(1)} %get-tuple-element.230), kind=kOutput, calls=%fused_computation.2 | convolution fusion | flops 7256408064 | bytes 14942208 | tf_op jit(solution)/shard_map/dot_general | solution.py:901
  177.2 40.4 %shard_map.414 = (bf16[1024,768]{1,0:T(8,128)(2,1)S(1)}, f32[8,4,256,256]{3,2,1,0:T(8,128)}) custom-call(s32[4]{0:T(128)S(1)} %pad_add_fusion.len_ref, f32[8,2]{1,0:T(8,128)S(1)} %copy.236.mix_ref, f32[8,8,256]{2,1,0:T(8,128)S(1)} %pad.11.base_ref, bf16[1024,2304]{1,0:T(8,128)(2,1)} %convolution_convert_fusion.1.proj_ref.refs_1_), custom_call_target="tpu_custom_call" | custom-call | flops 20132659200 | bytes 20971520 | tf_op jit(solution)/shard_map/pallas_call | solution.py:494
  240.0 31.6 %collective-permute-done.30.refs_2_ = bf16[512,1536]{1,0:T(8,128)(2,1)} collective-permute-done((bf16[512,1536]{1,0:T(8,128)(2,1)}, bf16[512,1536]{1,0:T(8,128)(2,1)}, u32[]{:S(2)}, u32[]{:S(2)}) %collective-permute-start.30) | collective-permute-done | bytes 1572896 | tf_op jit(solution)/shard_map/ppermute | solution.py:26
  271.7 20.3 %collective-permute-done.36.refs_3_ = bf16[2,2,576,512]{3,2,1,0:T(8,128)(2,1)} collective-permute-done((bf16[2,2,576,512]{3,2,1,0:T(8,128)(2,1)}, bf16[2,2,576,512]{3,2,1,0:T(8,128)(2,1)}, u32[]{:S(2)}, u32[]{:S(2)}) %collective-permute-start.36) | collective-permute-done | bytes 2359328 | tf_op jit(solution)/shard_map/ppermute | solution.py:26
  293.6 12.0 %shard_map.420 = (bf16[4,1536,512]{2,1,0:T(8,128)(2,1)}, bf16[1024,1536]{1,0:T(8,128)(2,1)}) custom-call(s32[2]{0:T(128)S(1)} %pad_add_fusion.2.index_ref, bf16[2,2,576,512]{3,2,1,0:T(8,128)(2,1)S(1)} %copy-done.1, bf16[2,2,576,512]{3,2,1,0:T(8,128)(2,1)S(1)} %copy-done.8, bf16[2,2,576,512]{3,2,1,0:T(8,128)(2,1)} %pad_maximum_fusion.2.refs_2_, ...), custom_call_target="tpu_custom_call" | custom-call | tf_op jit(solution)/shard_map/pallas_call | solution.py:327
  305.6 50.6 %shard_map.421 = (bf16[2048,1024]{1,0:T(8,128)(2,1)}, bf16[2048,2048]{1,0:T(8,128)(2,1)}, bf16[16,384,512]{2,1,0:T(8,128)(2,1)}, bf16[16,192,512]{2,1,0:T(8,128)(2,1)}) custom-call(bf16[512,1536]{1,0:T(8,128)(2,1)} %multiply_convert_fusion.refs_0_, bf16[512,1536]{1,0:T(8,128)(2,1)} %collective-permute-done.29.refs_1_, ...), custom_call_target="tpu_custom_call" | custom-call | flops 38654705664 | bytes 50331648 | tf_op jit(solution)/shard_map/pallas_call | solution.py:735
  356.2 10.7 %shard_map.422 = bf16[1024,1536]{1,0:T(8,128)(2,1)S(1)} custom-call(bf16[2048,2048]{1,0:T(8,128)(2,1)} %get-tuple-element.52.d_ref, bf16[4,1536,512]{2,1,0:T(8,128)(2,1)} %get-tuple-element.48.refs_8_.gu_ref), custom_call_target="tpu_custom_call" | custom-call | flops 6442450944 | bytes 16777216 | tf_op jit(solution)/shard_map/pallas_call | solution.py:775
  386.3 12.4 %shard_map.426 = f32[1024,1536]{1,0:T(8,128)} custom-call(bf16[2048,2048]{1,0:T(8,128)(2,1)} %get-tuple-element.52.d_ref, bf16[4,1536,512]{2,1,0:T(8,128)(2,1)} %get-tuple-element.48.refs_8_.gu_ref, bf16[2,2,576,512]{3,2,1,0:T(8,128)(2,1)} %pad_maximum_fusion.3.refs_1_.refs_0_, bf16[2,2,576,512]{3,2,1,0:T(8,128)(2,1)S(1)} %pad_maximum_fusion.4.refs_2_.refs_1_), custom_call_target="tpu_custom_call" | custom-call | flops 6442450944 | bytes 16777216 | tf_op jit(solution)/shard_map/pallas_call | solution.py:775
  402.6 12.7 %fusion.75 = (bf16[2048,1536]{1,0:T(8,128)(2,1)S(1)}, f32[2048,1536]{1,0:T(8,128)}) fusion(bf16[2048,1024]{1,0:T(8,128)(2,1)} %shard_map.425, bf16[1024,1536]{1,0:T(8,128)(2,1)} %get-tuple-element.49.refs_9_), kind=kOutput, calls=%fused_computation.218 | convolution fusion | flops 6445596672 | bytes 26214400 | tf_op jit(solution)/shard_map/dot_general | solution.py:901
  465.8 46.3 %shard_map.431 = (bf16[1024,2304]{1,0:T(8,128)(2,1)}, f32[8,8,256]{2,1,0:T(8,128)S(1)}, f32[4,8,256]{2,1,0:T(8,128)S(1)}) custom-call(s32[4]{0:T(128)S(1)} %pad_add_fusion.len_ref, f32[8,2]{1,0:T(8,128)S(1)} %copy.236.mix_ref, f32[8,8,256]{2,1,0:T(8,128)S(1)} %pad.13.base_ref, bf16[1024,2304]{1,0:T(8,128)(2,1)} %convolution_convert_fusion.1.proj_ref.refs_1_, ...), custom_call_target="tpu_custom_call" | custom-call | flops 15971909632 | bytes 20971520 | tf_op jit(solution)/shard_map/pallas_call | solution.py:618
  513.8 10.6 %convolution_convert_fusion = bf16[1536,2304]{1,0:T(8,128)(2,1)S(1)} fusion(bf16[1024,2304]{1,0:T(8,128)(2,1)} %shard_map.432.refs_0_, bf16[512,1536]{1,0:T(8,128)(2,1)} %copy-done.60, bf16[512,1536]{1,0:T(8,128)(2,1)} %copy-done.59), kind=kOutput, calls=%fused_computation.1 | convolution fusion | flops 7257587712 | bytes 14942208 | tf_op jit(solution)/shard_map/dot_general | solution.py:901
  546.4 11.7 %fusion.76.refs_0_ = f32[1024,1536]{1,0:T(8,128)} fusion(bf16[1024,2304]{1,0:T(8,128)(2,1)S(1)} %copy-done.29, bf16[1536,2304]{1,0:T(8,128)(2,1)} %bitcast.272), kind=kOutput, calls=%fused_computation.219 | convolution fusion | flops 7247757312 | bytes 18087936 | tf_op jit(solution)/shard_map/dot_general | solution.py:901
  580.9 6.3 collective-permute-done.67
  599.4 16.7 %collective-permute-done.61 = bf16[2,576,512]{2,1,0:T(8,128)(2,1)S(1)} collective-permute-done((bf16[2,576,512]{2,1,0:T(8,128)(2,1)S(1)}, bf16[2,576,512]{2,1,0:T(8,128)(2,1)S(1)}, u32[]{:S(2)}, u32[]{:S(2)}) %collective-permute-start.61) | collective-permute-done | bytes 1179680 | tf_op jit(solution)/shard_map/ppermute | solution.py:26
  668.5 7.7 %shard_map.439 = (f32[96,2,4096]{2,1,0:T(2,128)}, f32[96,2,4096]{2,1,0:T(2,128)}, f32[96,2,4096]{2,1,0:T(2,128)}) custom-call(s32[1]{0:T(128)} %bitcast.10.quarter_ref, f32[96,2,4096]{2,1,0:T(2,128)S(1)} %copy-done.4, f32[96,2,4096]{2,1,0:T(2,128)S(1)} %copy-done.14, f32[96,2,4096]{2,1,0:T(2,128)S(1)} %copy-done.15, ...), custom_call_target="tpu_custom_call" | custom-call | tf_op jit(solution)/shard_map/pallas_call | solution.py:876
  688.9 5.5 collective-permute-start.72
  694.4 8.1 %fusion.9 = (bf16[512,1536]{1,0:T(8,128)(2,1)}, bf16[512,1536]{1,0:T(8,128)(2,1)}) fusion(f32[512]{0:T(512)S(1)} %broadcast_multiply_fusion, f32[1536]{0:T(1024)S(1)} %copy-done.78, f32[512]{0:T(512)S(1)} %bitcast.296, bf16[2,1,256,1536]{3,2,1,0:T(8,128)(2,1)} %param.24, f32[512,1536]{1,0:T(8,128)} %collective-permute-done.50, f32[1024,1536]{1,0:T(8,128)} %shard_map.436, ...), kind=kLoop, calls=%fused_computation.23 | loop fusion | flops 17301504 | bytes 25186304 | tf_op jit(solution)/shard_map/convert_element_type | solution.py:1130
  (525 shorter events, 338.5 us)
Async XLA Ops:
  54.2 37.4 %collective-permute-start.24 = (bf16[512,1536]{1,0:T(8,128)(2,1)}, bf16[512,1536]{1,0:T(8,128)(2,1)}, u32[]{:S(2)}, u32[]{:S(2)}) collective-permute-start(bf16[512,1536]{1,0:T(8,128)(2,1)} %bitcast), channel_id=1, source_target_pairs={{0,16},{16,0},{1,17},{17,1},{2,18},{18,2},{3,19},{19,3},{4,20},{20... | collective-permute-start | bytes 4718600 | tf_op jit(solution)/shard_map/ppermute | solution.py:30
  97.2 34.1 %collective-permute-start.21 = (bf16[2,576,512]{2,1,0:T(8,128)(2,1)}, bf16[2,576,512]{2,1,0:T(8,128)(2,1)}, u32[]{:S(2)}, u32[]{:S(2)}) collective-permute-start(bf16[2,576,512]{2,1,0:T(8,128)(2,1)} %collective-permute-done.20), channel_id=1, source_target_pairs={{4,8},{5,9},{6,10},{7,11},{8,12},{9,13},{10,14},{11,15},{20,24},{2... | collective-permute-start | bytes 3538952 | tf_op jit(solution)/shard_map/ppermute | solution.py:26
  123.4 52.9 %collective-permute-start = (s32[2]{0:T(128)S(1)}, s32[2]{0:T(128)S(1)}, u32[]{:S(2)}, u32[]{:S(2)}) collective-permute-start(s32[2]{0:T(128)S(1)} %bitcast.298), channel_id=1, source_target_pairs={{0,16},{16,0},{1,17},{17,1},{2,18},{18,2},{3,19},{19,3},{4,20},{20... | collective-permute-start | bytes 32 | tf_op jit(solution)/shard_map/ppermute | solution.py:30
  172.6 46.3 %collective-permute-start.25 = (bf16[2,2,576,512]{3,2,1,0:T(8,128)(2,1)}, bf16[2,2,576,512]{3,2,1,0:T(8,128)(2,1)S(1)}, u32[]{:S(2)}, u32[]{:S(2)}) collective-permute-start(bf16[2,2,576,512]{3,2,1,0:T(8,128)(2,1)} %shard_map.415.refs_0_), channel_id=1, source_target_pairs={{0,2},{1,3},{2,0},{3,1},{4,6},{5,7},{6,4},{7,5},{8,10},{9,11},{10,... | collective-permute-start | bytes 7077896 | tf_op jit(solution)/shard_map/ppermute | solution.py:26
  176.3 46.4 %collective-permute-start.27 = (bf16[1536,768]{1,0:T(8,128)(2,1)}, bf16[1536,768]{1,0:T(8,128)(2,1)}, u32[]{:S(2)}, u32[]{:S(2)}) collective-permute-start(bf16[1536,768]{1,0:T(8,128)(2,1)} %bitcast.24), channel_id=1, source_target_pairs={{0,16},{16,0},{1,17},{17,1},{2,18},{18,2},{3,19},{19,3},{4,20},{20... | collective-permute-start | bytes 7077896 | tf_op jit(solution)/shard_map/ppermute | solution.py:30
  176.4 42.4 %collective-permute-start.26 = (bf16[512,1536]{1,0:T(8,128)(2,1)}, bf16[512,1536]{1,0:T(8,128)(2,1)}, u32[]{:S(2)}, u32[]{:S(2)}) collective-permute-start(bf16[512,1536]{1,0:T(8,128)(2,1)} %shard_map.416), channel_id=1, source_target_pairs={{0,1},{1,0},{2,3},{3,2},{4,5},{5,4},{6,7},{7,6},{8,9},{9,8},{10,11... | collective-permute-start | bytes 4718600 | tf_op jit(solution)/shard_map/ppermute | solution.py:26
  234.6 37.0 %collective-permute-start.30 = (bf16[512,1536]{1,0:T(8,128)(2,1)}, bf16[512,1536]{1,0:T(8,128)(2,1)}, u32[]{:S(2)}, u32[]{:S(2)}) collective-permute-start(bf16[512,1536]{1,0:T(8,128)(2,1)} %multiply_convert_fusion.refs_0_), channel_id=1, source_target_pairs={{0,1},{1,0},{2,3},{3,2},{4,5},{5,4},{6,7},{7,6},{8,9},{9,8},{10,11... | collective-permute-start | bytes 4718600 | tf_op jit(solution)/shard_map/ppermute | solution.py:26
  238.0 53.9 %collective-permute-start.36 = (bf16[2,2,576,512]{3,2,1,0:T(8,128)(2,1)}, bf16[2,2,576,512]{3,2,1,0:T(8,128)(2,1)}, u32[]{:S(2)}, u32[]{:S(2)}) collective-permute-start(bf16[2,2,576,512]{3,2,1,0:T(8,128)(2,1)} %pad_maximum_fusion.2.refs_2_), channel_id=1, source_target_pairs={{0,2},{1,3},{2,0},{3,1},{4,6},{5,7},{6,4},{7,5},{8,10},{9,11},{10,... | collective-permute-start | bytes 7077896 | tf_op jit(solution)/shard_map/ppermute | solution.py:26
  239.5 66.1 %collective-permute-start.32 = (bf16[512,1536]{1,0:T(8,128)(2,1)}, bf16[512,1536]{1,0:T(8,128)(2,1)}, u32[]{:S(2)}, u32[]{:S(2)}) collective-permute-start(bf16[512,1536]{1,0:T(8,128)(2,1)} %bitcast.22.refs_4_), channel_id=1, source_target_pairs={{0,16},{16,0},{1,17},{17,1},{2,18},{18,2},{3,19},{19,3},{4,20},{20... | collective-permute-start | bytes 4718600 | tf_op jit(solution)/shard_map/ppermute | solution.py:30
  239.5 66.1 %collective-permute-start.33 = (bf16[512,1536]{1,0:T(8,128)(2,1)}, bf16[512,1536]{1,0:T(8,128)(2,1)}, u32[]{:S(2)}, u32[]{:S(2)}) collective-permute-start(bf16[512,1536]{1,0:T(8,128)(2,1)} %collective-permute-done.26.refs_2_.refs_6_), channel_id=1, source_target_pairs={{0,16},{16,0},{1,17},{17,1},{2,18},{18,2},{3,19},{19,3},{4,20},{20... | collective-permute-start | bytes 4718600 | tf_op jit(solution)/shard_map/ppermute | solution.py:30
  240.0 65.6 %collective-permute-start.29 = (bf16[512,1536]{1,0:T(8,128)(2,1)}, bf16[512,1536]{1,0:T(8,128)(2,1)}, u32[]{:S(2)}, u32[]{:S(2)}) collective-permute-start(bf16[512,1536]{1,0:T(8,128)(2,1)} %multiply_convert_fusion.refs_0_), channel_id=1, source_target_pairs={{0,16},{16,0},{1,17},{17,1},{2,18},{18,2},{3,19},{19,3},{4,20},{20... | collective-permute-start | bytes 4718600 | tf_op jit(solution)/shard_map/ppermute | solution.py:30
  374.8 47.3 %collective-permute-start.41 = (bf16[512,1536]{1,0:T(8,128)(2,1)}, bf16[512,1536]{1,0:T(8,128)(2,1)}, u32[]{:S(2)}, u32[]{:S(2)}) collective-permute-start(bf16[512,1536]{1,0:T(8,128)(2,1)} %add_convert_fusion.3.refs_1_), channel_id=1, source_target_pairs={{0,1},{1,0},{2,3},{3,2},{4,5},{5,4},{6,7},{7,6},{8,9},{9,8},{10,11... | collective-permute-start | bytes 4718600 | tf_op jit(solution)/shard_map/ppermute | solution.py:26
  384.8 66.7 %collective-permute-start.44 = (bf16[2,2,576,512]{3,2,1,0:T(8,128)(2,1)}, bf16[2,2,576,512]{3,2,1,0:T(8,128)(2,1)}, u32[]{:S(2)}, u32[]{:S(2)}) collective-permute-start(bf16[2,2,576,512]{3,2,1,0:T(8,128)(2,1)} %pad_maximum_fusion.3.refs_1_.refs_0_), channel_id=1, source_target_pairs={{0,2},{1,3},{2,0},{3,1},{4,6},{5,7},{6,4},{7,5},{8,10},{9,11},{10,... | collective-permute-start | bytes 7077896 | tf_op jit(solution)/shard_map/ppermute | solution.py:26
  398.7 159.4 %collective-permute-start.59 = (bf16[2,2,576,512]{3,2,1,0:T(8,128)(2,1)S(1)}, bf16[2,2,576,512]{3,2,1,0:T(8,128)(2,1)}, u32[]{:S(2)}, u32[]{:S(2)}) collective-permute-start(bf16[2,2,576,512]{3,2,1,0:T(8,128)(2,1)S(1)} %pad_maximum_fusion.4.refs_2_.refs_1_), channel_id=1, source_target_pairs={{0,2},{1,3},{2,0},{3,1},{4,6},{5,7},{6,4},{7,5},{8,10},{9,11},{10,... | collective-permute-start | bytes 7077896 | tf_op jit(solution)/shard_map/ppermute | solution.py:26
  439.3 74.6 %collective-permute-start.42 = (bf16[512,1536]{1,0:T(8,128)(2,1)}, bf16[512,1536]{1,0:T(8,128)(2,1)}, u32[]{:S(2)}, u32[]{:S(2)}) collective-permute-start(bf16[512,1536]{1,0:T(8,128)(2,1)} %shard_map.428), channel_id=1, source_target_pairs={{0,1},{1,0},{2,3},{3,2},{4,5},{5,4},{6,7},{7,6},{8,9},{9,8},{10,11... | collective-permute-start | bytes 4718600 | tf_op jit(solution)/shard_map/ppermute | solution.py:26
  445.0 81.5 %collective-permute-start.47 = (bf16[1536,768]{1,0:T(8,128)(2,1)}, bf16[1536,768]{1,0:T(8,128)(2,1)}, u32[]{:S(2)}, u32[]{:S(2)}) collective-permute-start(bf16[1536,768]{1,0:T(8,128)(2,1)} %convolution_convert_fusion.3.refs_1_), channel_id=1, source_target_pairs={{0,16},{16,0},{1,17},{17,1},{2,18},{18,2},{3,19},{19,3},{4,20},{20... | collective-permute-start | bytes 7077896 | tf_op jit(solution)/shard_map/ppermute | solution.py:30
  458.0 55.8 %collective-permute-start.45 = (bf16[2,576,512]{2,1,0:T(8,128)(2,1)}, bf16[2,576,512]{2,1,0:T(8,128)(2,1)}, u32[]{:S(2)}, u32[]{:S(2)}) collective-permute-start(bf16[2,576,512]{2,1,0:T(8,128)(2,1)} %select_bitcast_fusion), channel_id=1, source_target_pairs={{0,4},{1,5},{2,6},{3,7},{16,20},{17,21},{18,22},{19,23}} | collective-permute-start | bytes 3538952 | tf_op jit(solution)/shard_map/ppermute | solution.py:26
  460.3 53.5 %collective-permute-start.46 = (bf16[2,576,512]{2,1,0:T(8,128)(2,1)}, bf16[2,576,512]{2,1,0:T(8,128)(2,1)}, u32[]{:S(2)}, u32[]{:S(2)}) collective-permute-start(bf16[2,576,512]{2,1,0:T(8,128)(2,1)} %select_bitcast_fusion), channel_id=1, source_target_pairs={{12,8},{13,9},{14,10},{15,11},{28,24},{29,25},{30,26},{31,27}} | collective-permute-start | bytes 3538952 | tf_op jit(solution)/shard_map/ppermute | solution.py:26
  534.4 39.7 %collective-permute-start.62 = (bf16[2,96,3072]{2,1,0:T(8,128)(2,1)}, bf16[2,96,3072]{2,1,0:T(8,128)(2,1)}, u32[]{:S(2)}, u32[]{:S(2)}) collective-permute-start(bf16[2,96,3072]{2,1,0:T(8,128)(2,1)} %pad_maximum_fusion.9.refs_2_), channel_id=1, source_target_pairs={{0,1},{1,0},{2,3},{3,2},{4,5},{5,4},{6,7},{7,6},{8,9},{9,8},{10,11... | collective-permute-start | bytes 3538952 | tf_op jit(solution)/shard_map/ppermute | solution.py:26
  569.1 55.5 %collective-permute-start.58 = (bf16[2,96,3072]{2,1,0:T(8,128)(2,1)S(1)}, bf16[2,96,3072]{2,1,0:T(8,128)(2,1)}, u32[]{:S(2)}, u32[]{:S(2)}) collective-permute-start(bf16[2,96,3072]{2,1,0:T(8,128)(2,1)S(1)} %copy-done.25), channel_id=1, source_target_pairs={{0,1},{1,0},{2,3},{3,2},{4,5},{5,4},{6,7},{7,6},{8,9},{9,8},{10,11... | collective-permute-start | bytes 3538952 | tf_op jit(solution)/shard_map/ppermute | solution.py:26
  574.1 74.1 %collective-permute-start.50 = (f32[512,1536]{1,0:T(8,128)}, f32[512,1536]{1,0:T(8,128)}, u32[]{:S(2)}, u32[]{:S(2)}) collective-permute-start(f32[512,1536]{1,0:T(8,128)} %slice.265), channel_id=1, source_target_pairs={{0,16},{16,0},{1,17},{17,1},{2,18},{18,2},{3,19},{19,3},{4,20},{20... | collective-permute-start | bytes 9437192 | tf_op jit(solution)/shard_map/ppermute | solution.py:30
  576.8 49.9 %collective-permute-start.63 = (bf16[2,96,3072]{2,1,0:T(8,128)(2,1)}, bf16[2,96,3072]{2,1,0:T(8,128)(2,1)}, u32[]{:S(2)}, u32[]{:S(2)}) collective-permute-start(bf16[2,96,3072]{2,1,0:T(8,128)(2,1)} %add_convert_fusion.7), channel_id=1, source_target_pairs={{0,2},{1,3},{2,0},{3,1},{4,6},{5,7},{6,4},{7,5},{8,10},{9,11},{10,... | collective-permute-start | bytes 3538952 | tf_op jit(solution)/shard_map/ppermute | solution.py:26
  616.2 78.2 %collective-permute-start.38 = (bf16[512,1536]{1,0:T(8,128)(2,1)}, bf16[512,1536]{1,0:T(8,128)(2,1)}, u32[]{:S(2)}, u32[]{:S(2)}) collective-permute-start(bf16[512,1536]{1,0:T(8,128)(2,1)} %get-tuple-element.189), channel_id=1, source_target_pairs={{0,16},{16,0},{1,17},{17,1},{2,18},{18,2},{3,19},{19,3},{4,20},{20... | collective-permute-start | bytes 4718600 | tf_op jit(solution)/shard_map/ppermute | solution.py:30
  636.8 47.1 %collective-permute-start.71 = (bf16[96,3072]{1,0:T(8,128)(2,1)}, bf16[96,3072]{1,0:T(8,128)(2,1)}, u32[]{:S(2)}, u32[]{:S(2)}) collective-permute-start(bf16[96,3072]{1,0:T(8,128)(2,1)} %get-tuple-element.219), channel_id=1, source_target_pairs={{0,4},{1,5},{2,6},{3,7},{4,8},{5,9},{6,10},{7,11},{16,20},{17,21},... | collective-permute-start | bytes 1769480 | tf_op jit(solution)/shard_map/ppermute | solution.py:26
  (153 other events, 1843.9 us)

commit v3 on v2

--- a/solution.py
+++ b/solution.py
@@ -20,6 +20,7 @@
 F32 = jnp.float32
 BF16 = jnp.bfloat16
 SCALE = 1.0 / math.sqrt(E)
+FREE = pl.CostEstimate(flops=1, bytes_accessed=1, transcendentals=0)
 
 
 def permute(values, pairs):
@@ -51,6 +52,7 @@
 
     return pl.pallas_call(
         nothing,
+        cost_estimate=FREE,
         out_shape=jax.ShapeDtypeStruct(values.shape, values.dtype),
         in_specs=[pl.BlockSpec(memory_space=pl.ANY)] * (1 + len(needed)),
         out_specs=pl.BlockSpec(memory_space=pl.ANY),
@@ -155,6 +157,7 @@
 
     full = pl.pallas_call(
         assemble,
+        cost_estimate=FREE,
         out_shape=[jax.ShapeDtypeStruct((4, 4, rows, width), piece.dtype) for width in widths],
         in_specs=[pl.BlockSpec(memory_space=pltpu.SMEM)]
         + [pl.BlockSpec(memory_space=pl.ANY)] * (len(arrays) + len(needed)),
@@ -326,6 +329,7 @@
 
     return pl.pallas_call(
         assemble,
+        cost_estimate=FREE,
         out_shape=(
             jax.ShapeDtypeStruct(gateup_shape, BF16),
             jax.ShapeDtypeStruct(down_shape, BF16),
@@ -450,8 +454,8 @@
                 return carry
 
             lax.fori_loop(0, heads, build, 0)
-            pad_top[0:8, :] = jnp.zeros((8, size), F32)
-            pad_low[0:8, :] = jnp.zeros((8, size), F32)
+            pad_top[:, 0:8, :] = jnp.zeros((G, 8, size), F32)
+            pad_low[:, 0:8, :] = jnp.zeros((G, 8, size), F32)
 
         for n in range(3 * heads):
             split[n] = proj_ref[:, n * E : (n + 1) * E]
@@ -464,16 +468,16 @@
                 raw = dot_nt(split[h], split[heads + h])
                 masked = jnp.where(allowed, raw * SCALE, 0.0)
                 top = masked.astype(BF16).astype(F32)
-                pad_top[8 : 8 + size, :] = top
-                pad_low[8 : 8 + size, :] = masked - top
+                pad_top[c, 8 : 8 + size, :] = top
+                pad_low[c, 8 : 8 + size, :] = masked - top
                 for a in range(lags):
                     cols = slice(a * size, (a + 1) * size)
-                    left_top[:, cols] = pad_top[8 - a : 8 - a + size, :].astype(BF16)
-                    left_low[:, cols] = pad_low[8 - a : 8 - a + size, :].astype(BF16)
+                    left_top[c, :, cols] = pad_top[c, 8 - a : 8 - a + size, :].astype(BF16)
+                    left_low[c, :, cols] = pad_low[c, 8 - a : 8 - a + size, :].astype(BF16)
                 logits = (
-                    dot_nn(left_top[...], top_taps[h])
-                    + dot_nn(left_low[...], top_taps[h])
-                    + dot_nn(left_top[...], low_taps[h])
+                    dot_nn(left_top[c], top_taps[h])
+                    + dot_nn(left_low[c], top_taps[h])
+                    + dot_nn(left_top[c], low_taps[h])
                 )
                 logits = jnp.where(allowed, logits, -jnp.inf)
                 terms = jnp.exp(logits - jnp.max(logits, axis=-1, keepdims=True))
@@ -486,13 +490,14 @@
                 joined[h] = dot_nn(mixed.astype(BF16), split[2 * heads + h]).astype(BF16)
             return carry
 
-        lax.fori_loop(0, groups, group_step, 0)
+        lax.fori_loop(0, groups, group_step, 0, unroll=4)
         for h in range(heads):
             ctx_ref[:, h * E : (h + 1) * E] = joined[h]
 
     flops = 2 * heads * seqs * size * size * (3 * lags * size + 2 * E)
     return pl.pallas_call(
         kernel,
+        cost_estimate=FREE,
         grid=(seqs,),
         out_shape=(
             jax.ShapeDtypeStruct((seqs * size, heads * E), BF16),
@@ -511,17 +516,14 @@
         scratch_shapes=[
             pltpu.VMEM((heads, lags * size, size), BF16),
             pltpu.VMEM((heads, lags * size, size), BF16),
-            pltpu.VMEM((size + 8, size), F32),
-            pltpu.VMEM((size + 8, size), F32),
-            pltpu.VMEM((size, lags * size), BF16),
-            pltpu.VMEM((size, lags * size), BF16),
+            pltpu.VMEM((G, size + 8, size), F32),
+            pltpu.VMEM((G, size + 8, size), F32),
+            pltpu.VMEM((G, size, lags * size), BF16),
+            pltpu.VMEM((G, size, lags * size), BF16),
             pltpu.VMEM((3 * heads, size, E), BF16),
             pltpu.VMEM((heads, size, E), BF16),
         ],
         compiler_params=pltpu.CompilerParams(vmem_limit_bytes=48 << 20),
-        cost_estimate=pl.CostEstimate(
-            flops=flops, bytes_accessed=20 << 20, transcendentals=heads * seqs * size * size
-        ),
     )(seq_lengths, head_mix, base_rows, projected)
 
 
@@ -554,7 +556,7 @@
                 return carry
 
             lax.fori_loop(0, heads, build, 0)
-            pad[size : size + 8, :] = jnp.zeros((8, size), F32)
+            pad[:, size : size + 8, :] = jnp.zeros((G, 8, size), F32)
             dmix_ref[...] = jnp.zeros_like(dmix_ref)
 
         for n in range(3 * heads):
@@ -583,20 +585,20 @@
                 h = G * group + c
                 prob = p_ref[h, 0]
                 weighted = prob * d_probs[c]
-                pad[0:size, :] = weighted - prob * jnp.sum(weighted, axis=-1, keepdims=True)
+                pad[c, 0:size, :] = weighted - prob * jnp.sum(weighted, axis=-1, keepdims=True)
                 for a in range(lags):
-                    left[:, a * size : (a + 1) * size] = pad[a : a + size, :].astype(BF16)
-                d_masked = dot_nn(left[...], back_taps[h])
+                    left[c, :, a * size : (a + 1) * size] = pad[c, a : a + size, :].astype(BF16)
+                d_masked = dot_nn(left[c], back_taps[h])
                 raw = dot_nt(split[h], split[heads + h])
                 masked = jnp.where(allowed, raw * SCALE, 0.0).astype(BF16)
                 turned = dot_nn(masked, reverse).astype(BF16)
-                products[h] += dot_tn(turned, left[...])
+                products[h] += dot_tn(turned, left[c])
                 d_raw = jnp.where(allowed, d_masked * SCALE, 0.0).astype(BF16)
                 joined[h] = dot_nn(d_raw, split[heads + h]).astype(BF16)
                 joined[heads + h] = dot_tn(d_raw, split[h]).astype(BF16)
             return carry
 
-        lax.fori_loop(0, groups, group_step, 0)
+        lax.fori_loop(0, groups, group_step, 0, unroll=4)
         for n in range(3 * heads):
             dproj_ref[:, n * E : (n + 1) * E] = joined[n]
 
@@ -617,6 +619,7 @@
     flops = 2 * heads * seqs * size * size * ((2 * lags + 1) * size + 5 * E)
     d_projected, taps_rows, mix_rows = pl.pallas_call(
         kernel,
+        cost_estimate=FREE,
         grid=(seqs,),
         out_shape=(
             jax.ShapeDtypeStruct(projected.shape, BF16),
@@ -638,17 +641,14 @@
         ),
         scratch_shapes=[
             pltpu.VMEM((heads, lags * size, size), BF16),
-            pltpu.VMEM((size + 8, size), F32),
-            pltpu.VMEM((size, lags * size), BF16),
+            pltpu.VMEM((G, size + 8, size), F32),
+            pltpu.VMEM((G, size, lags * size), BF16),
             pltpu.VMEM((heads, size, lags * size), F32),
             pltpu.VMEM((3 * heads, size, E), BF16),
             pltpu.VMEM((heads, size, E), BF16),
             pltpu.VMEM((3 * heads, size, E), BF16),
         ],
         compiler_params=pltpu.CompilerParams(vmem_limit_bytes=52 << 20),
-        cost_estimate=pl.CostEstimate(
-            flops=flops, bytes_accessed=20 << 20, transcendentals=0
-        ),
     )(seq_lengths, head_mix, base_rows, projected, probs, d_context)
     shifts = 2 * reach + 1
     at = [(size - 1 - reach + b) % size for b in range(shifts)]
@@ -734,6 +734,7 @@
         grad_specs = (gateup_part, down_part)
     hidden, d_gate_up, gateup_grad, down_grad = pl.pallas_call(
         kernel,
+        cost_estimate=FREE,
         grid=(blocks,),
         out_shape=(
             jax.ShapeDtypeStruct((tokens, blocks * block), BF16),
@@ -748,11 +749,6 @@
         + grad_specs,
         scratch_shapes=[pltpu.VMEM((width, tokens), BF16)],
         compiler_params=pltpu.CompilerParams(vmem_limit_bytes=56 << 20),
-        cost_estimate=pl.CostEstimate(
-            flops=12 * tokens * width * blocks * block,
-            bytes_accessed=48 << 20,
-            transcendentals=tokens * blocks * block,
-        ),
     )(*seconds, *d_finals, gateup, down)
     if not packed:
         gateup_grad = gateup_grad.reshape(blocks, count, rows, 2 * block)
@@ -774,6 +770,7 @@
 
     return pl.pallas_call(
         kernel,
+        cost_estimate=FREE,
         grid=(count // part,),
         out_shape=jax.ShapeDtypeStruct((count, width), kind),
         in_specs=[
@@ -783,11 +780,6 @@
         + [pl.BlockSpec(memory_space=pl.ANY)] * len(needed),
         out_specs=pl.BlockSpec((part, width), lambda m: (m, 0)),
         compiler_params=pltpu.CompilerParams(vmem_limit_bytes=48 << 20),
-        cost_estimate=pl.CostEstimate(
-            flops=2 * count * width * blocks * columns,
-            bytes_accessed=16 << 20,
-            transcendentals=0,
-        ),
     )(d_gate_up, gateup, *needed)
 
 
@@ -826,6 +818,7 @@
     part = pl.BlockSpec((rows, 2 * block), lambda j: (j, 0))
     return pl.pallas_call(
         kernel,
+        cost_estimate=FREE,
         grid=(blocks,),
         out_shape=(jax.ShapeDtypeStruct((blocks * rows, 2 * block), BF16),) * 2,
         in_specs=[
@@ -875,6 +868,7 @@
     part = pl.BlockSpec((rows, 2 * block), lambda j: (j, 0))
     return pl.pallas_call(
         kernel,
+        cost_estimate=FREE,
         grid=(blocks,),
         out_shape=(jax.ShapeDtypeStruct(master.shape, F32),) * 3,
         in_specs=[pl.BlockSpec(memory_space=pltpu.SMEM)] + [whole] * 3 + [part] * 4,
@@ -1019,7 +1013,7 @@
 
     normed = jnp.concatenate([first_norm(inputs_own), first_norm(inputs_other)])
     d_final_own = cotangent.reshape(tokens, width)
-    d_final_beside = permute(when(d_final_own, qkv_full), x_pairs())
+    d_final_beside = permute(d_final_own, x_pairs())
     d_finals = [d_final_own, swap_cores(d_final_own), d_final_beside, swap_cores(d_final_beside)]
     all_tokens = cores * tokens
 
@@ -1030,20 +1024,19 @@
     if wide == BLOCK:
         ff_near = after(ff_lines[0], qkv_full)
         ff_near_across = ff_cross(ff_near)
-        ff_far = ff_lines[1](projected)
-        ff_far_across = ff_cross(ff_far)
     context_own, probs = attention_forward(
         projected, base_rows_of(taps_own, seq_len, False), mix_own, seq_lengths, lags, reach
     )
     if wide == BLOCK:
         context_own = after(context_own, ff_near_across, d_final_beside)
+        ff_far = ff_lines[1](context_own)
+        ff_far_across = ff_cross(ff_far)
         ff_arrays = (ff_near, ff_near_across, ff_far, ff_far_across)
     else:
         ff_arrays = (pair,)
     gateup_full, down_full = ff_end(ff_arrays, rows, units)
     context_mine = context_own[:tokens]
     context_theirs = swap_cores(context_own[tokens:])
-    context = by_core(context_mine, context_theirs, 1)
     middle = states + (
         matmul(context_mine, out_mine, ((1,), (0,)))
         + matmul(context_theirs, out_theirs, ((1,), (0,)))
@@ -1051,6 +1044,9 @@
     second_scale = rms_scale(middle)
     second_own = (middle * second_scale * gains_full[1]).astype(BF16)
     second_beside = permute(second_own, x_pairs())
+    context = by_core(context_mine, when(context_theirs, second_own), 1)
+    if wide == BLOCK:
+        second_beside = after(second_beside, ff_far_across)
     seconds = [second_own, swap_cores(second_own), second_beside, swap_cores(second_beside)]
 
     hidden, d_gate_up, gateup_grad, down_grad = feed_forward(

time: 726 us -> 699 us (0.963)
  Pallas kernels: 191 us -> 178 us
  waiting for transfers between devices: 161 us -> 149 us
    pallas_call x34 -> x35, Pallas kernels: 191 us -> 178 us  [the longest x1 50.4 us: feed_forward(): pl.pallas_call(kernel, cost_estimate=FREE, grid=(blocks,), out_shape=(jax...]
    ppermute x58, waiting for transfers between devices: 159 us -> 148 us  [permute(): return lax.ppermute(values, 'wide', pairs)]
    select_n x1, other arithmetic: 4.66 us -> 13.5 us  [by_core(): jnp.where(core == 0, jnp.concatenate([mine, other], axis=axis), jnp.conca...]
    unnamed x214 -> x221, local copies, waits for them, and re-layouts: 37 us -> 42.8 us
  transfers between devices with their start and end apart: 77 -> 77, of which waited for: 28 -> 24; matrix products, arithmetic and copies ran while one was open for 31% -> 30% of each run, Pallas kernels for 18% -> 17%
where the time goes in v3:
time: 699 us; the launch traced here: 689 us
  Pallas kernels  178 us (25%)
  waiting for transfers between devices  149 us (21%)
  other arithmetic  126 us (18%)
  starting transfers between devices  101 us (14%)
  local copies, waits for them, and re-layouts  68.7 us (10%)
  matrix products  63.2 us (9%)
    ppermute x58, waiting for transfers between devices, permute(): return lax.ppermute(values, 'wide', pairs)  148 us
    ppermute x58, starting transfers between devices, permute(): return lax.ppermute(values, 'wide', pairs)  97.7 us
    dot_general x10, matrix products, matmul(): lax.dot_general(a, b, (dims, ((), ())), preferred_element_type=F32)  63.2 us
    pallas_call x1, Pallas kernels, feed_forward(): pl.pallas_call(kernel, cost_estimate=FREE, grid=(blocks,), out_shape=(jax...  50.4 us
    unnamed x221, local copies, waits for them, and re-layouts  42.8 us
    convert_element_type x15, other arithmetic, fold(): return sum((term.astype(F32) for term in terms)).astype(BF16)  42.2 us
    pallas_call x1, Pallas kernels, attention_backward(): pl.pallas_call(kernel, cost_estimate=FREE, grid=(seqs,), out_shape=(jax.S...  39.6 us
    pallas_call x1, Pallas kernels, attention_forward(): pl.pallas_call(kernel, cost_estimate=FREE, grid=(seqs,), out_shape=(jax.S...  35.2 us
  transfers between devices with their start and end apart: 77, of which 24 were waited for; matrix products, arithmetic and copies ran while one was open for 30% of the time, Pallas kernels for 17%

profile of v3, /device:TPU:0, one launch (start us, length us, event | category | flops | bytes accessed | tf_op | source)
XLA Modules:
  0.0 688.9 jit_solution(7355711470653244292)
XLA Ops:
  17.1 7.8 %collective-permute-done.5 = bf16[96,3200]{1,0:T(8,128)(2,1)S(1)} collective-permute-done((bf16[96,3200]{1,0:T(8,128)(2,1)}, bf16[96,3200]{1,0:T(8,128)(2,1)S(1)}, u32[]{:S(2)}, u32[]{:S(2)}) %collective-permute-start.5) | collective-permute-done | bytes 614432 | tf_op jit(solution)/shard_map/ppermute | solution.py:27
  52.2 6.6 collective-permute-done.19
  60.0 9.5 %collective-permute-done.15 = bf16[96,3200]{1,0:T(8,128)(2,1)S(1)} collective-permute-done((bf16[96,3200]{1,0:T(8,128)(2,1)}, bf16[96,3200]{1,0:T(8,128)(2,1)S(1)}, u32[]{:S(2)}, u32[]{:S(2)}) %collective-permute-start.15) | collective-permute-done | bytes 614432 | tf_op jit(solution)/shard_map/ppermute | solution.py:27
  80.0 12.0 %collective-permute-done.3.refs_3_ = bf16[96,3200]{1,0:T(8,128)(2,1)S(1)} collective-permute-done((bf16[96,3200]{1,0:T(8,128)(2,1)S(1)}, bf16[96,3200]{1,0:T(8,128)(2,1)S(1)}, u32[]{:S(2)}, u32[]{:S(2)}) %collective-permute-start.3) | collective-permute-done | bytes 614432 | tf_op jit(solution)/shard_map/ppermute | solution.py:27
  110.2 11.8 %collective-permute-done.16.refs_13_ = bf16[96,3200]{1,0:T(8,128)(2,1)} collective-permute-done((bf16[96,3200]{1,0:T(8,128)(2,1)S(1)}, bf16[96,3200]{1,0:T(8,128)(2,1)}, u32[]{:S(2)}, u32[]{:S(2)}) %collective-permute-start.16) | collective-permute-done | bytes 614432 | tf_op jit(solution)/shard_map/ppermute | solution.py:27
  126.5 8.6 %collective-permute-done.14.refs_11_ = bf16[96,3200]{1,0:T(8,128)(2,1)S(1)} collective-permute-done((bf16[96,3200]{1,0:T(8,128)(2,1)}, bf16[96,3200]{1,0:T(8,128)(2,1)S(1)}, u32[]{:S(2)}, u32[]{:S(2)}) %collective-permute-start.14) | collective-permute-done | bytes 614432 | tf_op jit(solution)/shard_map/ppermute | solution.py:27
  137.5 7.7 %shard_map.413 = (bf16[4,4,96,2304]{3,2,1,0:T(8,128)(2,1)}, bf16[4,4,96,768]{3,2,1,0:T(8,128)(2,1)}, bf16[4,4,96,128]{3,2,1,0:T(8,128)(2,1)S(1)}) custom-call(s32[2]{0:T(128)S(1)} %pad_add_fusion.1.index_ref, bf16[96,3200]{1,0:T(8,128)(2,1)} %fusion.52.refs_0_, bf16[96,3200]{1,0:T(8,128)(2,1)S(1)} %copy-done.11, bf16[96,3200]{1,0:T(8,128)(2,1)S(1)} %copy-done.13, ...), custom_call_target="tpu_custom_call" | custom-call | flops 1 | bytes 1 | tf_op jit(solution)/shard_map/pallas_call | solution.py:158
  153.6 13.4 %convolution_convert_fusion.1.proj_ref = bf16[1024,2304]{1,0:T(8,128)(2,1)} fusion(bf16[1536,2304]{1,0:T(8,128)(2,1)} %bitcast.276, bf16[512,1536]{1,0:T(8,128)(2,1)S(1)} %get-tuple-element.231, bf16[512,1536]{1,0:T(8,128)(2,1)S(1)} %get-tuple-element.230), kind=kOutput, calls=%fused_computation.2 | convolution fusion | flops 7256408064 | bytes 14942208 | tf_op jit(solution)/shard_map/dot_general | solution.py:895
  167.0 35.2 %shard_map.414 = (bf16[1024,768]{1,0:T(8,128)(2,1)S(1)}, f32[8,4,256,256]{3,2,1,0:T(8,128)}) custom-call(s32[4]{0:T(128)S(1)} %pad_add_fusion.len_ref, f32[8,2]{1,0:T(8,128)S(1)} %copy.237.mix_ref, f32[8,8,256]{2,1,0:T(8,128)S(1)} %pad.11.base_ref, bf16[1024,2304]{1,0:T(8,128)(2,1)} %convolution_convert_fusion.1.proj_ref), custom_call_target="tpu_custom_call" | custom-call | flops 1 | bytes 1 | tf_op jit(solution)/shard_map/pallas_call | solution.py:498
  214.2 13.5 %maximum_select_fusion = bf16[2,768,1536]{2,1,0:T(8,128)(2,1)S(1)} fusion(bf16[2,768,768]{2,1,0:T(8,128)(2,1)} %bitcast.25, bf16[2,768,768]{2,1,0:T(8,128)(2,1)S(1)} %bitcast.283, pred[]{:T(512)S(6)} %eq.58), kind=kLoop, calls=%fused_computation.3 | loop fusion | flops 21233664 | bytes 9437185 | tf_op jit(solution)/shard_map/jit(_where)/select_n | solution.py:946
  236.8 35.3 %collective-permute-done.30.refs_0_ = bf16[512,1536]{1,0:T(8,128)(2,1)} collective-permute-done((bf16[512,1536]{1,0:T(8,128)(2,1)}, bf16[512,1536]{1,0:T(8,128)(2,1)}, u32[]{:S(2)}, u32[]{:S(2)}) %collective-permute-start.30) | collective-permute-done | bytes 1572896 | tf_op jit(solution)/shard_map/ppermute | solution.py:27
  273.8 12.0 %shard_map.420 = (bf16[4,1536,512]{2,1,0:T(8,128)(2,1)}, bf16[1024,1536]{1,0:T(8,128)(2,1)}) custom-call(s32[2]{0:T(128)S(1)} %pad_add_fusion.2.index_ref, bf16[2,2,576,512]{3,2,1,0:T(8,128)(2,1)S(1)} %copy-done.5, bf16[2,2,576,512]{3,2,1,0:T(8,128)(2,1)S(1)} %copy-done.9, bf16[2,2,576,512]{3,2,1,0:T(8,128)(2,1)} %copy-done.36, ...), custom_call_target="tpu_custom_call" | custom-call | flops 1 | bytes 1 | tf_op jit(solution)/shard_map/pallas_call | solution.py:330
  285.9 50.4 %shard_map.421 = (bf16[2048,1024]{1,0:T(8,128)(2,1)}, bf16[2048,2048]{1,0:T(8,128)(2,1)}, bf16[16,384,512]{2,1,0:T(8,128)(2,1)}, bf16[16,192,512]{2,1,0:T(8,128)(2,1)}) custom-call(bf16[512,1536]{1,0:T(8,128)(2,1)} %multiply_convert_fusion.refs_0_.refs_1_, bf16[512,1536]{1,0:T(8,128)(2,1)} %collective-permute-done.29.refs_1_, ...), custom_call_target="tpu_custom_call" | custom-call | flops 1 | bytes 1 | tf_op jit(solution)/shard_map/pallas_call | solution.py:735
  336.3 10.9 %shard_map.422 = bf16[1024,1536]{1,0:T(8,128)(2,1)S(1)} custom-call(bf16[2048,2048]{1,0:T(8,128)(2,1)} %get-tuple-element.52.d_ref, bf16[4,1536,512]{2,1,0:T(8,128)(2,1)} %get-tuple-element.48.refs_8_.gu_ref), custom_call_target="tpu_custom_call" | custom-call | flops 1 | bytes 1 | tf_op jit(solution)/shard_map/pallas_call | solution.py:771
  366.7 11.6 %shard_map.426 = f32[1024,1536]{1,0:T(8,128)} custom-call(bf16[2048,2048]{1,0:T(8,128)(2,1)} %get-tuple-element.52.d_ref, bf16[4,1536,512]{2,1,0:T(8,128)(2,1)} %get-tuple-element.48.refs_8_.gu_ref, bf16[2,2,576,512]{3,2,1,0:T(8,128)(2,1)} %pad_maximum_fusion.3.refs_1_.refs_0_, bf16[2,2,576,512]{3,2,1,0:T(8,128)(2,1)S(1)} %pad_maximum_fusion.4.refs_2_.refs_1_), custom_call_target="tpu_custom_call" | custom-call | flops 1 | bytes 1 | tf_op jit(solution)/shard_map/pallas_call | solution.py:771
  383.4 11.4 %fusion.75 = (bf16[2048,1536]{1,0:T(8,128)(2,1)S(1)}, f32[2048,1536]{1,0:T(8,128)}) fusion(bf16[2048,1024]{1,0:T(8,128)(2,1)} %shard_map.425, bf16[1024,1536]{1,0:T(8,128)(2,1)S(1)} %copy-done.54), kind=kOutput, calls=%fused_computation.218 | convolution fusion | flops 6445596672 | bytes 26214400 | tf_op jit(solution)/shard_map/dot_general | solution.py:895
  424.8 8.0 %collective-permute-start.45 = (bf16[2,576,512]{2,1,0:T(8,128)(2,1)}, bf16[2,576,512]{2,1,0:T(8,128)(2,1)}, u32[]{:S(2)}, u32[]{:S(2)}) collective-permute-start(bf16[2,576,512]{2,1,0:T(8,128)(2,1)} %select_bitcast_fusion), channel_id=1, source_target_pairs={{0,4},{1,5},{2,6},{3,7},{16,20},{17,21},{18,22},{19,23}} | collective-permute-start | bytes 3538952 | tf_op jit(solution)/shard_map/ppermute | solution.py:27
  446.1 39.6 %shard_map.432 = (bf16[1024,2304]{1,0:T(8,128)(2,1)}, f32[8,8,256]{2,1,0:T(8,128)S(1)}, f32[4,8,256]{2,1,0:T(8,128)S(1)}) custom-call(s32[4]{0:T(128)S(1)} %pad_add_fusion.len_ref, f32[8,2]{1,0:T(8,128)S(1)} %copy.237.mix_ref, f32[8,8,256]{2,1,0:T(8,128)S(1)} %pad.13.base_ref, bf16[1024,2304]{1,0:T(8,128)(2,1)} %convolution_convert_fusion.1.proj_ref, ...), custom_call_target="tpu_custom_call" | custom-call | flops 1 | bytes 1 | tf_op jit(solution)/shard_map/pallas_call | solution.py:620
  487.4 10.8 %convolution_convert_fusion = bf16[1536,2304]{1,0:T(8,128)(2,1)S(1)} fusion(bf16[1024,2304]{1,0:T(8,128)(2,1)} %shard_map.433.refs_0_, bf16[512,1536]{1,0:T(8,128)(2,1)} %copy-done.61, bf16[512,1536]{1,0:T(8,128)(2,1)} %copy-done.60), kind=kOutput, calls=%fused_computation.1 | convolution fusion | flops 7257587712 | bytes 14942208 | tf_op jit(solution)/shard_map/dot_general | solution.py:895
  520.2 11.4 %fusion.76.refs_0_ = f32[1024,1536]{1,0:T(8,128)} fusion(bf16[1024,2304]{1,0:T(8,128)(2,1)S(1)} %copy-done.28, bf16[1536,2304]{1,0:T(8,128)(2,1)} %bitcast.277), kind=kOutput, calls=%fused_computation.219 | convolution fusion | flops 7247757312 | bytes 18087936 | tf_op jit(solution)/shard_map/dot_general | solution.py:895
  554.0 6.8 collective-permute-done.67
  573.0 17.0 %collective-permute-done.61 = bf16[2,576,512]{2,1,0:T(8,128)(2,1)S(1)} collective-permute-done((bf16[2,576,512]{2,1,0:T(8,128)(2,1)S(1)}, bf16[2,576,512]{2,1,0:T(8,128)(2,1)S(1)}, u32[]{:S(2)}, u32[]{:S(2)}) %collective-permute-start.61) | collective-permute-done | bytes 1179680 | tf_op jit(solution)/shard_map/ppermute | solution.py:27
  639.0 7.7 %shard_map.440 = (f32[96,2,4096]{2,1,0:T(2,128)}, f32[96,2,4096]{2,1,0:T(2,128)}, f32[96,2,4096]{2,1,0:T(2,128)}) custom-call(s32[1]{0:T(128)} %bitcast.10.quarter_ref, f32[96,2,4096]{2,1,0:T(2,128)S(1)} %copy-done.7, f32[96,2,4096]{2,1,0:T(2,128)S(1)} %copy-done.15, f32[96,2,4096]{2,1,0:T(2,128)S(1)} %copy-done.16, ...), custom_call_target="tpu_custom_call" | custom-call | flops 1 | bytes 1 | tf_op jit(solution)/shard_map/pallas_call | solution.py:869
  666.2 8.1 %fusion.9 = (bf16[512,1536]{1,0:T(8,128)(2,1)}, bf16[512,1536]{1,0:T(8,128)(2,1)}) fusion(f32[512]{0:T(512)S(1)} %broadcast_multiply_fusion, f32[1536]{0:T(1024)S(1)} %copy-done.82, f32[512]{0:T(512)S(1)} %bitcast.300, bf16[2,1,256,1536]{3,2,1,0:T(8,128)(2,1)} %param.24, f32[512,1536]{1,0:T(8,128)} %collective-permute-done.50, f32[1024,1536]{1,0:T(8,128)} %shard_map.437, ...), kind=kLoop, calls=%fused_computation.23 | loop fusion | flops 17301504 | bytes 25186304 | tf_op jit(solution)/shard_map/convert_element_type | solution.py:1126
  (535 shorter events, 319.0 us)
Async XLA Ops:
  51.7 41.1 %collective-permute-start.24 = (bf16[512,1536]{1,0:T(8,128)(2,1)}, bf16[512,1536]{1,0:T(8,128)(2,1)}, u32[]{:S(2)}, u32[]{:S(2)}) collective-permute-start(bf16[512,1536]{1,0:T(8,128)(2,1)} %bitcast), channel_id=1, source_target_pairs={{0,16},{16,0},{1,17},{17,1},{2,18},{18,2},{3,19},{19,3},{4,20},{20... | collective-permute-start | bytes 4718600 | tf_op jit(solution)/shard_map/ppermute | solution.py:31
  96.1 38.9 %collective-permute-start.21 = (bf16[2,576,512]{2,1,0:T(8,128)(2,1)}, bf16[2,576,512]{2,1,0:T(8,128)(2,1)S(1)}, u32[]{:S(2)}, u32[]{:S(2)}) collective-permute-start(bf16[2,576,512]{2,1,0:T(8,128)(2,1)} %collective-permute-done.20), channel_id=1, source_target_pairs={{4,8},{5,9},{6,10},{7,11},{8,12},{9,13},{10,14},{11,15},{20,24},{2... | collective-permute-start | bytes 3538952 | tf_op jit(solution)/shard_map/ppermute | solution.py:27
  125.7 77.7 %collective-permute-start.26 = (bf16[512,1536]{1,0:T(8,128)(2,1)}, bf16[512,1536]{1,0:T(8,128)(2,1)}, u32[]{:S(2)}, u32[]{:S(2)}) collective-permute-start(bf16[512,1536]{1,0:T(8,128)(2,1)} %bitcast.22.refs_4_), channel_id=1, source_target_pairs={{0,1},{1,0},{2,3},{3,2},{4,5},{5,4},{6,7},{7,6},{8,9},{9,8},{10,11... | collective-permute-start | bytes 4718600 | tf_op jit(solution)/shard_map/ppermute | solution.py:27
  145.6 57.7 %collective-permute-start.25 = (bf16[2,2,576,512]{3,2,1,0:T(8,128)(2,1)}, bf16[2,2,576,512]{3,2,1,0:T(8,128)(2,1)S(1)}, u32[]{:S(2)}, u32[]{:S(2)}) collective-permute-start(bf16[2,2,576,512]{3,2,1,0:T(8,128)(2,1)} %shard_map.415.refs_0_), channel_id=1, source_target_pairs={{0,2},{1,3},{2,0},{3,1},{4,6},{5,7},{6,4},{7,5},{8,10},{9,11},{10,... | collective-permute-start | bytes 7077896 | tf_op jit(solution)/shard_map/ppermute | solution.py:27
  146.2 67.3 %collective-permute-start.27 = (bf16[1536,768]{1,0:T(8,128)(2,1)}, bf16[1536,768]{1,0:T(8,128)(2,1)}, u32[]{:S(2)}, u32[]{:S(2)}) collective-permute-start(bf16[1536,768]{1,0:T(8,128)(2,1)} %bitcast.282), channel_id=1, source_target_pairs={{0,16},{16,0},{1,17},{17,1},{2,18},{18,2},{3,19},{19,3},{4,20},{20... | collective-permute-start | bytes 7077896 | tf_op jit(solution)/shard_map/ppermute | solution.py:31
  146.2 61.7 %collective-permute-start.31 = (bf16[2,576,512]{2,1,0:T(8,128)(2,1)}, bf16[2,576,512]{2,1,0:T(8,128)(2,1)}, u32[]{:S(2)}, u32[]{:S(2)}) collective-permute-start(bf16[2,576,512]{2,1,0:T(8,128)(2,1)} %copy-done.45), channel_id=1, source_target_pairs={{8,12},{9,13},{10,14},{11,15},{24,28},{25,29},{26,30},{27,31}} | collective-permute-start | bytes 3538952 | tf_op jit(solution)/shard_map/ppermute | solution.py:27
  148.0 59.9 %collective-permute-start.32 = (bf16[2,576,512]{2,1,0:T(8,128)(2,1)}, bf16[2,576,512]{2,1,0:T(8,128)(2,1)}, u32[]{:S(2)}, u32[]{:S(2)}) collective-permute-start(bf16[2,576,512]{2,1,0:T(8,128)(2,1)} %copy-done.47), channel_id=1, source_target_pairs={{4,0},{5,1},{6,2},{7,3},{20,16},{21,17},{22,18},{23,19}} | collective-permute-start | bytes 3538952 | tf_op jit(solution)/shard_map/ppermute | solution.py:27
  211.9 60.2 %collective-permute-start.33 = (bf16[2,2,576,512]{3,2,1,0:T(8,128)(2,1)S(1)}, bf16[2,2,576,512]{3,2,1,0:T(8,128)(2,1)}, u32[]{:S(2)}, u32[]{:S(2)}) collective-permute-start(bf16[2,2,576,512]{3,2,1,0:T(8,128)(2,1)S(1)} %pad_maximum_fusion.2.refs_2_), channel_id=1, source_target_pairs={{0,2},{1,3},{2,0},{3,1},{4,6},{5,7},{6,4},{7,5},{8,10},{9,11},{10,... | collective-permute-start | bytes 7077896 | tf_op jit(solution)/shard_map/ppermute | solution.py:27
  236.3 49.5 %collective-permute-start.35 = (bf16[512,1536]{1,0:T(8,128)(2,1)}, bf16[512,1536]{1,0:T(8,128)(2,1)}, u32[]{:S(2)}, u32[]{:S(2)}) collective-permute-start(bf16[512,1536]{1,0:T(8,128)(2,1)} %bitcast.22.refs_4_), channel_id=1, source_target_pairs={{0,16},{16,0},{1,17},{17,1},{2,18},{18,2},{3,19},{19,3},{4,20},{20... | collective-permute-start | bytes 4718600 | tf_op jit(solution)/shard_map/ppermute | solution.py:31
  236.3 49.5 %collective-permute-start.36 = (bf16[512,1536]{1,0:T(8,128)(2,1)}, bf16[512,1536]{1,0:T(8,128)(2,1)}, u32[]{:S(2)}, u32[]{:S(2)}) collective-permute-start(bf16[512,1536]{1,0:T(8,128)(2,1)} %collective-permute-done.26.refs_2_.refs_6_), channel_id=1, source_target_pairs={{0,16},{16,0},{1,17},{17,1},{2,18},{18,2},{3,19},{19,3},{4,20},{20... | collective-permute-start | bytes 4718600 | tf_op jit(solution)/shard_map/ppermute | solution.py:31
  236.8 49.0 %collective-permute-start.29 = (bf16[512,1536]{1,0:T(8,128)(2,1)}, bf16[512,1536]{1,0:T(8,128)(2,1)}, u32[]{:S(2)}, u32[]{:S(2)}) collective-permute-start(bf16[512,1536]{1,0:T(8,128)(2,1)} %multiply_convert_fusion.refs_0_.refs_1_), channel_id=1, source_target_pairs={{0,16},{16,0},{1,17},{17,1},{2,18},{18,2},{3,19},{19,3},{4,20},{20... | collective-permute-start | bytes 4718600 | tf_op jit(solution)/shard_map/ppermute | solution.py:31
  355.2 46.4 %collective-permute-start.41 = (bf16[512,1536]{1,0:T(8,128)(2,1)}, bf16[512,1536]{1,0:T(8,128)(2,1)}, u32[]{:S(2)}, u32[]{:S(2)}) collective-permute-start(bf16[512,1536]{1,0:T(8,128)(2,1)} %add_convert_fusion.3.refs_1_), channel_id=1, source_target_pairs={{0,1},{1,0},{2,3},{3,2},{4,5},{5,4},{6,7},{7,6},{8,9},{9,8},{10,11... | collective-permute-start | bytes 4718600 | tf_op jit(solution)/shard_map/ppermute | solution.py:27
  365.1 55.9 %collective-permute-start.44 = (bf16[2,2,576,512]{3,2,1,0:T(8,128)(2,1)}, bf16[2,2,576,512]{3,2,1,0:T(8,128)(2,1)}, u32[]{:S(2)}, u32[]{:S(2)}) collective-permute-start(bf16[2,2,576,512]{3,2,1,0:T(8,128)(2,1)} %pad_maximum_fusion.3.refs_1_.refs_0_), channel_id=1, source_target_pairs={{0,2},{1,3},{2,0},{3,1},{4,6},{5,7},{6,4},{7,5},{8,10},{9,11},{10,... | collective-permute-start | bytes 7077896 | tf_op jit(solution)/shard_map/ppermute | solution.py:27
  419.7 67.7 %collective-permute-start.42 = (bf16[512,1536]{1,0:T(8,128)(2,1)}, bf16[512,1536]{1,0:T(8,128)(2,1)}, u32[]{:S(2)}, u32[]{:S(2)}) collective-permute-start(bf16[512,1536]{1,0:T(8,128)(2,1)} %shard_map.428), channel_id=1, source_target_pairs={{0,1},{1,0},{2,3},{3,2},{4,5},{5,4},{6,7},{7,6},{8,9},{9,8},{10,11... | collective-permute-start | bytes 4718600 | tf_op jit(solution)/shard_map/ppermute | solution.py:27
  424.8 62.6 %collective-permute-start.45 = (bf16[2,576,512]{2,1,0:T(8,128)(2,1)}, bf16[2,576,512]{2,1,0:T(8,128)(2,1)}, u32[]{:S(2)}, u32[]{:S(2)}) collective-permute-start(bf16[2,576,512]{2,1,0:T(8,128)(2,1)} %select_bitcast_fusion), channel_id=1, source_target_pairs={{0,4},{1,5},{2,6},{3,7},{16,20},{17,21},{18,22},{19,23}} | collective-permute-start | bytes 3538952 | tf_op jit(solution)/shard_map/ppermute | solution.py:27
  432.8 54.6 %collective-permute-start.46 = (bf16[2,576,512]{2,1,0:T(8,128)(2,1)}, bf16[2,576,512]{2,1,0:T(8,128)(2,1)}, u32[]{:S(2)}, u32[]{:S(2)}) collective-permute-start(bf16[2,576,512]{2,1,0:T(8,128)(2,1)} %select_bitcast_fusion), channel_id=1, source_target_pairs={{12,8},{13,9},{14,10},{15,11},{28,24},{29,25},{30,26},{31,27}} | collective-permute-start | bytes 3538952 | tf_op jit(solution)/shard_map/ppermute | solution.py:27
  444.0 87.7 %collective-permute-start.59 = (bf16[2,2,576,512]{3,2,1,0:T(8,128)(2,1)S(1)}, bf16[2,2,576,512]{3,2,1,0:T(8,128)(2,1)}, u32[]{:S(2)}, u32[]{:S(2)}) collective-permute-start(bf16[2,2,576,512]{3,2,1,0:T(8,128)(2,1)S(1)} %copy-done.4), channel_id=1, source_target_pairs={{0,2},{1,3},{2,0},{3,1},{4,6},{5,7},{6,4},{7,5},{8,10},{9,11},{10,... | collective-permute-start | bytes 7077896 | tf_op jit(solution)/shard_map/ppermute | solution.py:27
  444.7 55.3 %collective-permute-start.47 = (bf16[1536,768]{1,0:T(8,128)(2,1)}, bf16[1536,768]{1,0:T(8,128)(2,1)}, u32[]{:S(2)}, u32[]{:S(2)}) collective-permute-start(bf16[1536,768]{1,0:T(8,128)(2,1)} %convolution_convert_fusion.3.refs_1_), channel_id=1, source_target_pairs={{0,16},{16,0},{1,17},{17,1},{2,18},{18,2},{3,19},{19,3},{4,20},{20... | collective-permute-start | bytes 7077896 | tf_op jit(solution)/shard_map/ppermute | solution.py:31
  510.1 37.8 %collective-permute-start.62 = (bf16[2,96,3072]{2,1,0:T(8,128)(2,1)}, bf16[2,96,3072]{2,1,0:T(8,128)(2,1)}, u32[]{:S(2)}, u32[]{:S(2)}) collective-permute-start(bf16[2,96,3072]{2,1,0:T(8,128)(2,1)} %pad_maximum_fusion.9.refs_2_), channel_id=1, source_target_pairs={{0,1},{1,0},{2,3},{3,2},{4,5},{5,4},{6,7},{7,6},{8,9},{9,8},{10,11... | collective-permute-start | bytes 3538952 | tf_op jit(solution)/shard_map/ppermute | solution.py:27
  543.4 56.1 %collective-permute-start.58 = (bf16[2,96,3072]{2,1,0:T(8,128)(2,1)S(1)}, bf16[2,96,3072]{2,1,0:T(8,128)(2,1)}, u32[]{:S(2)}, u32[]{:S(2)}) collective-permute-start(bf16[2,96,3072]{2,1,0:T(8,128)(2,1)S(1)} %copy-done.26), channel_id=1, source_target_pairs={{0,1},{1,0},{2,3},{3,2},{4,5},{5,4},{6,7},{7,6},{8,9},{9,8},{10,11... | collective-permute-start | bytes 3538952 | tf_op jit(solution)/shard_map/ppermute | solution.py:27
  547.9 72.4 %collective-permute-start.50 = (f32[512,1536]{1,0:T(8,128)}, f32[512,1536]{1,0:T(8,128)}, u32[]{:S(2)}, u32[]{:S(2)}) collective-permute-start(f32[512,1536]{1,0:T(8,128)} %slice.265), channel_id=1, source_target_pairs={{0,16},{16,0},{1,17},{17,1},{2,18},{18,2},{3,19},{19,3},{4,20},{20... | collective-permute-start | bytes 9437192 | tf_op jit(solution)/shard_map/ppermute | solution.py:31
  550.6 50.3 %collective-permute-start.63 = (bf16[2,96,3072]{2,1,0:T(8,128)(2,1)}, bf16[2,96,3072]{2,1,0:T(8,128)(2,1)}, u32[]{:S(2)}, u32[]{:S(2)}) collective-permute-start(bf16[2,96,3072]{2,1,0:T(8,128)(2,1)} %add_convert_fusion.7), channel_id=1, source_target_pairs={{0,2},{1,3},{2,0},{3,1},{4,6},{5,7},{6,4},{7,5},{8,10},{9,11},{10,... | collective-permute-start | bytes 3538952 | tf_op jit(solution)/shard_map/ppermute | solution.py:27
  590.0 76.2 %collective-permute-start.38 = (bf16[512,1536]{1,0:T(8,128)(2,1)}, bf16[512,1536]{1,0:T(8,128)(2,1)}, u32[]{:S(2)}, u32[]{:S(2)}) collective-permute-start(bf16[512,1536]{1,0:T(8,128)(2,1)} %get-tuple-element.189), channel_id=1, source_target_pairs={{0,16},{16,0},{1,17},{17,1},{2,18},{18,2},{3,19},{19,3},{4,20},{20... | collective-permute-start | bytes 4718600 | tf_op jit(solution)/shard_map/ppermute | solution.py:31
  610.3 45.4 %collective-permute-start.71 = (bf16[96,3072]{1,0:T(8,128)(2,1)}, bf16[96,3072]{1,0:T(8,128)(2,1)}, u32[]{:S(2)}, u32[]{:S(2)}) collective-permute-start(bf16[96,3072]{1,0:T(8,128)(2,1)} %get-tuple-element.217), channel_id=1, source_target_pairs={{0,4},{1,5},{2,6},{3,7},{4,8},{5,9},{6,10},{7,11},{16,20},{17,21},... | collective-permute-start | bytes 1769480 | tf_op jit(solution)/shard_map/ppermute | solution.py:27
  (157 other events, 1686.1 us)

commit v4 on v3

--- a/solution.py
+++ b/solution.py
@@ -300,11 +300,12 @@
     index = jnp.stack([me // 8, (me // 2) % 2]).astype(jnp.int32)
 
     def assemble(index_ref, *refs):
-        gateup_ref, down_ref, sems = refs[len(arrays) :]
-        copies = []
-
-        def copy(source, target):
-            copies.append(pltpu.make_async_copy(source, target, sems.at[len(copies)]))
+        gateup_out, down_out, gateup_ref, down_ref, sems, out_sems = refs[len(arrays) :]
+        groups = [[] for _ in range(blocks + 1)]
+
+        def copy(group, source, target):
+            number = sum(len(known) for known in groups)
+            groups[group].append(pltpu.make_async_copy(source, target, sems.at[number]))
 
         for n in range(len(arrays)):
             half, lane = n // 2, n % 2
@@ -315,17 +316,27 @@
                     source = refs[n].at[z, x]
                     for j in range(blocks):
                         target = gateup_ref.at[j, pl.ds(pl.multiple_of(at * rows, 16), rows)]
-                        copy(source.at[pl.ds(j * rows, rows)], target)
+                        copy(j, source.at[pl.ds(j * rows, rows)], target)
                     for i in range(cols):
                         target = down_ref.at[
                             pl.ds(pl.multiple_of(at * units, 16), units),
                             pl.ds(i * columns, columns),
                         ]
-                        copy(source.at[pl.ds(blocks * rows + i * units, units)], target)
-        for started in copies:
-            started.start()
-        for started in copies:
-            started.wait()
+                        copy(blocks, source.at[pl.ds(blocks * rows + i * units, units)], target)
+        for group in groups:
+            for started in group:
+                started.start()
+        outs = [
+            pltpu.make_async_copy(gateup_ref.at[j], gateup_out.at[j], out_sems.at[j])
+            for j in range(blocks)
+        ]
+        outs.append(pltpu.make_async_copy(down_ref, down_out, out_sems.at[blocks]))
+        for group, out in zip(groups, outs):
+            for started in group:
+                started.wait()
+            out.start()
+        for out in outs:
+            out.wait()
 
     return pl.pallas_call(
         assemble,
@@ -336,8 +347,13 @@
         ),
         in_specs=[pl.BlockSpec(memory_space=pltpu.SMEM)]
         + [pl.BlockSpec(memory_space=pl.ANY)] * len(arrays),
-        out_specs=(pl.BlockSpec(memory_space=pltpu.VMEM),) * 2,
-        scratch_shapes=[pltpu.SemaphoreType.DMA((len(arrays) * 4 * (blocks + cols),))],
+        out_specs=(pl.BlockSpec(memory_space=pl.ANY),) * 2,
+        scratch_shapes=[
+            pltpu.VMEM(gateup_shape, BF16),
+            pltpu.VMEM(down_shape, BF16),
+            pltpu.SemaphoreType.DMA((len(arrays) * 4 * (blocks + cols),)),
+            pltpu.SemaphoreType.DMA((blocks + 1,)),
+        ],
         compiler_params=pltpu.CompilerParams(vmem_limit_bytes=48 << 20),
     )(index, *arrays)
 

time: 699 us -> 697 us (level)
  transfers between devices with their start and end apart: 77 -> 77, of which waited for: 24 -> 24; matrix products, arithmetic and copies ran while one was open for 30% -> 31% of each run, Pallas kernels for 17% -> 17%
where the time goes in v4:
time: 697 us; the launch traced here: 687 us
  Pallas kernels  177 us (25%)
  waiting for transfers between devices  149 us (21%)
  other arithmetic  126 us (18%)
  starting transfers between devices  101 us (14%)
  local copies, waits for them, and re-layouts  68.7 us (10%)
  matrix products  63.2 us (9%)
    ppermute x58, waiting for transfers between devices, permute(): return lax.ppermute(values, 'wide', pairs)  148 us
    ppermute x58, starting transfers between devices, permute(): return lax.ppermute(values, 'wide', pairs)  97.6 us
    dot_general x10, matrix products, matmul(): lax.dot_general(a, b, (dims, ((), ())), preferred_element_type=F32)  63.2 us
    pallas_call x1, Pallas kernels, feed_forward(): pl.pallas_call(kernel, cost_estimate=FREE, grid=(blocks,), out_shape=(jax...  50.4 us
    unnamed x221, local copies, waits for them, and re-layouts  42.8 us
    convert_element_type x15, other arithmetic, fold(): return sum((term.astype(F32) for term in terms)).astype(BF16)  42.2 us
    pallas_call x1, Pallas kernels, attention_backward(): pl.pallas_call(kernel, cost_estimate=FREE, grid=(seqs,), out_shape=(jax.S...  39.6 us
    pallas_call x1, Pallas kernels, attention_forward(): pl.pallas_call(kernel, cost_estimate=FREE, grid=(seqs,), out_shape=(jax.S...  35.2 us
  transfers between devices with their start and end apart: 77, of which 24 were waited for; matrix products, arithmetic and copies ran while one was open for 31% of the time, Pallas kernels for 17%

profile of v4, /device:TPU:0, one launch (start us, length us, event | category | flops | bytes accessed | tf_op | source)
XLA Modules:
  0.0 687.1 jit_solution(11305059922775843697)
XLA Ops:
  17.1 7.8 %collective-permute-done.5 = bf16[96,3200]{1,0:T(8,128)(2,1)S(1)} collective-permute-done((bf16[96,3200]{1,0:T(8,128)(2,1)}, bf16[96,3200]{1,0:T(8,128)(2,1)S(1)}, u32[]{:S(2)}, u32[]{:S(2)}) %collective-permute-start.5) | collective-permute-done | bytes 614432 | tf_op jit(solution)/shard_map/ppermute | solution.py:27
  52.2 6.6 collective-permute-done.19
  60.0 9.5 %collective-permute-done.15 = bf16[96,3200]{1,0:T(8,128)(2,1)S(1)} collective-permute-done((bf16[96,3200]{1,0:T(8,128)(2,1)}, bf16[96,3200]{1,0:T(8,128)(2,1)S(1)}, u32[]{:S(2)}, u32[]{:S(2)}) %collective-permute-start.15) | collective-permute-done | bytes 614432 | tf_op jit(solution)/shard_map/ppermute | solution.py:27
  80.0 12.0 %collective-permute-done.3.refs_3_ = bf16[96,3200]{1,0:T(8,128)(2,1)S(1)} collective-permute-done((bf16[96,3200]{1,0:T(8,128)(2,1)S(1)}, bf16[96,3200]{1,0:T(8,128)(2,1)S(1)}, u32[]{:S(2)}, u32[]{:S(2)}) %collective-permute-start.3) | collective-permute-done | bytes 614432 | tf_op jit(solution)/shard_map/ppermute | solution.py:27
  110.2 11.8 %collective-permute-done.16.refs_13_ = bf16[96,3200]{1,0:T(8,128)(2,1)} collective-permute-done((bf16[96,3200]{1,0:T(8,128)(2,1)S(1)}, bf16[96,3200]{1,0:T(8,128)(2,1)}, u32[]{:S(2)}, u32[]{:S(2)}) %collective-permute-start.16) | collective-permute-done | bytes 614432 | tf_op jit(solution)/shard_map/ppermute | solution.py:27
  126.5 8.6 %collective-permute-done.14.refs_11_ = bf16[96,3200]{1,0:T(8,128)(2,1)S(1)} collective-permute-done((bf16[96,3200]{1,0:T(8,128)(2,1)}, bf16[96,3200]{1,0:T(8,128)(2,1)S(1)}, u32[]{:S(2)}, u32[]{:S(2)}) %collective-permute-start.14) | collective-permute-done | bytes 614432 | tf_op jit(solution)/shard_map/ppermute | solution.py:27
  137.5 7.7 %shard_map.413 = (bf16[4,4,96,2304]{3,2,1,0:T(8,128)(2,1)}, bf16[4,4,96,768]{3,2,1,0:T(8,128)(2,1)}, bf16[4,4,96,128]{3,2,1,0:T(8,128)(2,1)S(1)}) custom-call(s32[2]{0:T(128)S(1)} %pad_add_fusion.1.index_ref, bf16[96,3200]{1,0:T(8,128)(2,1)} %fusion.52.refs_0_, bf16[96,3200]{1,0:T(8,128)(2,1)S(1)} %copy-done.11, bf16[96,3200]{1,0:T(8,128)(2,1)S(1)} %copy-done.13, ...), custom_call_target="tpu_custom_call" | custom-call | flops 1 | bytes 1 | tf_op jit(solution)/shard_map/pallas_call | solution.py:158
  153.6 13.4 %convolution_convert_fusion.1.proj_ref = bf16[1024,2304]{1,0:T(8,128)(2,1)} fusion(bf16[1536,2304]{1,0:T(8,128)(2,1)} %bitcast.276, bf16[512,1536]{1,0:T(8,128)(2,1)S(1)} %get-tuple-element.231, bf16[512,1536]{1,0:T(8,128)(2,1)S(1)} %get-tuple-element.230), kind=kOutput, calls=%fused_computation.2 | convolution fusion | flops 7256408064 | bytes 14942208 | tf_op jit(solution)/shard_map/dot_general | solution.py:911
  167.0 35.2 %shard_map.414 = (bf16[1024,768]{1,0:T(8,128)(2,1)S(1)}, f32[8,4,256,256]{3,2,1,0:T(8,128)}) custom-call(s32[4]{0:T(128)S(1)} %pad_add_fusion.len_ref, f32[8,2]{1,0:T(8,128)S(1)} %copy.237.mix_ref, f32[8,8,256]{2,1,0:T(8,128)S(1)} %pad.11.base_ref, bf16[1024,2304]{1,0:T(8,128)(2,1)} %convolution_convert_fusion.1.proj_ref), custom_call_target="tpu_custom_call" | custom-call | flops 1 | bytes 1 | tf_op jit(solution)/shard_map/pallas_call | solution.py:514
  214.2 13.5 %maximum_select_fusion = bf16[2,768,1536]{2,1,0:T(8,128)(2,1)S(1)} fusion(bf16[2,768,768]{2,1,0:T(8,128)(2,1)} %bitcast.25, bf16[2,768,768]{2,1,0:T(8,128)(2,1)S(1)} %bitcast.283, pred[]{:T(512)S(6)} %eq.58), kind=kLoop, calls=%fused_computation.3 | loop fusion | flops 21233664 | bytes 9437185 | tf_op jit(solution)/shard_map/jit(_where)/select_n | solution.py:962
  236.8 35.3 %collective-permute-done.30.refs_0_ = bf16[512,1536]{1,0:T(8,128)(2,1)} collective-permute-done((bf16[512,1536]{1,0:T(8,128)(2,1)}, bf16[512,1536]{1,0:T(8,128)(2,1)}, u32[]{:S(2)}, u32[]{:S(2)}) %collective-permute-start.30) | collective-permute-done | bytes 1572896 | tf_op jit(solution)/shard_map/ppermute | solution.py:27
  273.9 10.1 %shard_map.420 = (bf16[4,1536,512]{2,1,0:T(8,128)(2,1)}, bf16[1024,1536]{1,0:T(8,128)(2,1)}) custom-call(s32[2]{0:T(128)S(1)} %pad_add_fusion.2.index_ref, bf16[2,2,576,512]{3,2,1,0:T(8,128)(2,1)S(1)} %copy-done.5, bf16[2,2,576,512]{3,2,1,0:T(8,128)(2,1)S(1)} %copy-done.9, bf16[2,2,576,512]{3,2,1,0:T(8,128)(2,1)} %copy-done.36, ...), custom_call_target="tpu_custom_call" | custom-call | flops 1 | bytes 1 | tf_op jit(solution)/shard_map/pallas_call | solution.py:341
  284.1 50.4 %shard_map.421 = (bf16[2048,1024]{1,0:T(8,128)(2,1)}, bf16[2048,2048]{1,0:T(8,128)(2,1)}, bf16[16,384,512]{2,1,0:T(8,128)(2,1)}, bf16[16,192,512]{2,1,0:T(8,128)(2,1)}) custom-call(bf16[512,1536]{1,0:T(8,128)(2,1)} %multiply_convert_fusion.refs_0_.refs_1_, bf16[512,1536]{1,0:T(8,128)(2,1)} %collective-permute-done.29.refs_1_, ...), custom_call_target="tpu_custom_call" | custom-call | flops 1 | bytes 1 | tf_op jit(solution)/shard_map/pallas_call | solution.py:751
  334.5 10.9 %shard_map.422 = bf16[1024,1536]{1,0:T(8,128)(2,1)S(1)} custom-call(bf16[2048,2048]{1,0:T(8,128)(2,1)} %get-tuple-element.52.d_ref, bf16[4,1536,512]{2,1,0:T(8,128)(2,1)} %get-tuple-element.48.refs_8_.gu_ref), custom_call_target="tpu_custom_call" | custom-call | flops 1 | bytes 1 | tf_op jit(solution)/shard_map/pallas_call | solution.py:787
  364.9 11.6 %shard_map.426 = f32[1024,1536]{1,0:T(8,128)} custom-call(bf16[2048,2048]{1,0:T(8,128)(2,1)} %get-tuple-element.52.d_ref, bf16[4,1536,512]{2,1,0:T(8,128)(2,1)} %get-tuple-element.48.refs_8_.gu_ref, bf16[2,2,576,512]{3,2,1,0:T(8,128)(2,1)} %pad_maximum_fusion.3.refs_1_.refs_0_, bf16[2,2,576,512]{3,2,1,0:T(8,128)(2,1)S(1)} %pad_maximum_fusion.4.refs_2_.refs_1_), custom_call_target="tpu_custom_call" | custom-call | flops 1 | bytes 1 | tf_op jit(solution)/shard_map/pallas_call | solution.py:787
  381.6 11.4 %fusion.75 = (bf16[2048,1536]{1,0:T(8,128)(2,1)S(1)}, f32[2048,1536]{1,0:T(8,128)}) fusion(bf16[2048,1024]{1,0:T(8,128)(2,1)} %shard_map.425, bf16[1024,1536]{1,0:T(8,128)(2,1)S(1)} %copy-done.54), kind=kOutput, calls=%fused_computation.218 | convolution fusion | flops 6445596672 | bytes 26214400 | tf_op jit(solution)/shard_map/dot_general | solution.py:911
  423.0 8.0 %collective-permute-start.45 = (bf16[2,576,512]{2,1,0:T(8,128)(2,1)}, bf16[2,576,512]{2,1,0:T(8,128)(2,1)}, u32[]{:S(2)}, u32[]{:S(2)}) collective-permute-start(bf16[2,576,512]{2,1,0:T(8,128)(2,1)} %select_bitcast_fusion), channel_id=1, source_target_pairs={{0,4},{1,5},{2,6},{3,7},{16,20},{17,21},{18,22},{19,23}} | collective-permute-start | bytes 3538952 | tf_op jit(solution)/shard_map/ppermute | solution.py:27
  444.3 39.6 %shard_map.432 = (bf16[1024,2304]{1,0:T(8,128)(2,1)}, f32[8,8,256]{2,1,0:T(8,128)S(1)}, f32[4,8,256]{2,1,0:T(8,128)S(1)}) custom-call(s32[4]{0:T(128)S(1)} %pad_add_fusion.len_ref, f32[8,2]{1,0:T(8,128)S(1)} %copy.237.mix_ref, f32[8,8,256]{2,1,0:T(8,128)S(1)} %pad.13.base_ref, bf16[1024,2304]{1,0:T(8,128)(2,1)} %convolution_convert_fusion.1.proj_ref, ...), custom_call_target="tpu_custom_call" | custom-call | flops 1 | bytes 1 | tf_op jit(solution)/shard_map/pallas_call | solution.py:636
  485.6 10.8 %convolution_convert_fusion = bf16[1536,2304]{1,0:T(8,128)(2,1)S(1)} fusion(bf16[1024,2304]{1,0:T(8,128)(2,1)} %shard_map.433.refs_0_, bf16[512,1536]{1,0:T(8,128)(2,1)} %copy-done.61, bf16[512,1536]{1,0:T(8,128)(2,1)} %copy-done.60), kind=kOutput, calls=%fused_computation.1 | convolution fusion | flops 7257587712 | bytes 14942208 | tf_op jit(solution)/shard_map/dot_general | solution.py:911
  518.4 11.4 %fusion.76.refs_0_ = f32[1024,1536]{1,0:T(8,128)} fusion(bf16[1024,2304]{1,0:T(8,128)(2,1)S(1)} %copy-done.28, bf16[1536,2304]{1,0:T(8,128)(2,1)} %bitcast.277), kind=kOutput, calls=%fused_computation.219 | convolution fusion | flops 7247757312 | bytes 18087936 | tf_op jit(solution)/shard_map/dot_general | solution.py:911
  552.2 6.8 collective-permute-done.67
  571.1 17.1 %collective-permute-done.61 = bf16[2,576,512]{2,1,0:T(8,128)(2,1)S(1)} collective-permute-done((bf16[2,576,512]{2,1,0:T(8,128)(2,1)S(1)}, bf16[2,576,512]{2,1,0:T(8,128)(2,1)S(1)}, u32[]{:S(2)}, u32[]{:S(2)}) %collective-permute-start.61) | collective-permute-done | bytes 1179680 | tf_op jit(solution)/shard_map/ppermute | solution.py:27
  637.1 7.7 %shard_map.440 = (f32[96,2,4096]{2,1,0:T(2,128)}, f32[96,2,4096]{2,1,0:T(2,128)}, f32[96,2,4096]{2,1,0:T(2,128)}) custom-call(s32[1]{0:T(128)} %bitcast.10.quarter_ref, f32[96,2,4096]{2,1,0:T(2,128)S(1)} %copy-done.7, f32[96,2,4096]{2,1,0:T(2,128)S(1)} %copy-done.15, f32[96,2,4096]{2,1,0:T(2,128)S(1)} %copy-done.16, ...), custom_call_target="tpu_custom_call" | custom-call | flops 1 | bytes 1 | tf_op jit(solution)/shard_map/pallas_call | solution.py:885
  664.4 8.1 %fusion.9 = (bf16[512,1536]{1,0:T(8,128)(2,1)}, bf16[512,1536]{1,0:T(8,128)(2,1)}) fusion(f32[512]{0:T(512)S(1)} %broadcast_multiply_fusion, f32[1536]{0:T(1024)S(1)} %copy-done.82, f32[512]{0:T(512)S(1)} %bitcast.300, bf16[2,1,256,1536]{3,2,1,0:T(8,128)(2,1)} %param.24, f32[512,1536]{1,0:T(8,128)} %collective-permute-done.50, f32[1024,1536]{1,0:T(8,128)} %shard_map.437, ...), kind=kLoop, calls=%fused_computation.23 | loop fusion | flops 17301504 | bytes 25186304 | tf_op jit(solution)/shard_map/convert_element_type | solution.py:1142
  (535 shorter events, 319.0 us)
Async XLA Ops:
  51.7 41.1 %collective-permute-start.24 = (bf16[512,1536]{1,0:T(8,128)(2,1)}, bf16[512,1536]{1,0:T(8,128)(2,1)}, u32[]{:S(2)}, u32[]{:S(2)}) collective-permute-start(bf16[512,1536]{1,0:T(8,128)(2,1)} %bitcast), channel_id=1, source_target_pairs={{0,16},{16,0},{1,17},{17,1},{2,18},{18,2},{3,19},{19,3},{4,20},{20... | collective-permute-start | bytes 4718600 | tf_op jit(solution)/shard_map/ppermute | solution.py:31
  96.1 38.9 %collective-permute-start.21 = (bf16[2,576,512]{2,1,0:T(8,128)(2,1)}, bf16[2,576,512]{2,1,0:T(8,128)(2,1)S(1)}, u32[]{:S(2)}, u32[]{:S(2)}) collective-permute-start(bf16[2,576,512]{2,1,0:T(8,128)(2,1)} %collective-permute-done.20), channel_id=1, source_target_pairs={{4,8},{5,9},{6,10},{7,11},{8,12},{9,13},{10,14},{11,15},{20,24},{2... | collective-permute-start | bytes 3538952 | tf_op jit(solution)/shard_map/ppermute | solution.py:27
  125.7 77.7 %collective-permute-start.26 = (bf16[512,1536]{1,0:T(8,128)(2,1)}, bf16[512,1536]{1,0:T(8,128)(2,1)}, u32[]{:S(2)}, u32[]{:S(2)}) collective-permute-start(bf16[512,1536]{1,0:T(8,128)(2,1)} %bitcast.22.refs_4_), channel_id=1, source_target_pairs={{0,1},{1,0},{2,3},{3,2},{4,5},{5,4},{6,7},{7,6},{8,9},{9,8},{10,11... | collective-permute-start | bytes 4718600 | tf_op jit(solution)/shard_map/ppermute | solution.py:27
  145.6 57.7 %collective-permute-start.25 = (bf16[2,2,576,512]{3,2,1,0:T(8,128)(2,1)}, bf16[2,2,576,512]{3,2,1,0:T(8,128)(2,1)S(1)}, u32[]{:S(2)}, u32[]{:S(2)}) collective-permute-start(bf16[2,2,576,512]{3,2,1,0:T(8,128)(2,1)} %shard_map.415.refs_0_), channel_id=1, source_target_pairs={{0,2},{1,3},{2,0},{3,1},{4,6},{5,7},{6,4},{7,5},{8,10},{9,11},{10,... | collective-permute-start | bytes 7077896 | tf_op jit(solution)/shard_map/ppermute | solution.py:27
  146.2 67.3 %collective-permute-start.27 = (bf16[1536,768]{1,0:T(8,128)(2,1)}, bf16[1536,768]{1,0:T(8,128)(2,1)}, u32[]{:S(2)}, u32[]{:S(2)}) collective-permute-start(bf16[1536,768]{1,0:T(8,128)(2,1)} %bitcast.282), channel_id=1, source_target_pairs={{0,16},{16,0},{1,17},{17,1},{2,18},{18,2},{3,19},{19,3},{4,20},{20... | collective-permute-start | bytes 7077896 | tf_op jit(solution)/shard_map/ppermute | solution.py:31
  146.2 61.7 %collective-permute-start.31 = (bf16[2,576,512]{2,1,0:T(8,128)(2,1)}, bf16[2,576,512]{2,1,0:T(8,128)(2,1)}, u32[]{:S(2)}, u32[]{:S(2)}) collective-permute-start(bf16[2,576,512]{2,1,0:T(8,128)(2,1)} %copy-done.45), channel_id=1, source_target_pairs={{8,12},{9,13},{10,14},{11,15},{24,28},{25,29},{26,30},{27,31}} | collective-permute-start | bytes 3538952 | tf_op jit(solution)/shard_map/ppermute | solution.py:27
  148.0 59.9 %collective-permute-start.32 = (bf16[2,576,512]{2,1,0:T(8,128)(2,1)}, bf16[2,576,512]{2,1,0:T(8,128)(2,1)}, u32[]{:S(2)}, u32[]{:S(2)}) collective-permute-start(bf16[2,576,512]{2,1,0:T(8,128)(2,1)} %copy-done.47), channel_id=1, source_target_pairs={{4,0},{5,1},{6,2},{7,3},{20,16},{21,17},{22,18},{23,19}} | collective-permute-start | bytes 3538952 | tf_op jit(solution)/shard_map/ppermute | solution.py:27
  211.9 60.2 %collective-permute-start.33 = (bf16[2,2,576,512]{3,2,1,0:T(8,128)(2,1)S(1)}, bf16[2,2,576,512]{3,2,1,0:T(8,128)(2,1)}, u32[]{:S(2)}, u32[]{:S(2)}) collective-permute-start(bf16[2,2,576,512]{3,2,1,0:T(8,128)(2,1)S(1)} %pad_maximum_fusion.2.refs_2_), channel_id=1, source_target_pairs={{0,2},{1,3},{2,0},{3,1},{4,6},{5,7},{6,4},{7,5},{8,10},{9,11},{10,... | collective-permute-start | bytes 7077896 | tf_op jit(solution)/shard_map/ppermute | solution.py:27
  236.3 47.7 %collective-permute-start.35 = (bf16[512,1536]{1,0:T(8,128)(2,1)}, bf16[512,1536]{1,0:T(8,128)(2,1)}, u32[]{:S(2)}, u32[]{:S(2)}) collective-permute-start(bf16[512,1536]{1,0:T(8,128)(2,1)} %bitcast.22.refs_4_), channel_id=1, source_target_pairs={{0,16},{16,0},{1,17},{17,1},{2,18},{18,2},{3,19},{19,3},{4,20},{20... | collective-permute-start | bytes 4718600 | tf_op jit(solution)/shard_map/ppermute | solution.py:31
  236.3 47.7 %collective-permute-start.36 = (bf16[512,1536]{1,0:T(8,128)(2,1)}, bf16[512,1536]{1,0:T(8,128)(2,1)}, u32[]{:S(2)}, u32[]{:S(2)}) collective-permute-start(bf16[512,1536]{1,0:T(8,128)(2,1)} %collective-permute-done.26.refs_2_.refs_6_), channel_id=1, source_target_pairs={{0,16},{16,0},{1,17},{17,1},{2,18},{18,2},{3,19},{19,3},{4,20},{20... | collective-permute-start | bytes 4718600 | tf_op jit(solution)/shard_map/ppermute | solution.py:31
  236.8 47.2 %collective-permute-start.29 = (bf16[512,1536]{1,0:T(8,128)(2,1)}, bf16[512,1536]{1,0:T(8,128)(2,1)}, u32[]{:S(2)}, u32[]{:S(2)}) collective-permute-start(bf16[512,1536]{1,0:T(8,128)(2,1)} %multiply_convert_fusion.refs_0_.refs_1_), channel_id=1, source_target_pairs={{0,16},{16,0},{1,17},{17,1},{2,18},{18,2},{3,19},{19,3},{4,20},{20... | collective-permute-start | bytes 4718600 | tf_op jit(solution)/shard_map/ppermute | solution.py:31
  353.4 46.4 %collective-permute-start.41 = (bf16[512,1536]{1,0:T(8,128)(2,1)}, bf16[512,1536]{1,0:T(8,128)(2,1)}, u32[]{:S(2)}, u32[]{:S(2)}) collective-permute-start(bf16[512,1536]{1,0:T(8,128)(2,1)} %add_convert_fusion.3.refs_1_), channel_id=1, source_target_pairs={{0,1},{1,0},{2,3},{3,2},{4,5},{5,4},{6,7},{7,6},{8,9},{9,8},{10,11... | collective-permute-start | bytes 4718600 | tf_op jit(solution)/shard_map/ppermute | solution.py:27
  363.3 55.9 %collective-permute-start.44 = (bf16[2,2,576,512]{3,2,1,0:T(8,128)(2,1)}, bf16[2,2,576,512]{3,2,1,0:T(8,128)(2,1)}, u32[]{:S(2)}, u32[]{:S(2)}) collective-permute-start(bf16[2,2,576,512]{3,2,1,0:T(8,128)(2,1)} %pad_maximum_fusion.3.refs_1_.refs_0_), channel_id=1, source_target_pairs={{0,2},{1,3},{2,0},{3,1},{4,6},{5,7},{6,4},{7,5},{8,10},{9,11},{10,... | collective-permute-start | bytes 7077896 | tf_op jit(solution)/shard_map/ppermute | solution.py:27
  417.9 67.7 %collective-permute-start.42 = (bf16[512,1536]{1,0:T(8,128)(2,1)}, bf16[512,1536]{1,0:T(8,128)(2,1)}, u32[]{:S(2)}, u32[]{:S(2)}) collective-permute-start(bf16[512,1536]{1,0:T(8,128)(2,1)} %shard_map.428), channel_id=1, source_target_pairs={{0,1},{1,0},{2,3},{3,2},{4,5},{5,4},{6,7},{7,6},{8,9},{9,8},{10,11... | collective-permute-start | bytes 4718600 | tf_op jit(solution)/shard_map/ppermute | solution.py:27
  423.0 62.6 %collective-permute-start.45 = (bf16[2,576,512]{2,1,0:T(8,128)(2,1)}, bf16[2,576,512]{2,1,0:T(8,128)(2,1)}, u32[]{:S(2)}, u32[]{:S(2)}) collective-permute-start(bf16[2,576,512]{2,1,0:T(8,128)(2,1)} %select_bitcast_fusion), channel_id=1, source_target_pairs={{0,4},{1,5},{2,6},{3,7},{16,20},{17,21},{18,22},{19,23}} | collective-permute-start | bytes 3538952 | tf_op jit(solution)/shard_map/ppermute | solution.py:27
  431.0 54.6 %collective-permute-start.46 = (bf16[2,576,512]{2,1,0:T(8,128)(2,1)}, bf16[2,576,512]{2,1,0:T(8,128)(2,1)}, u32[]{:S(2)}, u32[]{:S(2)}) collective-permute-start(bf16[2,576,512]{2,1,0:T(8,128)(2,1)} %select_bitcast_fusion), channel_id=1, source_target_pairs={{12,8},{13,9},{14,10},{15,11},{28,24},{29,25},{30,26},{31,27}} | collective-permute-start | bytes 3538952 | tf_op jit(solution)/shard_map/ppermute | solution.py:27
  442.2 87.7 %collective-permute-start.59 = (bf16[2,2,576,512]{3,2,1,0:T(8,128)(2,1)S(1)}, bf16[2,2,576,512]{3,2,1,0:T(8,128)(2,1)}, u32[]{:S(2)}, u32[]{:S(2)}) collective-permute-start(bf16[2,2,576,512]{3,2,1,0:T(8,128)(2,1)S(1)} %copy-done.4), channel_id=1, source_target_pairs={{0,2},{1,3},{2,0},{3,1},{4,6},{5,7},{6,4},{7,5},{8,10},{9,11},{10,... | collective-permute-start | bytes 7077896 | tf_op jit(solution)/shard_map/ppermute | solution.py:27
  442.9 55.3 %collective-permute-start.47 = (bf16[1536,768]{1,0:T(8,128)(2,1)}, bf16[1536,768]{1,0:T(8,128)(2,1)}, u32[]{:S(2)}, u32[]{:S(2)}) collective-permute-start(bf16[1536,768]{1,0:T(8,128)(2,1)} %convolution_convert_fusion.3.refs_1_), channel_id=1, source_target_pairs={{0,16},{16,0},{1,17},{17,1},{2,18},{18,2},{3,19},{19,3},{4,20},{20... | collective-permute-start | bytes 7077896 | tf_op jit(solution)/shard_map/ppermute | solution.py:31
  508.3 37.8 %collective-permute-start.62 = (bf16[2,96,3072]{2,1,0:T(8,128)(2,1)}, bf16[2,96,3072]{2,1,0:T(8,128)(2,1)}, u32[]{:S(2)}, u32[]{:S(2)}) collective-permute-start(bf16[2,96,3072]{2,1,0:T(8,128)(2,1)} %pad_maximum_fusion.9.refs_2_), channel_id=1, source_target_pairs={{0,1},{1,0},{2,3},{3,2},{4,5},{5,4},{6,7},{7,6},{8,9},{9,8},{10,11... | collective-permute-start | bytes 3538952 | tf_op jit(solution)/shard_map/ppermute | solution.py:27
  541.7 56.1 %collective-permute-start.58 = (bf16[2,96,3072]{2,1,0:T(8,128)(2,1)S(1)}, bf16[2,96,3072]{2,1,0:T(8,128)(2,1)}, u32[]{:S(2)}, u32[]{:S(2)}) collective-permute-start(bf16[2,96,3072]{2,1,0:T(8,128)(2,1)S(1)} %copy-done.26), channel_id=1, source_target_pairs={{0,1},{1,0},{2,3},{3,2},{4,5},{5,4},{6,7},{7,6},{8,9},{9,8},{10,11... | collective-permute-start | bytes 3538952 | tf_op jit(solution)/shard_map/ppermute | solution.py:27
  546.0 72.5 %collective-permute-start.50 = (f32[512,1536]{1,0:T(8,128)}, f32[512,1536]{1,0:T(8,128)}, u32[]{:S(2)}, u32[]{:S(2)}) collective-permute-start(f32[512,1536]{1,0:T(8,128)} %slice.265), channel_id=1, source_target_pairs={{0,16},{16,0},{1,17},{17,1},{2,18},{18,2},{3,19},{19,3},{4,20},{20... | collective-permute-start | bytes 9437192 | tf_op jit(solution)/shard_map/ppermute | solution.py:31
  548.8 50.3 %collective-permute-start.63 = (bf16[2,96,3072]{2,1,0:T(8,128)(2,1)}, bf16[2,96,3072]{2,1,0:T(8,128)(2,1)}, u32[]{:S(2)}, u32[]{:S(2)}) collective-permute-start(bf16[2,96,3072]{2,1,0:T(8,128)(2,1)} %add_convert_fusion.7), channel_id=1, source_target_pairs={{0,2},{1,3},{2,0},{3,1},{4,6},{5,7},{6,4},{7,5},{8,10},{9,11},{10,... | collective-permute-start | bytes 3538952 | tf_op jit(solution)/shard_map/ppermute | solution.py:27
  588.2 76.2 %collective-permute-start.38 = (bf16[512,1536]{1,0:T(8,128)(2,1)}, bf16[512,1536]{1,0:T(8,128)(2,1)}, u32[]{:S(2)}, u32[]{:S(2)}) collective-permute-start(bf16[512,1536]{1,0:T(8,128)(2,1)} %get-tuple-element.189), channel_id=1, source_target_pairs={{0,16},{16,0},{1,17},{17,1},{2,18},{18,2},{3,19},{19,3},{4,20},{20... | collective-permute-start | bytes 4718600 | tf_op jit(solution)/shard_map/ppermute | solution.py:31
  608.5 45.4 %collective-permute-start.71 = (bf16[96,3072]{1,0:T(8,128)(2,1)}, bf16[96,3072]{1,0:T(8,128)(2,1)}, u32[]{:S(2)}, u32[]{:S(2)}) collective-permute-start(bf16[96,3072]{1,0:T(8,128)(2,1)} %get-tuple-element.217), channel_id=1, source_target_pairs={{0,4},{1,5},{2,6},{3,7},{4,8},{5,9},{6,10},{7,11},{16,20},{17,21},... | collective-permute-start | bytes 1769480 | tf_op jit(solution)/shard_map/ppermute | solution.py:27
  (157 other events, 1684.2 us)
